TPU v7x, 128 devices: a whole 4x4x4 slice. The times are simulated.
128 devices in a mesh: section: 4 (over z), expert: 32 (over y, x, core).
Axes of the slice: x: 4, y: 4, z: 4, core: 2. Of those that a mesh axis runs over, the one named last changes fastest.
Arguments:
- tokens: bfloat16 [4, 512, 7168], P('section', 'expert'), may hold values from -6 to 6
- norm_gain: float32 [4, 7168], P('section'), may hold values from 0.5 to 1.5
- gate_weight: bfloat16 [4, 7168, 16384], P('section', None, 'expert'), may hold values from -0.0625 to 0.0625
- up_weight: bfloat16 [4, 7168, 16384], P('section', None, 'expert'), may hold values from -0.0625 to 0.0625
- down_weight: bfloat16 [4, 16384, 7168], P('section', 'expert'), may hold values from -0.125 to 0.125
- routes: int32 [4, 4, 512, 2], P('section', None, 'expert'), may hold values from 0 to 7, all different within a row; in each aligned block of 16 rows (0 to 15, 16 to 31, ..., all dimensions but the last counted through in order) at most 6 rows name the same one
- route_weights: float32 [4, 4, 512, 2], P('section', None, 'expert'), may hold values from 0.2 to 1.2
Outputs:
- targets: bfloat16 [4, 512, 7168], P('section', 'expert')
Inputs may be any that keep to these rules, and one draw needn't show every extreme that they name: Within the 16 tokens of one device for one layer and micro-batch, no expert is named by more than 6 routes, a bound that some block reaches.
All inputs are finite; a program needn't handle non-finite values.
Results may differ from a plain program's by a relative error of at most 0.019.
Values may be sent and summed in bfloat16 or wider, within the bound.
No kernel may reach another device: no remote copies, remote signals or barrier semaphores. Data moves between devices by JAX's collectives and lax.ppermute only.
A program may use at most 128 MiB of HBM per device.

v0:
```python
import jax
import jax.numpy as jnp
from jax import lax
from jax.sharding import PartitionSpec as P

SHARDS = 4


def from_behind(value, axis, by):
    size = lax.axis_size(axis)
    pairs = [(i, i + by) for i in range(size) if 0 <= i + by < size]
    return lax.ppermute(value, axis, pairs)


def per_device(tokens, norm_gain, gate_weight, up_weight, down_weight, routes, route_weights):
    sections = lax.axis_size("section")
    devices = lax.axis_size("expert")
    experts = devices // SHARDS
    batches = routes.shape[1]
    tok_rows = routes.shape[2]
    routes_each = routes.shape[3]
    widths = tokens.shape[2]
    capacity = min(tok_rows, tok_rows * routes_each * 3 // (2 * experts))
    section_pos = lax.axis_index("section")
    loaded = lax.all_gather(tokens, "section", axis=0, tiled=True)
    norm_row = norm_gain[0]
    gate_local = gate_weight[0]
    up_local = up_weight[0]
    down_local = down_weight[0]
    finished = jnp.zeros((batches, tok_rows, widths), jnp.bfloat16)
    current = jnp.zeros((tok_rows, widths), jnp.bfloat16)
    for step_index in range(batches + sections - 1):
        carried = current
        if step_index > 0:
            carried = from_behind(current, "section", 1)
        incoming = loaded[min(step_index, batches - 1)]
        hidden = jnp.where(section_pos == 0, incoming, carried)
        batch_pos = jnp.clip(step_index - section_pos, 0, batches - 1)
        route_ids = lax.dynamic_index_in_dim(routes[0], batch_pos, 0, keepdims=False)
        route_scale = lax.dynamic_index_in_dim(route_weights[0], batch_pos, 0, keepdims=False)
        widened = hidden.astype(jnp.float32)
        scale = lax.rsqrt(jnp.mean(widened * widened, axis=-1, keepdims=True) + 1e-06)
        normed = (widened * scale * norm_row).astype(jnp.bfloat16)
        flat_ids = route_ids.reshape(-1)
        flat_scale = route_scale.reshape(-1)
        onehot = (flat_ids[:, None] == jnp.arange(experts, dtype=jnp.int32)[None, :]).astype(
            jnp.int32
        )
        ranking = jnp.sum((jnp.cumsum(onehot, axis=0) - 1) * onehot, axis=1)
        target = flat_ids * capacity + ranking
        slots_all = experts * capacity
        matches = (jnp.arange(slots_all, dtype=jnp.int32)[:, None] == target[None, :]).astype(
            jnp.float32
        )
        picking = jnp.sum(matches.reshape(slots_all, tok_rows, routes_each), axis=2)
        outgoing = jnp.dot(
            picking.astype(jnp.bfloat16), normed, preferred_element_type=jnp.float32
        ).astype(jnp.bfloat16)
        outgoing = jnp.broadcast_to(
            outgoing.reshape(experts, 1, capacity, widths), (experts, SHARDS, capacity, widths)
        )
        outgoing = outgoing.reshape(devices, capacity, widths)
        arrived = lax.all_to_all(outgoing, "expert", split_axis=0, concat_axis=0, tiled=True)
        slot_rows = arrived.reshape(-1, widths)
        gate_pre = jnp.dot(slot_rows, gate_local, preferred_element_type=jnp.float32)
        up_pre = jnp.dot(slot_rows, up_local, preferred_element_type=jnp.float32)
        inner = (jax.nn.silu(gate_pre) * up_pre).astype(jnp.bfloat16)
        partial_value = jnp.dot(inner, down_local, preferred_element_type=jnp.float32).astype(
            jnp.bfloat16
        )
        partial_value = partial_value.reshape(arrived.shape)
        returned = lax.all_to_all(partial_value, "expert", split_axis=0, concat_axis=0, tiled=True)
        summed = jnp.sum(
            returned.reshape(experts, SHARDS, capacity, widths).astype(jnp.float32), axis=1
        )
        summed = summed.reshape(slots_all, widths)
        weighing = jnp.sum(
            (matches * flat_scale[None, :]).reshape(slots_all, tok_rows, routes_each), axis=2
        )
        mixed = lax.dot_general(
            weighing,
            summed,
            (((0,), (0,)), ((), ())),
            precision=lax.Precision.HIGHEST,
            preferred_element_type=jnp.float32,
        )
        current = (widened + mixed).astype(jnp.bfloat16)
        finished_pos = step_index - (sections - 1)
        if 0 <= finished_pos < batches:
            finished = finished.at[finished_pos].set(current)
    owned = batches // sections
    received = lax.all_to_all(finished, "section", split_axis=0, concat_axis=0, tiled=True)
    return received[(sections - 1) * owned :]


def solution(mesh):
    return jax.shard_map(
        per_device,
        mesh=mesh,
        in_specs=(
            P("section", "expert", None),
            P("section", None),
            P("section", None, "expert"),
            P("section", None, "expert"),
            P("section", "expert", None),
            P("section", None, "expert", None),
            P("section", None, "expert", None),
        ),
        out_specs=P("section", "expert", None),
        check_vma=False,
    )
```

profile of v0, /device:TPU:1, one launch (start us, length us, event | category | flops | bytes accessed | tf_op | source)
XLA Modules:
  0.0 990.0 jit_solution(11592037662425358653)
XLA Ops:
  2.3 14.5 %all_gather.3 = bf16[4,16,7168]{2,1,0:T(8,128)(2,1)S(1)} all-gather(bf16[1,16,7168]{2,1,0:T(8,128)(2,1)} %param.15), channel_id=1, replica_groups=mesh['section'=4,'expert'=32] {'section'}, dimensions={0}, use_global_device_ids=true | all-gather | bytes 1146880 | tf_op jit(solution)/shard_map/all_gather | solution.py:25
  19.6 54.8 %all_to_all.75 = bf16[32,6,7168]{2,1,0:T(8,128)(2,1)} all-to-all(bf16[32,6,7168]{2,1,0:T(8,128)(2,1)S(1)} %bitcast.236), channel_id=1, replica_groups=mesh['section'=4,'expert'=32] {'expert'}, dimensions={0} | all-to-all | bytes 5505024 | tf_op jit(solution)/shard_map/all_to_all | solution.py:63
  74.4 3.2 reshape.610
  77.6 4.7 fusion.42
  82.3 9.9 convolution_convert_fusion.6
  92.1 4.6 reshape.611
  96.7 4.9 all-to-all-start.1
  102.9 43.9 %all-to-all-done.1 = bf16[32,6,7168]{2,1,0:T(8,128)(2,1)} async-done(((bf16[32,6,7168]{2,1,0:T(8,128)(2,1)}), bf16[32,6,7168]{2,1,0:T(8,128)(2,1)}, u32[]{:S(2)}, u32[]{:S(2)}) %all-to-all-start.1) | async-done | bytes 2752544 | tf_op jit(solution)/shard_map/all_to_all | solution.py:72
  146.8 3.0 convert_reduce_fusion.6
  151.1 2.1 fusion
  153.3 3.9 collective-permute-start
  157.3 2.8 collective-permute-done
  161.4 52.6 %all_to_all.76 = bf16[32,6,7168]{2,1,0:T(8,128)(2,1)} all-to-all(bf16[32,6,7168]{2,1,0:T(8,128)(2,1)S(1)} %bitcast.237), channel_id=1, replica_groups=mesh['section'=4,'expert'=32] {'expert'}, dimensions={0} | all-to-all | bytes 5505024 | tf_op jit(solution)/shard_map/all_to_all | solution.py:63
  214.1 3.2 reshape.614
  217.3 4.7 fusion.40
  222.0 9.9 convolution_convert_fusion.5
  231.8 4.6 reshape.615
  236.4 49.5 %all_to_all.77 = bf16[32,6,7168]{2,1,0:T(8,128)(2,1)S(1)} all-to-all(bf16[32,6,7168]{2,1,0:T(8,128)(2,1)} %reshape.615), channel_id=1, replica_groups=mesh['section'=4,'expert'=32] {'expert'}, dimensions={0} | all-to-all | bytes 5505024 | tf_op jit(solution)/shard_map/all_to_all | solution.py:72
  287.8 4.1 collective-permute-start.1
  292.0 4.4 collective-permute-done.1
  298.6 50.3 %all_to_all.78 = bf16[32,6,7168]{2,1,0:T(8,128)(2,1)} all-to-all(bf16[32,6,7168]{2,1,0:T(8,128)(2,1)S(1)} %bitcast.238), channel_id=1, replica_groups=mesh['section'=4,'expert'=32] {'expert'}, dimensions={0} | all-to-all | bytes 5505024 | tf_op jit(solution)/shard_map/all_to_all | solution.py:63
  348.9 3.2 reshape.618
  352.1 4.7 fusion.38
  356.8 9.9 convolution_convert_fusion.4
  366.7 4.6 reshape.619
  371.3 4.9 all-to-all-start.5
  377.5 43.9 %all-to-all-done.5 = bf16[32,6,7168]{2,1,0:T(8,128)(2,1)} async-done(((bf16[32,6,7168]{2,1,0:T(8,128)(2,1)}), bf16[32,6,7168]{2,1,0:T(8,128)(2,1)}, u32[]{:S(2)}, u32[]{:S(2)}) %all-to-all-start.5) | async-done | bytes 2752544 | tf_op jit(solution)/shard_map/all_to_all | solution.py:72
  421.4 3.0 convert_reduce_fusion.4
  425.4 4.1 collective-permute-start.2
  429.6 2.8 collective-permute-done.2
  434.7 52.7 %all_to_all.79 = bf16[32,6,7168]{2,1,0:T(8,128)(2,1)} all-to-all(bf16[32,6,7168]{2,1,0:T(8,128)(2,1)S(1)} %bitcast.239), channel_id=1, replica_groups=mesh['section'=4,'expert'=32] {'expert'}, dimensions={0} | all-to-all | bytes 5505024 | tf_op jit(solution)/shard_map/all_to_all | solution.py:63
  487.4 3.2 reshape.622
  490.6 4.7 fusion.36
  495.3 9.9 convolution_convert_fusion.3
  505.2 4.6 reshape.623
  509.8 49.5 %all_to_all.80 = bf16[32,6,7168]{2,1,0:T(8,128)(2,1)S(1)} all-to-all(bf16[32,6,7168]{2,1,0:T(8,128)(2,1)} %reshape.623), channel_id=1, replica_groups=mesh['section'=4,'expert'=32] {'expert'}, dimensions={0} | all-to-all | bytes 5505024 | tf_op jit(solution)/shard_map/all_to_all | solution.py:72
  561.1 4.1 collective-permute-start.3
  565.3 4.4 collective-permute-done.3
  572.0 50.5 %all_to_all.81 = bf16[32,6,7168]{2,1,0:T(8,128)(2,1)} all-to-all(bf16[32,6,7168]{2,1,0:T(8,128)(2,1)S(1)} %bitcast.240), channel_id=1, replica_groups=mesh['section'=4,'expert'=32] {'expert'}, dimensions={0} | all-to-all | bytes 5505024 | tf_op jit(solution)/shard_map/all_to_all | solution.py:63
  622.5 3.2 reshape.627
  625.7 4.7 fusion.34
  630.4 9.9 convolution_convert_fusion.2
  640.3 4.6 reshape.628
  644.9 5.0 all-to-all-start.9
  652.3 42.8 %all-to-all-done.9 = bf16[32,6,7168]{2,1,0:T(8,128)(2,1)} async-done(((bf16[32,6,7168]{2,1,0:T(8,128)(2,1)}), bf16[32,6,7168]{2,1,0:T(8,128)(2,1)}, u32[]{:S(2)}, u32[]{:S(2)}) %all-to-all-start.9) | async-done | bytes 2752544 | tf_op jit(solution)/shard_map/all_to_all | solution.py:72
  695.1 3.0 convert_reduce_fusion.2
  698.4 1.5 bitcast_dynamic-update-slice_fusion.1
  699.8 4.1 collective-permute-start.4
  704.0 2.8 collective-permute-done.4
  709.1 52.6 %all_to_all.82 = bf16[32,6,7168]{2,1,0:T(8,128)(2,1)} all-to-all(bf16[32,6,7168]{2,1,0:T(8,128)(2,1)S(1)} %bitcast.241), channel_id=1, replica_groups=mesh['section'=4,'expert'=32] {'expert'}, dimensions={0} | all-to-all | bytes 5505024 | tf_op jit(solution)/shard_map/all_to_all | solution.py:63
  761.7 3.2 reshape.632
  765.0 4.7 fusion.32
  769.6 9.9 convolution_convert_fusion.1
  779.5 4.6 reshape.633
  784.1 49.5 %all_to_all.83 = bf16[32,6,7168]{2,1,0:T(8,128)(2,1)S(1)} all-to-all(bf16[32,6,7168]{2,1,0:T(8,128)(2,1)} %reshape.633), channel_id=1, replica_groups=mesh['section'=4,'expert'=32] {'expert'}, dimensions={0} | all-to-all | bytes 5505024 | tf_op jit(solution)/shard_map/all_to_all | solution.py:72
  836.1 4.1 collective-permute-start.5
  840.3 4.4 collective-permute-done.5
  847.0 50.3 %all_to_all.84 = bf16[32,6,7168]{2,1,0:T(8,128)(2,1)} all-to-all(bf16[32,6,7168]{2,1,0:T(8,128)(2,1)S(1)} %bitcast.242), channel_id=1, replica_groups=mesh['section'=4,'expert'=32] {'expert'}, dimensions={0} | all-to-all | bytes 5505024 | tf_op jit(solution)/shard_map/all_to_all | solution.py:63
  897.3 3.2 reshape.637
  900.5 4.7 fusion.30
  905.1 9.9 convolution_convert_fusion
  915.0 4.6 reshape.638
  919.6 49.5 %all_to_all.85 = bf16[32,6,7168]{2,1,0:T(8,128)(2,1)S(1)} all-to-all(bf16[32,6,7168]{2,1,0:T(8,128)(2,1)} %reshape.638), channel_id=1, replica_groups=mesh['section'=4,'expert'=32] {'expert'}, dimensions={0} | all-to-all | bytes 5505024 | tf_op jit(solution)/shard_map/all_to_all | solution.py:72
  971.7 17.4 %all_to_all.86 = bf16[4,16,7168]{2,1,0:T(8,128)(2,1)S(1)} all-to-all(bf16[4,16,7168]{2,1,0:T(8,128)(2,1)} %fusion.8), channel_id=1, replica_groups=mesh['section'=4,'expert'=32] {'section'}, dimensions={0} | all-to-all | bytes 1835008 | tf_op jit(solution)/shard_map/all_to_all | solution.py:92
  (125 shorter events, 34.5 us)
Async XLA Ops:
  16.8 0.9 copy-start
  96.7 50.1 %all-to-all-start.1 = ((bf16[32,6,7168]{2,1,0:T(8,128)(2,1)}), bf16[32,6,7168]{2,1,0:T(8,128)(2,1)}, u32[]{:S(2)}, u32[]{:S(2)}) async-start(bf16[32,6,7168]{2,1,0:T(8,128)(2,1)} %reshape.611), calls=%async_computation.1 | async-start | bytes 7340032 | tf_op jit(solution)/shard_map/all_to_all | solution.py:72
  102.9 48.2 %copy-start.1 = (bf16[4,16,7168]{2,1,0:T(8,128)(2,1)S(1)}, bf16[4,16,7168]{2,1,0:T(8,128)(2,1)}, u32[]{:S(2)}) copy-start(bf16[4,16,7168]{2,1,0:T(8,128)(2,1)} %copy-done) | copy-start | bytes 2752516
  149.8 10.5 %copy-start.2 = (f32[1,7168]{1,0:T(1,128)S(1)}, f32[1,7168]{1,0:T(1,128)}, u32[]{:S(2)}) copy-start(f32[1,7168]{1,0:T(1,128)} %param.16) | copy-start | bytes 86020
  153.3 6.9 collective-permute-start
  287.8 8.6 collective-permute-start.1
  371.3 50.1 %all-to-all-start.5 = ((bf16[32,6,7168]{2,1,0:T(8,128)(2,1)}), bf16[32,6,7168]{2,1,0:T(8,128)(2,1)}, u32[]{:S(2)}, u32[]{:S(2)}) async-start(bf16[32,6,7168]{2,1,0:T(8,128)(2,1)} %reshape.619), calls=%async_computation.5 | async-start | bytes 7340032 | tf_op jit(solution)/shard_map/all_to_all | solution.py:72
  425.4 7.1 collective-permute-start.2
  561.1 9.8 copy-start.3
  561.1 8.6 collective-permute-start.3
  644.9 6.4 copy-start.4
  644.9 50.3 %all-to-all-start.9 = ((bf16[32,6,7168]{2,1,0:T(8,128)(2,1)}), bf16[32,6,7168]{2,1,0:T(8,128)(2,1)}, u32[]{:S(2)}, u32[]{:S(2)}) async-start(bf16[32,6,7168]{2,1,0:T(8,128)(2,1)} %reshape.628), calls=%async_computation.9 | async-start | bytes 7340032 | tf_op jit(solution)/shard_map/all_to_all | solution.py:72
  699.8 7.0 collective-permute-start.4
  836.1 8.6 collective-permute-start.5
where the time goes:
time: 1000 us; the launch traced here: 990 us
  blocking collectives  594 us (59%)
  waiting for transfers between devices  152 us (15%)
  matrix products  114 us (11%)
  local copies, waits for them, and re-layouts  68.6 us (7%)
  starting transfers between devices  39.3 us (4%)
  other arithmetic  21.1 us (2%)
    all_to_all x7, blocking collectives, per_device(): lax.all_to_all(outgoing, 'expert', split_axis=0, concat_axis=0, tiled=True)  364 us
    all_to_all x4, blocking collectives, per_device(): lax.all_to_all(partial_value, 'expert', split_axis=0, concat_axis=0, tile...  198 us
    all_to_all x3, waiting for transfers between devices, per_device(): lax.all_to_all(partial_value, 'expert', split_axis=0, concat_axis=0, tile...  131 us
    dot_general x7, matrix products, per_device(): jnp.dot(inner, down_local, preferred_element_type=jnp.float32)  69 us
    dot_general x7, matrix products, per_device(): jnp.dot(slot_rows, gate_local, preferred_element_type=jnp.float32)  32.6 us
    reshape x7, local copies, waits for them, and re-layouts, per_device(): partial_value = partial_value.reshape(arrived.shape)  32.3 us
    ppermute x6, starting transfers between devices, from_behind(): return lax.ppermute(value, axis, pairs)  24.5 us
    reshape x7, local copies, waits for them, and re-layouts, per_device(): slot_rows = arrived.reshape(-1, widths)  22.5 us
  transfers between devices with their start and end apart: 9, of which 9 were waited for; matrix products, arithmetic and copies ran while one was open for 1% of the time, Pallas kernels for 0%

commit v1 on v0

v1 whole, which is shorter than its diff:
```python
import jax
import jax.numpy as jnp
from jax import lax
from jax.experimental import pallas as pl
from jax.experimental.pallas import tpu as pltpu
from jax.sharding import PartitionSpec as P

SHARDS = 4
PARTS = 4

F32 = jnp.float32
BF16 = jnp.bfloat16


def params():
    return pltpu.CompilerParams(vmem_limit_bytes=28 * 1024 * 1024)


def cost(flops, bytes_accessed):
    return pl.CostEstimate(flops=int(flops), bytes_accessed=int(bytes_accessed), transcendentals=0)


def mm(a, b):
    return jnp.dot(a, b, preferred_element_type=F32)


def front(pos, hidden, gain, pick, *, width):
    tok, full = hidden.shape
    rows, depth = pick.shape[1:]
    blocks = full // width

    def kernel(pos_ref, h_ref, g_ref, p_ref, o_ref):
        x = h_ref[...].astype(F32)
        scale = lax.rsqrt(jnp.mean(x * x, axis=-1, keepdims=True) + 1e-06)
        normed = (x * scale * g_ref[...]).astype(BF16)
        stack = jnp.concatenate([normed[:, b * width : (b + 1) * width] for b in range(blocks)], axis=0)
        o_ref[...] = mm(p_ref[0], stack).astype(BF16)

    return pl.pallas_call(
        kernel,
        out_shape=jax.ShapeDtypeStruct((rows, width), BF16),
        grid_spec=pltpu.PrefetchScalarGridSpec(
            num_scalar_prefetch=1,
            grid=(1,),
            in_specs=[
                pl.BlockSpec((tok, full), lambda i, s: (0, 0)),
                pl.BlockSpec((1, full), lambda i, s: (0, 0)),
                pl.BlockSpec((1, rows, depth), lambda i, s: (s[0], 0, 0)),
            ],
            out_specs=pl.BlockSpec((rows, width), lambda i, s: (0, 0)),
        ),
        compiler_params=params(),
        cost_estimate=cost(2 * rows * depth * width, 2 * rows * width),
    )(pos, hidden, gain, pick)


def unpack(packed_ref, perm, xs, slot_rows):
    group = perm.shape[0]
    piece = group // PARTS
    for g in range(slot_rows // piece):
        moved = mm(perm, packed_ref[g * group : (g + 1) * group, :]).astype(BF16)
        for b in range(PARTS):
            xs[b, g * piece : (g + 1) * piece, :] = moved[b * piece : (b + 1) * piece]


def repack(ys, perm, g):
    group = perm.shape[0]
    piece = group // PARTS
    stack = jnp.concatenate([ys[b, g * piece : (g + 1) * piece, :] for b in range(PARTS)], axis=0)
    return mm(perm, stack)


def first_half(core, arrived, perm, gate, up):
    all_rows, width = arrived.shape
    rows = all_rows // PARTS
    units = gate.shape[2]

    def kernel(core_ref, a_ref, p_ref, g_ref, u_ref, og_ref, ou_ref, xs):
        step = pl.program_id(0)

        @pl.when(step == 0)
        def _():
            unpack(a_ref, p_ref[...], xs, rows)
            og_ref[...] = jnp.zeros_like(og_ref)
            ou_ref[...] = jnp.zeros_like(ou_ref)

        x = xs[step]
        og_ref[...] += mm(x, g_ref[0])
        ou_ref[...] += mm(x, u_ref[0])

    weight = pl.BlockSpec((1, width, units), lambda i, s: (0, s[0] * PARTS + i, 0))
    total = pl.BlockSpec((rows, units), lambda i, s: (0, 0))
    return pl.pallas_call(
        kernel,
        out_shape=[jax.ShapeDtypeStruct((rows, units), F32)] * 2,
        grid_spec=pltpu.PrefetchScalarGridSpec(
            num_scalar_prefetch=1,
            grid=(PARTS,),
            in_specs=[
                pl.BlockSpec((all_rows, width), lambda i, s: (0, 0)),
                pl.BlockSpec(perm.shape, lambda i, s: (0, 0)),
                weight,
                weight,
            ],
            out_specs=[total, total],
            scratch_shapes=[pltpu.VMEM((PARTS, rows, width), BF16)],
        ),
        compiler_params=params(),
        cost_estimate=cost(4 * all_rows * width * units, 4 * PARTS * width * units),
    )(core, arrived, perm, gate, up)


def second_half(core, arrived, perm, back, gate, up, down, sum_gate, sum_up):
    all_rows, width = arrived.shape
    rows = all_rows // PARTS
    units = gate.shape[2]

    def kernel(core_ref, a_ref, p_ref, q_ref, g_ref, u_ref, d_ref, sg_ref, su_ref, o_ref, i_ref, xs, tg, tu):
        step = pl.program_id(0)

        @pl.when(step == 0)
        def _():
            unpack(a_ref, p_ref[...], xs, rows)
            tg[...] = sg_ref[...]
            tu[...] = su_ref[...]

        @pl.when(step < PARTS)
        def _():
            x = xs[step]
            tg[...] += mm(x, g_ref[0])
            tu[...] += mm(x, u_ref[0])

        @pl.when(step == PARTS - 1)
        def _():
            pre = tg[...]
            i_ref[...] = (pre * lax.logistic(pre) * tu[...]).astype(BF16)

        @pl.when(step >= PARTS)
        def _():
            xs[step - PARTS] = mm(i_ref[...], d_ref[0]).astype(BF16)

        @pl.when(step == 2 * PARTS - 1)
        def _():
            group = perm.shape[0]
            for g in range(all_rows // group):
                o_ref[g * group : (g + 1) * group, :] = repack(xs, q_ref[...], g).astype(BF16)

    last = PARTS - 1
    weight = pl.BlockSpec(
        (1, width, units), lambda i, s: (0, (1 - s[0]) * PARTS + jnp.minimum(i, last), 0)
    )
    lower = pl.BlockSpec(
        (1, units, width), lambda i, s: (0, 0, (1 - s[0]) * PARTS + jnp.maximum(i - PARTS, 0))
    )
    whole = lambda i, s: (0, 0)
    return pl.pallas_call(
        kernel,
        out_shape=[
            jax.ShapeDtypeStruct((all_rows, width), BF16),
            jax.ShapeDtypeStruct((rows, units), BF16),
        ],
        grid_spec=pltpu.PrefetchScalarGridSpec(
            num_scalar_prefetch=1,
            grid=(2 * PARTS,),
            in_specs=[
                pl.BlockSpec((all_rows, width), whole),
                pl.BlockSpec(perm.shape, whole),
                pl.BlockSpec(perm.shape, whole),
                weight,
                weight,
                lower,
                pl.BlockSpec((rows, units), whole),
                pl.BlockSpec((rows, units), whole),
            ],
            out_specs=[pl.BlockSpec((all_rows, width), whole), pl.BlockSpec((rows, units), whole)],
            scratch_shapes=[
                pltpu.VMEM((PARTS, rows, width), BF16),
                pltpu.VMEM((rows, units), F32),
                pltpu.VMEM((rows, units), F32),
            ],
        ),
        compiler_params=params(),
        cost_estimate=cost(6 * all_rows * width * units, 6 * PARTS * width * units),
    )(core, arrived, perm, back, gate, up, down, sum_gate, sum_up)


def own_down(core, inner, down, received, back):
    all_rows, width = received.shape
    rows, units = inner.shape

    def kernel(core_ref, i_ref, d_ref, r_ref, q_ref, o_ref, ys):
        step = pl.program_id(0)
        ys[step] = mm(i_ref[...], d_ref[0]).astype(BF16)

        @pl.when(step == PARTS - 1)
        def _():
            group = back.shape[0]
            for g in range(all_rows // group):
                part = slice(g * group, (g + 1) * group)
                o_ref[part, :] = (repack(ys, q_ref[...], g) + r_ref[part, :].astype(F32)).astype(BF16)

    whole = lambda i, s: (0, 0)
    return pl.pallas_call(
        kernel,
        out_shape=jax.ShapeDtypeStruct((all_rows, width), BF16),
        grid_spec=pltpu.PrefetchScalarGridSpec(
            num_scalar_prefetch=1,
            grid=(PARTS,),
            in_specs=[
                pl.BlockSpec((rows, units), whole),
                pl.BlockSpec((1, units, width), lambda i, s: (0, 0, s[0] * PARTS + i)),
                pl.BlockSpec((all_rows, width), whole),
                pl.BlockSpec(back.shape, whole),
            ],
            out_specs=pl.BlockSpec((all_rows, width), whole),
            scratch_shapes=[pltpu.VMEM((PARTS, rows, width), BF16)],
        ),
        compiler_params=params(),
        cost_estimate=cost(2 * all_rows * width * units, 2 * PARTS * width * units),
    )(core, inner, down, received, back)


def combine(flags, returned, spread, scales, hidden, tokens):
    rows, width = returned.shape
    tok, full = hidden.shape
    blocks = full // width
    picks = spread.shape[1] // blocks
    routes_each = picks // tok

    def kernel(f_ref, r_ref, s_ref, w_ref, h_ref, t_ref, o_ref):
        got = mm(s_ref[0], r_ref[...])
        live = f_ref[1] == 1
        for b in range(blocks):
            cols = slice(b * width, (b + 1) * width)
            total = h_ref[:, cols].astype(F32)
            for k in range(routes_each):
                at = b * picks + k * tok
                total += w_ref[0, k * tok : (k + 1) * tok, :] * got[at : at + tok]
            o_ref[:, cols] = jnp.where(live, total, t_ref[:, cols].astype(F32)).astype(BF16)

    whole = lambda i, s: (0, 0)
    return pl.pallas_call(
        kernel,
        out_shape=jax.ShapeDtypeStruct((tok, full), BF16),
        grid_spec=pltpu.PrefetchScalarGridSpec(
            num_scalar_prefetch=1,
            grid=(1,),
            in_specs=[
                pl.BlockSpec((rows, width), whole),
                pl.BlockSpec((1,) + spread.shape[1:], lambda i, s: (s[0], 0, 0)),
                pl.BlockSpec((1, picks, 1), lambda i, s: (s[0], 0, 0)),
                pl.BlockSpec((tok, full), whole),
                pl.BlockSpec((tok, full), whole),
            ],
            out_specs=pl.BlockSpec((tok, full), whole),
        ),
        compiler_params=params(),
        cost_estimate=cost(2 * spread.shape[1] * rows * width, 2 * rows * width),
    )(flags, returned, spread, scales, hidden, tokens)


def per_device(tokens, norm_gain, gate_weight, up_weight, down_weight, routes, route_weights):
    sections = lax.axis_size("section")
    devices = lax.axis_size("expert")
    experts = devices // SHARDS
    _, batches, tok, routes_each = routes.shape
    full = tokens.shape[2]
    capacity = min(tok, tok * routes_each * 3 // (2 * experts))
    width = full // (2 * PARTS)
    section = lax.axis_index("section")
    core = lax.rem(lax.axis_index("expert"), 2).astype(jnp.int32).reshape(1)
    own = tokens[0]

    ids = routes[0].reshape(batches, tok * routes_each)
    order = jnp.arange(tok * routes_each)
    same = (ids[:, :, None] == ids[:, None, :]) & (order[None, :] < order[:, None])
    code = (ids * capacity + jnp.sum(same.astype(jnp.int32), axis=2)).reshape(batches, tok, routes_each)
    row = jnp.arange(devices * PARTS * capacity, dtype=jnp.int32)
    device = row // (PARTS * capacity)
    row_block = (device % 2) * PARTS + (row % (PARTS * capacity)) // capacity
    row_slot = (device // SHARDS) * capacity + row % capacity
    blocks = jnp.arange(2 * PARTS, dtype=jnp.int32)
    code = jnp.moveaxis(code, 2, 1)
    hits = (code[:, None, :, :, None] == row_slot) & (blocks[:, None, None, None] == row_block)
    spread = hits.reshape(batches, -1, row.shape[0]).astype(BF16)
    hits_t = (row_slot[:, None, None, None] == code[:, None, :, None, :]) & (
        row_block[:, None, None, None] == blocks[:, None]
    )
    pick = jnp.any(hits_t, axis=2).reshape(batches, row.shape[0], -1).astype(BF16)
    scales = jnp.moveaxis(route_weights[0], 2, 1).reshape(batches, tok * routes_each, 1)

    group = 8 * PARTS * capacity
    at = jnp.arange(group, dtype=jnp.int32)
    wanted = (at % (8 * capacity)) // capacity * (PARTS * capacity) + at // (8 * capacity) * capacity + at % capacity
    perm = (wanted[:, None] == at[None, :]).astype(BF16)
    back = (at[:, None] == wanted[None, :]).astype(BF16)

    swap = [(i, i ^ 1) for i in range(devices)]
    hidden = own
    kept = None
    for step in range(batches + sections - 1):
        if step > 0:
            begins = max(0, step - batches)
            pairs = [(i, i + 1) for i in range(begins, min(step, sections - 1))]
            if step < batches:
                pairs.append((step, 0))
            else:
                pairs.append((sections - 1, step - batches))
            hidden = lax.ppermute(current, "section", pairs)
            if step >= batches:
                home = step - batches
                kept = hidden if kept is None else jnp.where(section == home, hidden, kept)
        batch = step - section
        pos = jnp.clip(batch, 0, batches - 1).astype(jnp.int32)
        flags = jnp.stack([pos, (batch >= 0).astype(jnp.int32)])
        packed = front(pos.reshape(1), hidden, norm_gain, pick, width=width)
        arrived = lax.all_to_all(packed, "expert", split_axis=0, concat_axis=0, tiled=True)
        others = lax.ppermute(arrived, "expert", swap)
        sum_gate, sum_up = first_half(core, arrived, perm, gate_weight, up_weight)
        leaving, inner = second_half(
            core, others, perm, back, gate_weight, up_weight, down_weight, sum_gate, sum_up
        )
        received = lax.ppermute(leaving, "expert", swap)
        partial_value = own_down(core, inner, down_weight, received, back)
        returned = lax.all_to_all(partial_value, "expert", split_axis=0, concat_axis=0, tiled=True)
        current = combine(flags, returned, spread, scales, hidden, own)
    return jnp.where(section == sections - 1, current, kept)[None]


def solution(mesh):
    return jax.shard_map(
        per_device,
        mesh=mesh,
        in_specs=(
            P("section", "expert", None),
            P("section", None),
            P("section", None, "expert"),
            P("section", None, "expert"),
            P("section", "expert", None),
            P("section", None, "expert", None),
            P("section", None, "expert", None),
        ),
        out_specs=P("section", "expert", None),
        check_vma=False,
    )
```

time: 1000 us -> 631 us (0.63)
  the two profiles are of different devices: /device:TPU:1 before, /device:TPU:64 now
where the time goes in v1:
time: 631 us; the launch traced here: 621 us
  waiting for transfers between devices  194 us (31%)
  blocking collectives  178 us (28%)
  Pallas kernels  108 us (17%)
  local copies, waits for them, and re-layouts  76.2 us (12%)
  starting transfers between devices  58.2 us (9%)
    all_to_all x7, blocking collectives, per_device(): lax.all_to_all(packed, 'expert', split_axis=0, concat_axis=0, tiled=True)  178 us
    all_to_all x7, waiting for transfers between devices, per_device(): lax.all_to_all(partial_value, 'expert', split_axis=0, concat_axis=0, tile...  150 us
    unnamed x74, local copies, waits for them, and re-layouts  73.3 us
    pallas_call x7, Pallas kernels, second_half(): pl.pallas_call(kernel, out_shape=[jax.ShapeDtypeStruct((all_rows, width),...  42.1 us
    all_to_all x7, starting transfers between devices, per_device(): lax.all_to_all(partial_value, 'expert', split_axis=0, concat_axis=0, tile...  32.9 us
    ppermute x6, waiting for transfers between devices, per_device(): hidden = lax.ppermute(current, 'section', pairs)  24.4 us
    pallas_call x7, Pallas kernels, first_half(): pl.pallas_call(kernel, out_shape=[jax.ShapeDtypeStruct((rows, units), F32...  22.5 us
    ppermute x6, starting transfers between devices, per_device(): hidden = lax.ppermute(current, 'section', pairs)  20.9 us
  transfers between devices with their start and end apart: 27, of which 19 were waited for; matrix products, arithmetic and copies ran while one was open for 0% of the time, Pallas kernels for 4%

profile of v1, /device:TPU:64, one launch (start us, length us, event | category | flops | bytes accessed | tf_op | source)
XLA Modules:
  0.0 620.7 jit_solution(9245754066459767949)
XLA Ops:
  7.8 28.1 %all_to_all.154 = bf16[32,24,896]{2,1,0:T(8,128)(2,1)} all-to-all(bf16[32,24,896]{2,1,0:T(8,128)(2,1)S(1)} %bitcast.77), channel_id=1, replica_groups=mesh['section'=4,'expert'=32] {'expert'}, dimensions={0} | all-to-all | bytes 2752512 | tf_op jit(solution)/shard_map/all_to_all | solution.py:317
  36.3 3.1 copy-done
  39.3 3.1 copy-done.7
  42.4 4.5 shard_map.74
  47.2 3.1 copy-done.8
  50.3 7.2 %shard_map.75 = (bf16[768,896]{1,0:T(8,128)(2,1)S(1)}, bf16[192,512]{1,0:T(8,128)(2,1)S(1)}) custom-call(s32[1]{0:T(128)} %bitcast.2.core_ref, bf16[768,896]{1,0:T(8,128)(2,1)} %collective-permute-done.a_ref, bf16[192,192]{1,0:T(8,128)(2,1)S(1)} %get-tuple-element.62.p_ref, bf16[192,192]{1,0:T(8,128)(2,1)S(1)} %get-tuple-element.61.q_ref, ...), custom_call_target="tpu_custom_call" | custom-call | flops 2113929216 | bytes 11010048 | tf_op jit(solution)/shard_map/pallas_call | solution.py:156
  60.7 3.6 shard_map.76
  64.3 4.8 all-to-all-start.1
  69.9 20.8 %all-to-all-done.1 = bf16[32,24,896]{2,1,0:T(8,128)(2,1)} async-done(((bf16[32,24,896]{2,1,0:T(8,128)(2,1)}), bf16[32,24,896]{2,1,0:T(8,128)(2,1)}, u32[]{:S(2)}, u32[]{:S(2)}) %all-to-all-start.1) | async-done | bytes 1376288 | tf_op jit(solution)/shard_map/all_to_all | solution.py:325
  94.6 23.8 %all_to_all.155 = bf16[32,24,896]{2,1,0:T(8,128)(2,1)S(1)} all-to-all(bf16[32,24,896]{2,1,0:T(8,128)(2,1)S(1)} %bitcast.78), channel_id=1, replica_groups=mesh['section'=4,'expert'=32] {'expert'}, dimensions={0} | all-to-all | bytes 2752512 | tf_op jit(solution)/shard_map/all_to_all | solution.py:317
  118.7 3.1 copy-done.1
  121.7 3.1 copy-done.9
  127.9 3.1 copy-done.16
  130.9 5.8 shard_map.80
  143.8 4.7 all-to-all-start.3
  148.6 21.5 %all-to-all-done.3 = bf16[32,24,896]{2,1,0:T(8,128)(2,1)} async-done(((bf16[32,24,896]{2,1,0:T(8,128)(2,1)}), bf16[32,24,896]{2,1,0:T(8,128)(2,1)}, u32[]{:S(2)}, u32[]{:S(2)}) %all-to-all-start.3) | async-done | bytes 1376288 | tf_op jit(solution)/shard_map/all_to_all | solution.py:325
  172.5 10.3 %collective-permute-start.5 = (bf16[16,7168]{1,0:T(8,128)(2,1)S(1)}, bf16[16,7168]{1,0:T(8,128)(2,1)S(1)}, u32[]{:S(2)}, u32[]{:S(2)}) collective-permute-start(bf16[16,7168]{1,0:T(8,128)(2,1)S(1)} %shard_map.82), channel_id=1, source_target_pairs={{0,32},{32,64},{64,0},{1,33},{33,65},{65,1},{2,34},{34,66},{66,2},... | collective-permute-start | bytes 688136 | tf_op jit(solution)/shard_map/ppermute | solution.py:309
  182.8 4.5 collective-permute-done.5.h_ref
  188.0 25.1 %all_to_all.156 = bf16[32,24,896]{2,1,0:T(8,128)(2,1)S(1)} all-to-all(bf16[32,24,896]{2,1,0:T(8,128)(2,1)S(1)} %bitcast.79), channel_id=1, replica_groups=mesh['section'=4,'expert'=32] {'expert'}, dimensions={0} | all-to-all | bytes 2752512 | tf_op jit(solution)/shard_map/all_to_all | solution.py:317
  213.4 3.1 copy-done.2
  216.4 3.1 copy-done.10
  219.5 3.0 shard_map.84
  222.6 3.1 copy-done.17
  225.6 5.8 shard_map.85
  238.3 4.7 all-to-all-start.5
  243.1 21.5 %all-to-all-done.5 = bf16[32,24,896]{2,1,0:T(8,128)(2,1)} async-done(((bf16[32,24,896]{2,1,0:T(8,128)(2,1)}), bf16[32,24,896]{2,1,0:T(8,128)(2,1)}, u32[]{:S(2)}, u32[]{:S(2)}) %all-to-all-start.5) | async-done | bytes 1376288 | tf_op jit(solution)/shard_map/all_to_all | solution.py:325
  267.2 6.0 collective-permute-done.8.h_ref
  273.9 25.1 %all_to_all.157 = bf16[32,24,896]{2,1,0:T(8,128)(2,1)S(1)} all-to-all(bf16[32,24,896]{2,1,0:T(8,128)(2,1)S(1)} %bitcast.80), channel_id=1, replica_groups=mesh['section'=4,'expert'=32] {'expert'}, dimensions={0} | all-to-all | bytes 2752512 | tf_op jit(solution)/shard_map/all_to_all | solution.py:317
  299.4 3.1 copy-done.3
  302.5 3.1 copy-done.11
  305.6 3.0 shard_map.89
  308.6 3.1 copy-done.18
  311.7 5.9 shard_map.90
  324.4 4.7 all-to-all-start.7
  329.2 21.5 %all-to-all-done.7 = bf16[32,24,896]{2,1,0:T(8,128)(2,1)} async-done(((bf16[32,24,896]{2,1,0:T(8,128)(2,1)}), bf16[32,24,896]{2,1,0:T(8,128)(2,1)}, u32[]{:S(2)}, u32[]{:S(2)}) %all-to-all-start.7) | async-done | bytes 1376288 | tf_op jit(solution)/shard_map/all_to_all | solution.py:325
  354.8 4.5 collective-permute-done.11.h_ref
  360.0 25.1 %all_to_all.158 = bf16[32,24,896]{2,1,0:T(8,128)(2,1)S(1)} all-to-all(bf16[32,24,896]{2,1,0:T(8,128)(2,1)S(1)} %bitcast.81), channel_id=1, replica_groups=mesh['section'=4,'expert'=32] {'expert'}, dimensions={0} | all-to-all | bytes 2752512 | tf_op jit(solution)/shard_map/all_to_all | solution.py:317
  385.3 3.1 copy-done.4
  388.4 3.1 copy-done.12
  394.5 3.1 copy-done.19
  397.6 5.8 shard_map.95
  410.3 4.7 all-to-all-start.9
  415.1 21.5 %all-to-all-done.9 = bf16[32,24,896]{2,1,0:T(8,128)(2,1)} async-done(((bf16[32,24,896]{2,1,0:T(8,128)(2,1)}), bf16[32,24,896]{2,1,0:T(8,128)(2,1)}, u32[]{:S(2)}, u32[]{:S(2)}) %all-to-all-start.9) | async-done | bytes 1376288 | tf_op jit(solution)/shard_map/all_to_all | solution.py:325
  436.6 3.1 shard_map.97
  439.7 4.7 collective-permute-start.14
  444.4 4.6 collective-permute-done.14.h_ref
  449.7 25.4 %all_to_all.159 = bf16[32,24,896]{2,1,0:T(8,128)(2,1)S(1)} all-to-all(bf16[32,24,896]{2,1,0:T(8,128)(2,1)S(1)} %bitcast.82), channel_id=1, replica_groups=mesh['section'=4,'expert'=32] {'expert'}, dimensions={0} | all-to-all | bytes 2752512 | tf_op jit(solution)/shard_map/all_to_all | solution.py:317
  475.3 3.1 copy-done.5
  478.4 3.1 copy-done.13
  484.5 3.1 copy-done.20
  487.5 5.8 shard_map.100
  500.3 4.7 all-to-all-start.11
  505.0 21.5 %all-to-all-done.11 = bf16[32,24,896]{2,1,0:T(8,128)(2,1)} async-done(((bf16[32,24,896]{2,1,0:T(8,128)(2,1)}), bf16[32,24,896]{2,1,0:T(8,128)(2,1)}, u32[]{:S(2)}, u32[]{:S(2)}) %all-to-all-start.11) | async-done | bytes 1376288 | tf_op jit(solution)/shard_map/all_to_all | solution.py:325
  526.6 3.1 shard_map.102
  529.7 3.5 collective-permute-start.17
  533.2 4.8 collective-permute-done.17.h_ref
  539.6 25.1 %all_to_all.160 = bf16[32,24,896]{2,1,0:T(8,128)(2,1)S(1)} all-to-all(bf16[32,24,896]{2,1,0:T(8,128)(2,1)S(1)} %bitcast.76), channel_id=1, replica_groups=mesh['section'=4,'expert'=32] {'expert'}, dimensions={0} | all-to-all | bytes 2752512 | tf_op jit(solution)/shard_map/all_to_all | solution.py:317
  564.9 3.1 copy-done.6
  568.0 3.1 copy-done.14
  571.1 3.0 shard_map.104
  574.1 3.1 copy-done.21
  577.2 5.8 shard_map.105
  589.9 4.7 all-to-all-start.13
  594.6 21.5 %all-to-all-done.13 = bf16[32,24,896]{2,1,0:T(8,128)(2,1)} async-done(((bf16[32,24,896]{2,1,0:T(8,128)(2,1)}), bf16[32,24,896]{2,1,0:T(8,128)(2,1)}, u32[]{:S(2)}, u32[]{:S(2)}) %all-to-all-start.13) | async-done | bytes 1376288 | tf_op jit(solution)/shard_map/all_to_all | solution.py:325
  (138 shorter events, 86.1 us)
Async XLA Ops:
  2.5 3.5 copy-start.24
  2.5 3.5 copy-start.32
  3.6 43.4 %slice-start = ((s8[7340032]{0:T(1024)(128)(4,1)}), s8[3145728]{0:T(1024)(128)(4,1)S(1)}, s32[]{:S(2)}) async-start(s8[7340032]{0:T(1024)(128)(4,1)} %bitcast.65), calls=%async_computation.14 | async-start | bytes 6291456
  6.0 1.1 copy-start.22
  35.9 11.1 %collective-permute-start = (bf16[768,896]{1,0:T(8,128)(2,1)}, bf16[768,896]{1,0:T(8,128)(2,1)}, u32[]{:S(2)}, u32[]{:S(2)}) collective-permute-start(bf16[768,896]{1,0:T(8,128)(2,1)} %bitcast.22.a_ref), channel_id=1, source_target_pairs={{0,1},{1,0},{2,3},{3,2},{4,5},{5,4},{6,7},{7,6},{8,9},{9,8},{10,11... | collective-permute-start | bytes 4128776 | tf_op jit(solution)/shard_map/ppermute | solution.py:318
  36.3 3.1 copy-start
  39.3 3.1 copy-start.7
  42.4 4.5 slice-start.1
  42.4 4.8 copy-start.15
  47.2 3.1 copy-start.8
  57.5 3.2 collective-permute-start.1
  64.3 4.8 copy-start.33
  64.3 26.4 %all-to-all-start.1 = ((bf16[32,24,896]{2,1,0:T(8,128)(2,1)}), bf16[32,24,896]{2,1,0:T(8,128)(2,1)}, u32[]{:S(2)}, u32[]{:S(2)}) async-start(bf16[32,24,896]{2,1,0:T(8,128)(2,1)} %bitcast.23), calls=%async_computation.1 | async-start | bytes 2752512 | tf_op jit(solution)/shard_map/all_to_all | solution.py:325
  69.1 21.6 %copy-start.25 = (bf16[1,16,7168]{2,1,0:T(8,128)(2,1)S(1)}, bf16[1,16,7168]{2,1,0:T(8,128)(2,1)}, u32[]{:S(2)}) copy-start(bf16[1,16,7168]{2,1,0:T(8,128)(2,1)} %param.7) | copy-start | bytes 688132
  90.7 3.2 copy-start.23
  93.2 0.7 collective-permute-start.2
  118.4 9.4 %collective-permute-start.3 = (bf16[768,896]{1,0:T(8,128)(2,1)S(1)}, bf16[768,896]{1,0:T(8,128)(2,1)S(1)}, u32[]{:S(2)}, u32[]{:S(2)}) collective-permute-start(bf16[768,896]{1,0:T(8,128)(2,1)S(1)} %bitcast.89), channel_id=1, source_target_pairs={{0,1},{1,0},{2,3},{3,2},{4,5},{5,4},{6,7},{7,6},{8,9},{9,8},{10,11... | collective-permute-start | bytes 4128776 | tf_op jit(solution)/shard_map/ppermute | solution.py:318
  118.7 3.1 copy-start.1
  121.7 3.1 copy-start.9
  127.8 3.1 copy-start.16
  136.8 3.4 collective-permute-start.4
  142.7 1.1 copy-start.27
  143.8 26.3 %all-to-all-start.3 = ((bf16[32,24,896]{2,1,0:T(8,128)(2,1)}), bf16[32,24,896]{2,1,0:T(8,128)(2,1)}, u32[]{:S(2)}, u32[]{:S(2)}) async-start(bf16[32,24,896]{2,1,0:T(8,128)(2,1)} %bitcast.84), calls=%async_computation.3 | async-start | bytes 2752512 | tf_op jit(solution)/shard_map/all_to_all | solution.py:325
  172.5 14.8 %collective-permute-start.5 = (bf16[16,7168]{1,0:T(8,128)(2,1)S(1)}, bf16[16,7168]{1,0:T(8,128)(2,1)S(1)}, u32[]{:S(2)}, u32[]{:S(2)}) collective-permute-start(bf16[16,7168]{1,0:T(8,128)(2,1)S(1)} %shard_map.82), channel_id=1, source_target_pairs={{0,32},{32,64},{64,0},{1,33},{33,65},{65,1},{2,34},{34,66},{66,2},... | collective-permute-start | bytes 688136 | tf_op jit(solution)/shard_map/ppermute | solution.py:309
  213.1 9.4 %collective-permute-start.6 = (bf16[768,896]{1,0:T(8,128)(2,1)S(1)}, bf16[768,896]{1,0:T(8,128)(2,1)S(1)}, u32[]{:S(2)}, u32[]{:S(2)}) collective-permute-start(bf16[768,896]{1,0:T(8,128)(2,1)S(1)} %bitcast.91), channel_id=1, source_target_pairs={{0,1},{1,0},{2,3},{3,2},{4,5},{5,4},{6,7},{7,6},{8,9},{9,8},{10,11... | collective-permute-start | bytes 4128776 | tf_op jit(solution)/shard_map/ppermute | solution.py:318
  213.3 3.1 copy-start.2
  216.4 3.1 copy-start.10
  222.5 3.1 copy-start.17
  231.5 3.2 collective-permute-start.7
  237.3 1.1 copy-start.28
  238.3 26.3 %all-to-all-start.5 = ((bf16[32,24,896]{2,1,0:T(8,128)(2,1)}), bf16[32,24,896]{2,1,0:T(8,128)(2,1)}, u32[]{:S(2)}, u32[]{:S(2)}) async-start(bf16[32,24,896]{2,1,0:T(8,128)(2,1)} %bitcast.85), calls=%async_computation.5 | async-start | bytes 2752512 | tf_op jit(solution)/shard_map/all_to_all | solution.py:325
  267.1 6.1 collective-permute-start.8
  298.9 9.6 %collective-permute-start.9 = (bf16[768,896]{1,0:T(8,128)(2,1)S(1)}, bf16[768,896]{1,0:T(8,128)(2,1)S(1)}, u32[]{:S(2)}, u32[]{:S(2)}) collective-permute-start(bf16[768,896]{1,0:T(8,128)(2,1)S(1)} %bitcast.93), channel_id=1, source_target_pairs={{0,1},{1,0},{2,3},{3,2},{4,5},{5,4},{6,7},{7,6},{8,9},{9,8},{10,11... | collective-permute-start | bytes 4128776 | tf_op jit(solution)/shard_map/ppermute | solution.py:318
  299.4 3.1 copy-start.3
  302.5 3.1 copy-start.11
  308.6 3.1 copy-start.18
  317.5 3.2 collective-permute-start.10
  323.3 1.1 copy-start.29
  324.4 26.3 %all-to-all-start.7 = ((bf16[32,24,896]{2,1,0:T(8,128)(2,1)}), bf16[32,24,896]{2,1,0:T(8,128)(2,1)}, u32[]{:S(2)}, u32[]{:S(2)}) async-start(bf16[32,24,896]{2,1,0:T(8,128)(2,1)} %bitcast.86), calls=%async_computation.7 | async-start | bytes 2752512 | tf_op jit(solution)/shard_map/all_to_all | solution.py:325
  353.2 6.2 collective-permute-start.11
  385.1 9.4 %collective-permute-start.12 = (bf16[768,896]{1,0:T(8,128)(2,1)S(1)}, bf16[768,896]{1,0:T(8,128)(2,1)S(1)}, u32[]{:S(2)}, u32[]{:S(2)}) collective-permute-start(bf16[768,896]{1,0:T(8,128)(2,1)S(1)} %bitcast.95), channel_id=1, source_target_pairs={{0,1},{1,0},{2,3},{3,2},{4,5},{5,4},{6,7},{7,6},{8,9},{9,8},{10,11... | collective-permute-start | bytes 4128776 | tf_op jit(solution)/shard_map/ppermute | solution.py:318
  385.3 3.1 copy-start.4
  388.4 3.1 copy-start.12
  394.5 3.1 copy-start.19
  403.4 3.2 collective-permute-start.13
  409.2 1.1 copy-start.30
  410.3 26.3 %all-to-all-start.9 = ((bf16[32,24,896]{2,1,0:T(8,128)(2,1)}), bf16[32,24,896]{2,1,0:T(8,128)(2,1)}, u32[]{:S(2)}, u32[]{:S(2)}) async-start(bf16[32,24,896]{2,1,0:T(8,128)(2,1)} %bitcast.87), calls=%async_computation.9 | async-start | bytes 2752512 | tf_op jit(solution)/shard_map/all_to_all | solution.py:325
  439.7 9.3 %collective-permute-start.14 = (bf16[16,7168]{1,0:T(8,128)(2,1)}, bf16[16,7168]{1,0:T(8,128)(2,1)S(1)}, u32[]{:S(2)}, u32[]{:S(2)}) collective-permute-start(bf16[16,7168]{1,0:T(8,128)(2,1)} %shard_map.97), channel_id=1, source_target_pairs={{32,64},{64,96},{96,32},{33,65},{65,97},{97,33},{34,66},{66,98},{9... | collective-permute-start | bytes 688136 | tf_op jit(solution)/shard_map/ppermute | solution.py:309
  475.1 9.4 %collective-permute-start.15 = (bf16[768,896]{1,0:T(8,128)(2,1)S(1)}, bf16[768,896]{1,0:T(8,128)(2,1)S(1)}, u32[]{:S(2)}, u32[]{:S(2)}) collective-permute-start(bf16[768,896]{1,0:T(8,128)(2,1)S(1)} %bitcast.97), channel_id=1, source_target_pairs={{0,1},{1,0},{2,3},{3,2},{4,5},{5,4},{6,7},{7,6},{8,9},{9,8},{10,11... | collective-permute-start | bytes 4128776 | tf_op jit(solution)/shard_map/ppermute | solution.py:318
  475.3 3.1 copy-start.5
  478.4 3.1 copy-start.13
  484.5 3.1 copy-start.20
  493.4 3.2 collective-permute-start.16
  499.2 1.1 copy-start.31
  500.3 26.3 %all-to-all-start.11 = ((bf16[32,24,896]{2,1,0:T(8,128)(2,1)}), bf16[32,24,896]{2,1,0:T(8,128)(2,1)}, u32[]{:S(2)}, u32[]{:S(2)}) async-start(bf16[32,24,896]{2,1,0:T(8,128)(2,1)} %bitcast.88), calls=%async_computation.11 | async-start | bytes 2752512 | tf_op jit(solution)/shard_map/all_to_all | solution.py:325
  529.7 8.2 %collective-permute-start.17 = (bf16[16,7168]{1,0:T(8,128)(2,1)}, bf16[16,7168]{1,0:T(8,128)(2,1)}, u32[]{:S(2)}, u32[]{:S(2)}) collective-permute-start(bf16[16,7168]{1,0:T(8,128)(2,1)} %shard_map.102), channel_id=1, source_target_pairs={{64,96},{96,64},{65,97},{97,65},{66,98},{98,66},{67,99},{99,67},{6... | collective-permute-start | bytes 688136 | tf_op jit(solution)/shard_map/ppermute | solution.py:309
  564.6 9.4 %collective-permute-start.18 = (bf16[768,896]{1,0:T(8,128)(2,1)S(1)}, bf16[768,896]{1,0:T(8,128)(2,1)S(1)}, u32[]{:S(2)}, u32[]{:S(2)}) collective-permute-start(bf16[768,896]{1,0:T(8,128)(2,1)S(1)} %bitcast.99), channel_id=1, source_target_pairs={{0,1},{1,0},{2,3},{3,2},{4,5},{5,4},{6,7},{7,6},{8,9},{9,8},{10,11... | collective-permute-start | bytes 4128776 | tf_op jit(solution)/shard_map/ppermute | solution.py:318
  564.9 3.1 copy-start.6
  568.0 3.1 copy-start.14
  574.1 3.1 copy-start.21
  583.0 3.2 collective-permute-start.19
  588.8 1.1 copy-start.26
  589.9 26.3 %all-to-all-start.13 = ((bf16[32,24,896]{2,1,0:T(8,128)(2,1)}), bf16[32,24,896]{2,1,0:T(8,128)(2,1)}, u32[]{:S(2)}, u32[]{:S(2)}) async-start(bf16[32,24,896]{2,1,0:T(8,128)(2,1)} %bitcast.83), calls=%async_computation.13 | async-start | bytes 2752512 | tf_op jit(solution)/shard_map/all_to_all | solution.py:325

commit v2 on v1

v2 whole, which is shorter than its diff:
```python
import jax
import jax.numpy as jnp
from jax import lax
from jax.experimental import pallas as pl
from jax.experimental.pallas import tpu as pltpu
from jax.sharding import PartitionSpec as P

SHARDS = 4
PARTS = 4

F32 = jnp.float32
BF16 = jnp.bfloat16


def params():
    return pltpu.CompilerParams(vmem_limit_bytes=12 * 1024 * 1024)


def cost(flops, bytes_accessed):
    return pl.CostEstimate(flops=int(flops), bytes_accessed=int(bytes_accessed), transcendentals=0)


def mm(a, b):
    return jnp.dot(a, b, preferred_element_type=F32)


def batch_at(step, place, batches):
    return jnp.clip(step - place[0], 0, batches - 1)


def front(place, hidden, gain, pick, step, *, width):
    tok, full = hidden.shape
    batches, rows, depth = pick.shape
    blocks = full // width

    def kernel(place_ref, h_ref, g_ref, p_ref, o_ref):
        x = h_ref[...].astype(F32)
        scale = lax.rsqrt(jnp.mean(x * x, axis=-1, keepdims=True) + 1e-06)
        normed = (x * scale * g_ref[...]).astype(BF16)
        stack = jnp.concatenate([normed[:, b * width : (b + 1) * width] for b in range(blocks)], axis=0)
        o_ref[...] = mm(p_ref[0], stack).astype(BF16)

    return pl.pallas_call(
        kernel,
        out_shape=jax.ShapeDtypeStruct((rows, width), BF16),
        grid_spec=pltpu.PrefetchScalarGridSpec(
            num_scalar_prefetch=1,
            grid=(1,),
            in_specs=[
                pl.BlockSpec((tok, full), lambda i, s: (0, 0)),
                pl.BlockSpec((1, full), lambda i, s: (0, 0)),
                pl.BlockSpec((1, rows, depth), lambda i, s: (batch_at(step, s, batches), 0, 0)),
            ],
            out_specs=pl.BlockSpec((rows, width), lambda i, s: (0, 0)),
        ),
        compiler_params=params(),
        cost_estimate=cost(2 * rows * depth * width, 2 * rows * width),
    )(place, hidden, gain, pick)


def stage(weights):
    def kernel(*refs):
        count = len(weights)
        sems = refs[-1]
        copies = [
            pltpu.make_async_copy(refs[i], refs[count + i], sems.at[i]) for i in range(count)
        ]
        for copy in copies:
            copy.start()
        for copy in copies:
            copy.wait()

    staged = pl.pallas_call(
        kernel,
        out_shape=[pltpu.VMEM(w.shape, w.dtype) for w in weights],
        in_specs=[pl.BlockSpec(memory_space=pltpu.HBM)] * len(weights),
        out_specs=[pl.BlockSpec(memory_space=pltpu.VMEM)] * len(weights),
        scratch_shapes=[pltpu.SemaphoreType.DMA((len(weights),))],
        compiler_params=params(),
        cost_estimate=cost(0, 2 * sum(w.size * 2 for w in weights)),
    )(*[pltpu.with_memory_space_constraint(w, pltpu.HBM) for w in weights])
    return staged


def held(array):
    return pltpu.with_memory_space_constraint(array, pltpu.VMEM)


def unpack(packed_ref, perm, xs, rows):
    group, width = perm.shape[0], packed_ref.shape[1]
    piece = group // PARTS
    for g in range(rows // piece):
        moved = mm(perm, packed_ref[g * group : (g + 1) * group, :]).astype(BF16)
        for b in range(PARTS):
            xs[g * piece : (g + 1) * piece, b * width : (b + 1) * width] = moved[b * piece : (b + 1) * piece]


def down_packed(inner, down_ref, half, perm, ys, out_ref):
    group, width = perm.shape[0], out_ref.shape[1]
    piece = group // PARTS
    for b in range(PARTS):
        cols = pl.ds(pl.multiple_of(half * (PARTS * width) + b * width, 128), width)
        ys[b] = mm(inner, down_ref[0, :, cols]).astype(BF16)
    for g in range(out_ref.shape[0] // group):
        stack = jnp.concatenate([ys[b, g * piece : (g + 1) * piece, :] for b in range(PARTS)], axis=0)
        out_ref[g * group : (g + 1) * group, :] = mm(perm, stack).astype(BF16)


SMEM_IN = pl.BlockSpec(memory_space=pltpu.SMEM)
VMEM_IN = pl.BlockSpec(memory_space=pltpu.VMEM)


def first_half(place, arrived, perm, gate, up):
    all_rows, width = arrived.shape
    rows = all_rows // PARTS
    units = gate.shape[2]

    def kernel(place_ref, a_ref, p_ref, g_ref, u_ref, og_ref, ou_ref, xs):
        unpack(a_ref, p_ref[...], xs, rows)
        depth = PARTS * width
        part = pl.ds(pl.multiple_of(place_ref[1] * depth, depth), depth)
        og_ref[...] = mm(xs[...], g_ref[0, part, :])
        ou_ref[...] = mm(xs[...], u_ref[0, part, :])

    return pl.pallas_call(
        kernel,
        out_shape=[jax.ShapeDtypeStruct((rows, units), F32)] * 2,
        in_specs=[SMEM_IN] + [VMEM_IN] * 4,
        out_specs=[VMEM_IN] * 2,
        scratch_shapes=[pltpu.VMEM((rows, PARTS * width), BF16)],
        compiler_params=params(),
        cost_estimate=cost(4 * all_rows * width * units, 4 * PARTS * width * units),
    )(place, arrived, perm, held(gate), held(up))


def second_half(place, arrived, perm, back, gate, up, down, sum_gate, sum_up):
    all_rows, width = arrived.shape
    rows = all_rows // PARTS
    units = gate.shape[2]

    def kernel(place_ref, a_ref, p_ref, q_ref, g_ref, u_ref, d_ref, sg_ref, su_ref, o_ref, i_ref, xs, ys):
        unpack(a_ref, p_ref[...], xs, rows)
        depth = PARTS * width
        other = 1 - place_ref[1]
        part = pl.ds(pl.multiple_of(other * depth, depth), depth)
        pre = sg_ref[...] + mm(xs[...], g_ref[0, part, :])
        upper = su_ref[...] + mm(xs[...], u_ref[0, part, :])
        i_ref[...] = (pre * lax.logistic(pre) * upper).astype(BF16)
        down_packed(i_ref[...], d_ref, other, q_ref[...], ys, o_ref)

    return pl.pallas_call(
        kernel,
        out_shape=[
            jax.ShapeDtypeStruct((all_rows, width), BF16),
            jax.ShapeDtypeStruct((rows, units), BF16),
        ],
        in_specs=[SMEM_IN] + [VMEM_IN] * 8,
        out_specs=[VMEM_IN] * 2,
        scratch_shapes=[
            pltpu.VMEM((rows, PARTS * width), BF16),
            pltpu.VMEM((PARTS, rows, width), BF16),
        ],
        compiler_params=params(),
        cost_estimate=cost(6 * all_rows * width * units, 6 * PARTS * width * units),
    )(place, arrived, perm, back, held(gate), held(up), held(down), sum_gate, sum_up)


def own_down(place, inner, down, back):
    rows, units = inner.shape
    width = down.shape[2] // (2 * PARTS)

    def kernel(place_ref, i_ref, d_ref, q_ref, o_ref, ys):
        down_packed(i_ref[...], d_ref, place_ref[1], q_ref[...], ys, o_ref)

    return pl.pallas_call(
        kernel,
        out_shape=jax.ShapeDtypeStruct((rows * PARTS, width), BF16),
        in_specs=[SMEM_IN] + [VMEM_IN] * 3,
        out_specs=VMEM_IN,
        scratch_shapes=[pltpu.VMEM((PARTS, rows, width), BF16)],
        compiler_params=params(),
        cost_estimate=cost(2 * rows * PARTS * width * units, 2 * PARTS * width * units),
    )(place, inner, held(down), back)


def combine(place, returned, spread, scales, hidden, tokens, step, finished=()):
    rows, width = returned.shape
    tok, full = hidden.shape
    batches = spread.shape[0]
    blocks = full // width
    picks = spread.shape[1] // blocks
    routes_each = picks // tok

    def kernel(place_ref, r_ref, s_ref, w_ref, h_ref, t_ref, *rest):
        o_ref = rest[-1]
        got = mm(s_ref[0], r_ref[...])
        section = place_ref[0]
        for b in range(blocks):
            cols = slice(b * width, (b + 1) * width)
            total = h_ref[:, cols].astype(F32)
            for k in range(routes_each):
                at = b * picks + k * tok
                total += w_ref[0, k * tok : (k + 1) * tok, :1] * got[at : at + tok]
            total = jnp.where(section <= step, total, t_ref[:, cols].astype(F32))
            for home, f_ref in enumerate(rest[:-1]):
                total = jnp.where(section == home, f_ref[:, cols].astype(F32), total)
            o_ref[:, cols] = total.astype(BF16)

    whole = lambda i, s: (0, 0)
    chosen = lambda i, s: (batch_at(step, s, batches), 0, 0)
    return pl.pallas_call(
        kernel,
        out_shape=jax.ShapeDtypeStruct((tok, full), BF16),
        grid_spec=pltpu.PrefetchScalarGridSpec(
            num_scalar_prefetch=1,
            grid=(1,),
            in_specs=[
                pl.BlockSpec((rows, width), whole),
                pl.BlockSpec((1,) + spread.shape[1:], chosen),
                pl.BlockSpec((1, picks, 128), chosen),
            ]
            + [pl.BlockSpec((tok, full), whole)] * (2 + len(finished)),
            out_specs=pl.BlockSpec((tok, full), whole),
        ),
        compiler_params=params(),
        cost_estimate=cost(2 * spread.shape[1] * rows * width, 2 * rows * width),
    )(place, returned, spread, scales, hidden, tokens, *finished)


def per_device(tokens, norm_gain, gate_weight, up_weight, down_weight, routes, route_weights):
    sections = lax.axis_size("section")
    devices = lax.axis_size("expert")
    experts = devices // SHARDS
    _, batches, tok, routes_each = routes.shape
    full = tokens.shape[2]
    capacity = min(tok, tok * routes_each * 3 // (2 * experts))
    width = full // (2 * PARTS)
    section = lax.axis_index("section")
    core = lax.axis_index("expert") % 2
    place = jnp.stack([section, core]).astype(jnp.int32)
    own = tokens[0]

    ids = routes[0].reshape(batches, tok * routes_each)
    order = jnp.arange(tok * routes_each)
    same = (ids[:, :, None] == ids[:, None, :]) & (order[None, :] < order[:, None])
    code = (ids * capacity + jnp.sum(same.astype(jnp.int32), axis=2)).reshape(batches, tok, routes_each)
    row = jnp.arange(devices * PARTS * capacity, dtype=jnp.int32)
    device = row // (PARTS * capacity)
    row_block = (device % 2) * PARTS + (row % (PARTS * capacity)) // capacity
    row_slot = (device // SHARDS) * capacity + row % capacity
    blocks = jnp.arange(2 * PARTS, dtype=jnp.int32)
    code = jnp.moveaxis(code, 2, 1)
    hits = (code[:, None, :, :, None] == row_slot) & (blocks[:, None, None, None] == row_block)
    spread = hits.reshape(batches, -1, row.shape[0]).astype(BF16)
    hits_t = (row_slot[:, None, None, None] == code[:, None, :, None, :]) & (
        row_block[:, None, None, None] == blocks[:, None]
    )
    pick = jnp.any(hits_t, axis=2).reshape(batches, row.shape[0], -1).astype(BF16)
    scales = jnp.moveaxis(route_weights[0], 2, 1).reshape(batches, tok * routes_each, 1)
    scales = jnp.broadcast_to(scales, scales.shape[:2] + (128,))

    group = 8 * PARTS * capacity
    at = jnp.arange(group, dtype=jnp.int32)
    wanted = (at % (8 * capacity)) // capacity * (PARTS * capacity) + at // (8 * capacity) * capacity + at % capacity
    perm = (wanted[:, None] == at[None, :]).astype(BF16)
    back = (at[:, None] == wanted[None, :]).astype(BF16)

    swap = [(i, i ^ 1) for i in range(devices)]
    place, pick, spread, scales, perm, back = lax.optimization_barrier((place, pick, spread, scales, perm, back))
    gate, up, down = stage([gate_weight, up_weight, down_weight])
    hidden = own
    finished = []
    for step in range(batches + sections - 1):
        if step > 0:
            begins = max(0, step - batches)
            pairs = [(i, i + 1) for i in range(begins, min(step, sections - 1))]
            if step < batches:
                pairs.append((step, 0))
            else:
                pairs.append((sections - 1, step - batches))
            hidden = lax.ppermute(current, "section", pairs)
            if step >= batches:
                finished.append(hidden)
        packed = front(place, hidden, norm_gain, pick, step, width=width)
        arrived = lax.all_to_all(packed, "expert", split_axis=0, concat_axis=0, tiled=True)
        others = lax.ppermute(arrived, "expert", swap)
        sum_gate, sum_up = first_half(place, arrived, perm, gate, up)
        leaving, inner = second_half(place, others, perm, back, gate, up, down, sum_gate, sum_up)
        received = lax.ppermute(leaving, "expert", swap)
        staying = own_down(place, inner, down, back)
        partial_value = (staying.astype(F32) + received.astype(F32)).astype(BF16)
        returned = lax.all_to_all(partial_value, "expert", split_axis=0, concat_axis=0, tiled=True)
        is_last = step == batches + sections - 2
        current = combine(
            place, returned, spread, scales, hidden, own, step, finished if is_last else ()
        )
    return current[None]


def solution(mesh):
    return jax.shard_map(
        per_device,
        mesh=mesh,
        in_specs=(
            P("section", "expert", None),
            P("section", None),
            P("section", None, "expert"),
            P("section", None, "expert"),
            P("section", "expert", None),
            P("section", None, "expert", None),
            P("section", None, "expert", None),
        ),
        out_specs=P("section", "expert", None),
        check_vma=False,
    )
```

time: 631 us -> 514 us (0.81)
  the two profiles are of different devices: /device:TPU:64 before, /device:TPU:97 now
where the time goes in v2:
time: 514 us; the launch traced here: 506 us
  blocking collectives  348 us (68%)
  Pallas kernels  84.3 us (16%)
  starting transfers between devices  34.5 us (7%)
  waiting for transfers between devices  29.4 us (6%)
  other arithmetic  5.56 us (1%)
    all_to_all x7, blocking collectives, per_device(): lax.all_to_all(packed, 'expert', split_axis=0, concat_axis=0, tiled=True)  178 us
    all_to_all x7, blocking collectives, per_device(): lax.all_to_all(partial_value, 'expert', split_axis=0, concat_axis=0, tile...  170 us
    ppermute x6, starting transfers between devices, per_device(): hidden = lax.ppermute(current, 'section', pairs)  28.8 us
    pallas_call x7, Pallas kernels, second_half(): pl.pallas_call(kernel, out_shape=[jax.ShapeDtypeStruct((all_rows, width),...  28 us
    ppermute x6, waiting for transfers between devices, per_device(): hidden = lax.ppermute(current, 'section', pairs)  21.7 us
    pallas_call x7, Pallas kernels, first_half(): pl.pallas_call(kernel, out_shape=[jax.ShapeDtypeStruct((rows, units), F32...  17.7 us
    pallas_call x7, Pallas kernels, own_down(): pl.pallas_call(kernel, out_shape=jax.ShapeDtypeStruct((rows * PARTS, widt...  14.2 us
  transfers between devices with their start and end apart: 20, of which 17 were waited for; matrix products, arithmetic and copies ran while one was open for 0% of the time, Pallas kernels for 8%

profile of v2, /device:TPU:97, one launch (start us, length us, event | category | flops | bytes accessed | tf_op | source)
XLA Modules:
  0.0 505.6 jit_solution(13919844176439141538)
XLA Ops:
  2.7 1.0 convert_element_type.108
  4.4 1.5 copy.43.p_ref
  6.0 1.2 shard_map.73
  7.2 28.4 %all_to_all.154 = bf16[32,24,896]{2,1,0:T(8,128)(2,1)S(1)} all-to-all(bf16[32,24,896]{2,1,0:T(8,128)(2,1)S(1)} %bitcast.62), channel_id=1, replica_groups=mesh['section'=4,'expert'=32] {'expert'}, dimensions={0} | all-to-all | bytes 2752512 | tf_op jit(solution)/shard_map/all_to_all | solution.py:285
  35.8 7.3 %shard_map.74 = (bf16[1,7168,512]{2,1,0:T(8,128)(2,1)S(1)}, bf16[1,7168,512]{2,1,0:T(8,128)(2,1)S(1)}, bf16[1,512,7168]{2,1,0:T(8,128)(2,1)S(1)}) custom-call(bf16[1,7168,512]{2,1,0:T(8,128)(2,1)} %refs_0_.1, bf16[1,7168,512]{2,1,0:T(8,128)(2,1)} %refs_1_.1, bf16[1,512,7168]{2,1,0:T(8,128)(2,1)} %refs_2_.1), custom_call_target="tpu_custom_call" | custom-call | bytes 44040192 | tf_op jit(solution)/shard_map/pallas_call | solution.py:73
  43.1 2.5 shard_map.75
  45.7 4.0 shard_map.76
  50.0 2.0 shard_map.77
  52.1 0.8 collective-permute-done.1
  53.3 24.4 %all_to_all.155 = bf16[32,24,896]{2,1,0:T(8,128)(2,1)S(1)} all-to-all(bf16[32,24,896]{2,1,0:T(8,128)(2,1)S(1)} %bitcast.88), channel_id=1, replica_groups=mesh['section'=4,'expert'=32] {'expert'}, dimensions={0} | all-to-all | bytes 2752512 | tf_op jit(solution)/shard_map/all_to_all | solution.py:292
  77.7 1.1 shard_map.78
  79.5 1.2 shard_map.79
  80.7 24.3 %all_to_all.156 = bf16[32,24,896]{2,1,0:T(8,128)(2,1)S(1)} all-to-all(bf16[32,24,896]{2,1,0:T(8,128)(2,1)S(1)} %bitcast.63), channel_id=1, replica_groups=mesh['section'=4,'expert'=32] {'expert'}, dimensions={0} | all-to-all | bytes 2752512 | tf_op jit(solution)/shard_map/all_to_all | solution.py:285
  105.5 2.5 shard_map.80
  108.3 4.0 shard_map.81
  112.7 2.0 shard_map.82
  114.7 0.8 collective-permute-done.4
  115.9 24.3 %all_to_all.157 = bf16[32,24,896]{2,1,0:T(8,128)(2,1)S(1)} all-to-all(bf16[32,24,896]{2,1,0:T(8,128)(2,1)S(1)} %bitcast.89), channel_id=1, replica_groups=mesh['section'=4,'expert'=32] {'expert'}, dimensions={0} | all-to-all | bytes 2752512 | tf_op jit(solution)/shard_map/all_to_all | solution.py:292
  140.2 1.1 shard_map.83
  142.0 1.2 shard_map.84
  143.3 24.3 %all_to_all.158 = bf16[32,24,896]{2,1,0:T(8,128)(2,1)S(1)} all-to-all(bf16[32,24,896]{2,1,0:T(8,128)(2,1)S(1)} %bitcast.64), channel_id=1, replica_groups=mesh['section'=4,'expert'=32] {'expert'}, dimensions={0} | all-to-all | bytes 2752512 | tf_op jit(solution)/shard_map/all_to_all | solution.py:285
  168.2 2.5 shard_map.85
  171.1 4.0 shard_map.86
  175.5 2.0 shard_map.87
  178.7 24.3 %all_to_all.159 = bf16[32,24,896]{2,1,0:T(8,128)(2,1)S(1)} all-to-all(bf16[32,24,896]{2,1,0:T(8,128)(2,1)S(1)} %bitcast.90), channel_id=1, replica_groups=mesh['section'=4,'expert'=32] {'expert'}, dimensions={0} | all-to-all | bytes 2752512 | tf_op jit(solution)/shard_map/all_to_all | solution.py:292
  203.0 1.1 shard_map.88
  204.1 18.5 %collective-permute-start.8 = (bf16[16,7168]{1,0:T(8,128)(2,1)S(1)}, bf16[16,7168]{1,0:T(8,128)(2,1)S(1)}, u32[]{:S(2)}, u32[]{:S(2)}) collective-permute-start(bf16[16,7168]{1,0:T(8,128)(2,1)S(1)} %shard_map.88), channel_id=1, source_target_pairs={{0,32},{32,64},{64,96},{96,0},{1,33},{33,65},{65,97},{97,1},{2,34}... | collective-permute-start | bytes 688136 | tf_op jit(solution)/shard_map/ppermute | solution.py:281
  222.7 4.7 collective-permute-done.8.h_ref
  227.4 1.2 shard_map.89
  228.6 25.2 %all_to_all.160 = bf16[32,24,896]{2,1,0:T(8,128)(2,1)S(1)} all-to-all(bf16[32,24,896]{2,1,0:T(8,128)(2,1)S(1)} %bitcast.65), channel_id=1, replica_groups=mesh['section'=4,'expert'=32] {'expert'}, dimensions={0} | all-to-all | bytes 2752512 | tf_op jit(solution)/shard_map/all_to_all | solution.py:285
  254.2 2.5 shard_map.90
  257.1 4.0 shard_map.91
  261.4 2.0 shard_map.92
  264.6 24.4 %all_to_all.161 = bf16[32,24,896]{2,1,0:T(8,128)(2,1)S(1)} all-to-all(bf16[32,24,896]{2,1,0:T(8,128)(2,1)S(1)} %bitcast.91), channel_id=1, replica_groups=mesh['section'=4,'expert'=32] {'expert'}, dimensions={0} | all-to-all | bytes 2752512 | tf_op jit(solution)/shard_map/all_to_all | solution.py:292
  289.0 1.1 shard_map.93
  290.1 3.5 collective-permute-start.11
  293.6 4.7 collective-permute-done.11.h_ref.rest_0_
  298.3 1.2 shard_map.94
  299.5 25.2 %all_to_all.162 = bf16[32,24,896]{2,1,0:T(8,128)(2,1)S(1)} all-to-all(bf16[32,24,896]{2,1,0:T(8,128)(2,1)S(1)} %bitcast.66), channel_id=1, replica_groups=mesh['section'=4,'expert'=32] {'expert'}, dimensions={0} | all-to-all | bytes 2752512 | tf_op jit(solution)/shard_map/all_to_all | solution.py:285
  325.2 2.5 shard_map.95
  328.0 4.0 shard_map.96
  332.4 2.0 shard_map.97
  334.4 0.8 collective-permute-done.13
  335.6 24.3 %all_to_all.163 = bf16[32,24,896]{2,1,0:T(8,128)(2,1)S(1)} all-to-all(bf16[32,24,896]{2,1,0:T(8,128)(2,1)S(1)} %bitcast.92), channel_id=1, replica_groups=mesh['section'=4,'expert'=32] {'expert'}, dimensions={0} | all-to-all | bytes 2752512 | tf_op jit(solution)/shard_map/all_to_all | solution.py:292
  359.9 1.1 shard_map.98
  361.1 3.5 collective-permute-start.14
  364.6 5.3 %collective-permute-done.14.h_ref.rest_1_ = bf16[16,7168]{1,0:T(8,128)(2,1)S(1)} collective-permute-done((bf16[16,7168]{1,0:T(8,128)(2,1)S(1)}, bf16[16,7168]{1,0:T(8,128)(2,1)S(1)}, u32[]{:S(2)}, u32[]{:S(2)}) %collective-permute-start.14) | collective-permute-done | bytes 229408 | tf_op jit(solution)/shard_map/ppermute | solution.py:281
  369.9 1.2 shard_map.99
  371.1 25.2 %all_to_all.164 = bf16[32,24,896]{2,1,0:T(8,128)(2,1)S(1)} all-to-all(bf16[32,24,896]{2,1,0:T(8,128)(2,1)S(1)} %bitcast.67), channel_id=1, replica_groups=mesh['section'=4,'expert'=32] {'expert'}, dimensions={0} | all-to-all | bytes 2752512 | tf_op jit(solution)/shard_map/all_to_all | solution.py:285
  396.8 2.5 shard_map.100
  399.6 4.0 shard_map.101
  404.0 2.0 shard_map.102
  407.2 24.3 %all_to_all.165 = bf16[32,24,896]{2,1,0:T(8,128)(2,1)S(1)} all-to-all(bf16[32,24,896]{2,1,0:T(8,128)(2,1)S(1)} %bitcast.93), channel_id=1, replica_groups=mesh['section'=4,'expert'=32] {'expert'}, dimensions={0} | all-to-all | bytes 2752512 | tf_op jit(solution)/shard_map/all_to_all | solution.py:292
  431.5 1.1 shard_map.103
  432.7 1.9 collective-permute-start.17
  434.6 6.9 %collective-permute-done.17.h_ref.rest_2_ = bf16[16,7168]{1,0:T(8,128)(2,1)S(1)} collective-permute-done((bf16[16,7168]{1,0:T(8,128)(2,1)S(1)}, bf16[16,7168]{1,0:T(8,128)(2,1)S(1)}, u32[]{:S(2)}, u32[]{:S(2)}) %collective-permute-start.17) | collective-permute-done | bytes 229408 | tf_op jit(solution)/shard_map/ppermute | solution.py:281
  441.5 1.2 shard_map.104
  442.7 25.2 %all_to_all.166 = bf16[32,24,896]{2,1,0:T(8,128)(2,1)S(1)} all-to-all(bf16[32,24,896]{2,1,0:T(8,128)(2,1)S(1)} %bitcast.61), channel_id=1, replica_groups=mesh['section'=4,'expert'=32] {'expert'}, dimensions={0} | all-to-all | bytes 2752512 | tf_op jit(solution)/shard_map/all_to_all | solution.py:285
  468.4 2.5 shard_map.105
  471.3 4.0 shard_map.106
  475.6 2.0 shard_map.107
  477.6 0.8 collective-permute-done.19
  478.9 24.3 %all_to_all.167 = bf16[32,24,896]{2,1,0:T(8,128)(2,1)S(1)} all-to-all(bf16[32,24,896]{2,1,0:T(8,128)(2,1)S(1)} %bitcast.94), channel_id=1, replica_groups=mesh['section'=4,'expert'=32] {'expert'}, dimensions={0} | all-to-all | bytes 2752512 | tf_op jit(solution)/shard_map/all_to_all | solution.py:292
  503.2 1.9 shard_map.108
  (66 shorter events, 17.3 us)
Async XLA Ops:
  0.0 3.7 copy-start.2
  4.0 1.9 copy-start
  4.0 1.9 copy-start.1
  35.6 10.1 %collective-permute-start = (bf16[768,896]{1,0:T(8,128)(2,1)S(1)}, bf16[768,896]{1,0:T(8,128)(2,1)S(1)}, u32[]{:S(2)}, u32[]{:S(2)}) collective-permute-start(bf16[768,896]{1,0:T(8,128)(2,1)S(1)} %bitcast.74), channel_id=1, source_target_pairs={{0,1},{1,0},{2,3},{3,2},{4,5},{5,4},{6,7},{7,6},{8,9},{9,8},{10,11... | collective-permute-start | bytes 4128776 | tf_op jit(solution)/shard_map/ppermute | solution.py:286
  49.7 3.2 collective-permute-start.1
  78.8 0.7 collective-permute-start.2
  105.0 3.3 collective-permute-start.3
  112.3 3.2 collective-permute-start.4
  141.4 0.7 collective-permute-start.5
  167.6 3.5 collective-permute-start.6
  175.1 3.2 collective-permute-start.7
  204.1 23.3 %collective-permute-start.8 = (bf16[16,7168]{1,0:T(8,128)(2,1)S(1)}, bf16[16,7168]{1,0:T(8,128)(2,1)S(1)}, u32[]{:S(2)}, u32[]{:S(2)}) collective-permute-start(bf16[16,7168]{1,0:T(8,128)(2,1)S(1)} %shard_map.88), channel_id=1, source_target_pairs={{0,32},{32,64},{64,96},{96,0},{1,33},{33,65},{65,97},{97,1},{2,34}... | collective-permute-start | bytes 688136 | tf_op jit(solution)/shard_map/ppermute | solution.py:281
  253.8 3.3 collective-permute-start.9
  261.1 3.2 collective-permute-start.10
  290.1 8.2 %collective-permute-start.11 = (bf16[16,7168]{1,0:T(8,128)(2,1)S(1)}, bf16[16,7168]{1,0:T(8,128)(2,1)S(1)}, u32[]{:S(2)}, u32[]{:S(2)}) collective-permute-start(bf16[16,7168]{1,0:T(8,128)(2,1)S(1)} %shard_map.93), channel_id=1, source_target_pairs={{0,32},{32,64},{64,96},{96,0},{1,33},{33,65},{65,97},{97,1},{2,34}... | collective-permute-start | bytes 688136 | tf_op jit(solution)/shard_map/ppermute | solution.py:281
  324.7 3.3 collective-permute-start.12
  332.0 3.2 collective-permute-start.13
  361.1 8.8 %collective-permute-start.14 = (bf16[16,7168]{1,0:T(8,128)(2,1)S(1)}, bf16[16,7168]{1,0:T(8,128)(2,1)S(1)}, u32[]{:S(2)}, u32[]{:S(2)}) collective-permute-start(bf16[16,7168]{1,0:T(8,128)(2,1)S(1)} %shard_map.98), channel_id=1, source_target_pairs={{32,64},{64,96},{96,32},{33,65},{65,97},{97,33},{34,66},{66,98},{9... | collective-permute-start | bytes 688136 | tf_op jit(solution)/shard_map/ppermute | solution.py:281
  396.3 3.4 collective-permute-start.15
  403.6 3.2 collective-permute-start.16
  432.7 8.8 %collective-permute-start.17 = (bf16[16,7168]{1,0:T(8,128)(2,1)S(1)}, bf16[16,7168]{1,0:T(8,128)(2,1)S(1)}, u32[]{:S(2)}, u32[]{:S(2)}) collective-permute-start(bf16[16,7168]{1,0:T(8,128)(2,1)S(1)} %shard_map.103), channel_id=1, source_target_pairs={{64,96},{96,64},{65,97},{97,65},{66,98},{98,66},{67,99},{99,67},{6... | collective-permute-start | bytes 688136 | tf_op jit(solution)/shard_map/ppermute | solution.py:281
  467.9 3.4 collective-permute-start.18
  475.3 3.2 collective-permute-start.19

commit v3 on v2

--- a/solution.py
+++ b/solution.py
@@ -1,5 +1,6 @@
 import jax
 import jax.numpy as jnp
+import numpy as np
 from jax import lax
 from jax.experimental import pallas as pl
 from jax.experimental.pallas import tpu as pltpu
@@ -28,58 +29,44 @@
     return jnp.clip(step - place[0], 0, batches - 1)
 
 
-def front(place, hidden, gain, pick, step, *, width):
+def front(place, hidden, gain, keys, row_keys, step, *, width, experts):
     tok, full = hidden.shape
-    batches, rows, depth = pick.shape
+    batches, routes_each, lanes = keys.shape
+    rows = row_keys.shape[0]
     blocks = full // width
-
-    def kernel(place_ref, h_ref, g_ref, p_ref, o_ref):
+    piece = rows // experts
+
+    def kernel(place_ref, h_ref, g_ref, k_ref, r_ref, o_ref):
         x = h_ref[...].astype(F32)
         scale = lax.rsqrt(jnp.mean(x * x, axis=-1, keepdims=True) + 1e-06)
         normed = (x * scale * g_ref[...]).astype(BF16)
         stack = jnp.concatenate([normed[:, b * width : (b + 1) * width] for b in range(blocks)], axis=0)
-        o_ref[...] = mm(p_ref[0], stack).astype(BF16)
-
-    return pl.pallas_call(
-        kernel,
-        out_shape=jax.ShapeDtypeStruct((rows, width), BF16),
+        hit = r_ref[...] == k_ref[0, :1, :]
+        for k in range(1, routes_each):
+            hit |= r_ref[...] == k_ref[0, k : k + 1, :]
+        out = mm(jnp.where(hit, 1.0, 0.0).astype(BF16), stack).astype(BF16)
+        for e in range(experts):
+            for chip in range(2):
+                at = (2 * e + chip) * piece
+                o_ref[at : at + piece, :] = out[e * piece : (e + 1) * piece]
+
+    return pl.pallas_call(
+        kernel,
+        out_shape=jax.ShapeDtypeStruct((2 * rows, width), BF16),
         grid_spec=pltpu.PrefetchScalarGridSpec(
             num_scalar_prefetch=1,
             grid=(1,),
             in_specs=[
                 pl.BlockSpec((tok, full), lambda i, s: (0, 0)),
                 pl.BlockSpec((1, full), lambda i, s: (0, 0)),
-                pl.BlockSpec((1, rows, depth), lambda i, s: (batch_at(step, s, batches), 0, 0)),
+                pl.BlockSpec((1, routes_each, lanes), lambda i, s: (batch_at(step, s, batches), 0, 0)),
+                pl.BlockSpec((rows, lanes), lambda i, s: (0, 0)),
             ],
-            out_specs=pl.BlockSpec((rows, width), lambda i, s: (0, 0)),
+            out_specs=pl.BlockSpec((2 * rows, width), lambda i, s: (0, 0)),
         ),
         compiler_params=params(),
-        cost_estimate=cost(2 * rows * depth * width, 2 * rows * width),
-    )(place, hidden, gain, pick)
-
-
-def stage(weights):
-    def kernel(*refs):
-        count = len(weights)
-        sems = refs[-1]
-        copies = [
-            pltpu.make_async_copy(refs[i], refs[count + i], sems.at[i]) for i in range(count)
-        ]
-        for copy in copies:
-            copy.start()
-        for copy in copies:
-            copy.wait()
-
-    staged = pl.pallas_call(
-        kernel,
-        out_shape=[pltpu.VMEM(w.shape, w.dtype) for w in weights],
-        in_specs=[pl.BlockSpec(memory_space=pltpu.HBM)] * len(weights),
-        out_specs=[pl.BlockSpec(memory_space=pltpu.VMEM)] * len(weights),
-        scratch_shapes=[pltpu.SemaphoreType.DMA((len(weights),))],
-        compiler_params=params(),
-        cost_estimate=cost(0, 2 * sum(w.size * 2 for w in weights)),
-    )(*[pltpu.with_memory_space_constraint(w, pltpu.HBM) for w in weights])
-    return staged
+        cost_estimate=cost(2 * rows * lanes * width, 4 * rows * width),
+    )(place, hidden, gain, keys, row_keys)
 
 
 def held(array):
@@ -110,59 +97,127 @@
 VMEM_IN = pl.BlockSpec(memory_space=pltpu.VMEM)
 
 
-def first_half(place, arrived, perm, gate, up):
+def halves(core, depth):
+    own = pl.ds(pl.multiple_of(core * depth, depth), depth)
+    other = pl.ds(pl.multiple_of((1 - core) * depth, depth), depth)
+    return own, other
+
+
+def in_hbm(array):
+    return pltpu.with_memory_space_constraint(array, pltpu.HBM)
+
+
+HBM_IN = pl.BlockSpec(memory_space=pltpu.HBM)
+
+
+def first_half(place, arrived, perm, gate, up, stage):
     all_rows, width = arrived.shape
     rows = all_rows // PARTS
     units = gate.shape[2]
+    depth = PARTS * width
+
+    def product(core, xs, g_ref, u_ref, og_ref, ou_ref):
+        own, _ = halves(core, depth)
+        og_ref[...] = mm(xs[...], g_ref[0, own, :])
+        ou_ref[...] = mm(xs[...], u_ref[0, own, :])
 
     def kernel(place_ref, a_ref, p_ref, g_ref, u_ref, og_ref, ou_ref, xs):
         unpack(a_ref, p_ref[...], xs, rows)
-        depth = PARTS * width
-        part = pl.ds(pl.multiple_of(place_ref[1] * depth, depth), depth)
-        og_ref[...] = mm(xs[...], g_ref[0, part, :])
-        ou_ref[...] = mm(xs[...], u_ref[0, part, :])
-
-    return pl.pallas_call(
-        kernel,
-        out_shape=[jax.ShapeDtypeStruct((rows, units), F32)] * 2,
+        product(place_ref[1], xs, g_ref, u_ref, og_ref, ou_ref)
+
+    def staging(place_ref, a_ref, p_ref, g_hbm, u_hbm, og_ref, ou_ref, g_ref, u_ref, xs, sems):
+        core = place_ref[1]
+        copies = []
+        for part in halves(core, depth):
+            for source, target in ((g_hbm, g_ref), (u_hbm, u_ref)):
+                copy = pltpu.make_async_copy(source.at[0, part, :], target.at[0, part, :], sems.at[len(copies)])
+                copy.start()
+                copies.append(copy)
+        unpack(a_ref, p_ref[...], xs, rows)
+        copies[0].wait()
+        copies[1].wait()
+        product(core, xs, g_ref, u_ref, og_ref, ou_ref)
+        copies[2].wait()
+        copies[3].wait()
+
+    sums = [jax.ShapeDtypeStruct((rows, units), F32)] * 2
+    scratch = [pltpu.VMEM((rows, depth), BF16)]
+    flops = 4 * all_rows * width * units
+    if stage:
+        return pl.pallas_call(
+            staging,
+            out_shape=sums + [pltpu.VMEM(gate.shape, BF16)] * 2,
+            in_specs=[SMEM_IN] + [VMEM_IN] * 2 + [HBM_IN] * 2,
+            out_specs=[VMEM_IN] * 4,
+            scratch_shapes=scratch + [pltpu.SemaphoreType.DMA((4,))],
+            compiler_params=params(),
+            cost_estimate=cost(flops, 8 * gate.size),
+        )(place, arrived, perm, in_hbm(gate), in_hbm(up))
+    return pl.pallas_call(
+        kernel,
+        out_shape=sums,
         in_specs=[SMEM_IN] + [VMEM_IN] * 4,
         out_specs=[VMEM_IN] * 2,
-        scratch_shapes=[pltpu.VMEM((rows, PARTS * width), BF16)],
-        compiler_params=params(),
-        cost_estimate=cost(4 * all_rows * width * units, 4 * PARTS * width * units),
-    )(place, arrived, perm, held(gate), held(up))
-
-
-def second_half(place, arrived, perm, back, gate, up, down, sum_gate, sum_up):
+        scratch_shapes=scratch,
+        compiler_params=params(),
+        cost_estimate=cost(flops, 2 * gate.size),
+    )(place, arrived, perm, held(gate), held(up)) + (gate, up)
+
+
+def second_half(place, arrived, perm, back, gate, up, down, sum_gate, sum_up, stage):
     all_rows, width = arrived.shape
     rows = all_rows // PARTS
     units = gate.shape[2]
-
-    def kernel(place_ref, a_ref, p_ref, q_ref, g_ref, u_ref, d_ref, sg_ref, su_ref, o_ref, i_ref, xs, ys):
+    depth = PARTS * width
+
+    def hidden_units(core, a_ref, p_ref, g_ref, u_ref, sg_ref, su_ref, i_ref, xs):
         unpack(a_ref, p_ref[...], xs, rows)
-        depth = PARTS * width
-        other = 1 - place_ref[1]
-        part = pl.ds(pl.multiple_of(other * depth, depth), depth)
-        pre = sg_ref[...] + mm(xs[...], g_ref[0, part, :])
-        upper = su_ref[...] + mm(xs[...], u_ref[0, part, :])
+        _, other = halves(core, depth)
+        pre = sg_ref[...] + mm(xs[...], g_ref[0, other, :])
+        upper = su_ref[...] + mm(xs[...], u_ref[0, other, :])
         i_ref[...] = (pre * lax.logistic(pre) * upper).astype(BF16)
-        down_packed(i_ref[...], d_ref, other, q_ref[...], ys, o_ref)
-
-    return pl.pallas_call(
-        kernel,
-        out_shape=[
-            jax.ShapeDtypeStruct((all_rows, width), BF16),
-            jax.ShapeDtypeStruct((rows, units), BF16),
-        ],
+
+    def kernel(place_ref, a_ref, p_ref, q_ref, g_ref, u_ref, sg_ref, su_ref, d_ref, o_ref, i_ref, xs, ys):
+        core = place_ref[1]
+        hidden_units(core, a_ref, p_ref, g_ref, u_ref, sg_ref, su_ref, i_ref, xs)
+        down_packed(i_ref[...], d_ref, 1 - core, q_ref[...], ys, o_ref)
+
+    def staging(
+        place_ref, a_ref, p_ref, q_ref, g_ref, u_ref, sg_ref, su_ref, d_hbm, o_ref, i_ref, d_ref, xs, ys, sem
+    ):
+        core = place_ref[1]
+        copy = pltpu.make_async_copy(d_hbm, d_ref, sem)
+        copy.start()
+        hidden_units(core, a_ref, p_ref, g_ref, u_ref, sg_ref, su_ref, i_ref, xs)
+        copy.wait()
+        down_packed(i_ref[...], d_ref, 1 - core, q_ref[...], ys, o_ref)
+
+    outs = [
+        jax.ShapeDtypeStruct((all_rows, width), BF16),
+        jax.ShapeDtypeStruct((rows, units), BF16),
+    ]
+    scratch = [pltpu.VMEM((rows, depth), BF16), pltpu.VMEM((PARTS, rows, width), BF16)]
+    estimate = cost(6 * all_rows * width * units, 3 * gate.size)
+    operands = (place, arrived, perm, back, held(gate), held(up), sum_gate, sum_up)
+    if stage:
+        return pl.pallas_call(
+            staging,
+            out_shape=outs + [pltpu.VMEM(down.shape, BF16)],
+            in_specs=[SMEM_IN] + [VMEM_IN] * 7 + [HBM_IN],
+            out_specs=[VMEM_IN] * 3,
+            scratch_shapes=scratch + [pltpu.SemaphoreType.DMA],
+            compiler_params=params(),
+            cost_estimate=estimate,
+        )(*operands, in_hbm(down))
+    return pl.pallas_call(
+        kernel,
+        out_shape=outs,
         in_specs=[SMEM_IN] + [VMEM_IN] * 8,
         out_specs=[VMEM_IN] * 2,
-        scratch_shapes=[
-            pltpu.VMEM((rows, PARTS * width), BF16),
-            pltpu.VMEM((PARTS, rows, width), BF16),
-        ],
-        compiler_params=params(),
-        cost_estimate=cost(6 * all_rows * width * units, 6 * PARTS * width * units),
-    )(place, arrived, perm, back, held(gate), held(up), held(down), sum_gate, sum_up)
+        scratch_shapes=scratch,
+        compiler_params=params(),
+        cost_estimate=estimate,
+    )(*operands, held(down)) + (down,)
 
 
 def own_down(place, inner, down, back):
@@ -240,22 +295,22 @@
     place = jnp.stack([section, core]).astype(jnp.int32)
     own = tokens[0]
 
-    ids = routes[0].reshape(batches, tok * routes_each)
-    order = jnp.arange(tok * routes_each)
+    slots = experts * capacity
+    ids = jnp.moveaxis(routes[0], 2, 1).reshape(batches, routes_each * tok)
+    order = jnp.arange(routes_each * tok)
     same = (ids[:, :, None] == ids[:, None, :]) & (order[None, :] < order[:, None])
-    code = (ids * capacity + jnp.sum(same.astype(jnp.int32), axis=2)).reshape(batches, tok, routes_each)
-    row = jnp.arange(devices * PARTS * capacity, dtype=jnp.int32)
-    device = row // (PARTS * capacity)
-    row_block = (device % 2) * PARTS + (row % (PARTS * capacity)) // capacity
-    row_slot = (device // SHARDS) * capacity + row % capacity
+    code = ids * capacity + jnp.sum(same.astype(jnp.int32), axis=2)
     blocks = jnp.arange(2 * PARTS, dtype=jnp.int32)
-    code = jnp.moveaxis(code, 2, 1)
-    hits = (code[:, None, :, :, None] == row_slot) & (blocks[:, None, None, None] == row_block)
-    spread = hits.reshape(batches, -1, row.shape[0]).astype(BF16)
-    hits_t = (row_slot[:, None, None, None] == code[:, None, :, None, :]) & (
-        row_block[:, None, None, None] == blocks[:, None]
-    )
-    pick = jnp.any(hits_t, axis=2).reshape(batches, row.shape[0], -1).astype(BF16)
+    keys = code.reshape(batches, routes_each, 1, tok) + (blocks * slots)[:, None]
+    keys = keys.reshape(batches, routes_each, -1)
+    unit = PARTS * capacity
+    row = np.arange(devices * unit // 2)
+    row_keys = (row // unit % 2 * PARTS + row % unit // capacity) * slots
+    row_keys = row_keys + row // (2 * unit) * capacity + row % capacity
+    sent = np.repeat(row_keys.reshape(experts, 1, 2 * unit), 2, axis=1).reshape(-1)
+    row_keys = jnp.asarray(np.repeat(row_keys[:, None], keys.shape[2], axis=1), jnp.int32)
+    wants = code[:, None, :] + (blocks * slots)[:, None]
+    spread = (wants[:, :, :, None] == jnp.asarray(sent, jnp.int32)).reshape(batches, -1, sent.size).astype(BF16)
     scales = jnp.moveaxis(route_weights[0], 2, 1).reshape(batches, tok * routes_each, 1)
     scales = jnp.broadcast_to(scales, scales.shape[:2] + (128,))
 
@@ -266,8 +321,10 @@
     back = (at[:, None] == wanted[None, :]).astype(BF16)
 
     swap = [(i, i ^ 1) for i in range(devices)]
-    place, pick, spread, scales, perm, back = lax.optimization_barrier((place, pick, spread, scales, perm, back))
-    gate, up, down = stage([gate_weight, up_weight, down_weight])
+    place, keys, row_keys, spread, scales, perm, back = lax.optimization_barrier(
+        (place, keys, row_keys, spread, scales, perm, back)
+    )
+    gate, up, down = gate_weight, up_weight, down_weight
     hidden = own
     finished = []
     for step in range(batches + sections - 1):
@@ -281,11 +338,14 @@
             hidden = lax.ppermute(current, "section", pairs)
             if step >= batches:
                 finished.append(hidden)
-        packed = front(place, hidden, norm_gain, pick, step, width=width)
+        packed = front(place, hidden, norm_gain, keys, row_keys, step, width=width, experts=experts)
         arrived = lax.all_to_all(packed, "expert", split_axis=0, concat_axis=0, tiled=True)
         others = lax.ppermute(arrived, "expert", swap)
-        sum_gate, sum_up = first_half(place, arrived, perm, gate, up)
-        leaving, inner = second_half(place, others, perm, back, gate, up, down, sum_gate, sum_up)
+        stage = step == 0
+        sum_gate, sum_up, gate, up = first_half(place, arrived, perm, gate, up, stage)
+        leaving, inner, down = second_half(
+            place, others, perm, back, gate, up, down, sum_gate, sum_up, stage
+        )
         received = lax.ppermute(leaving, "expert", swap)
         staying = own_down(place, inner, down, back)
         partial_value = (staying.astype(F32) + received.astype(F32)).astype(BF16)

time: 514 us -> 508 us (0.988)
    pallas_call x22 -> x21, Pallas kernels: 61.4 us -> 57.8 us  [the longest x6 24 us: second_half(): pl.pallas_call(kernel, out_shape=outs, in_specs=[SMEM_IN] + [VMEM_IN] * 8...]
  transfers between devices with their start and end apart: 20 -> 20, of which waited for: 17 -> 17; matrix products, arithmetic and copies ran while one was open for 0% -> 0% of each run, Pallas kernels for 8% -> 7%
where the time goes in v3:
time: 508 us; the launch traced here: 500 us
  blocking collectives  348 us (69%)
  Pallas kernels  80.6 us (16%)
  starting transfers between devices  34.8 us (7%)
  waiting for transfers between devices  29.4 us (6%)
    all_to_all x7, blocking collectives, per_device(): lax.all_to_all(packed, 'expert', split_axis=0, concat_axis=0, tiled=True)  178 us
    all_to_all x7, blocking collectives, per_device(): lax.all_to_all(partial_value, 'expert', split_axis=0, concat_axis=0, tile...  170 us
    ppermute x6, starting transfers between devices, per_device(): hidden = lax.ppermute(current, 'section', pairs)  28.8 us
    pallas_call x6, Pallas kernels, second_half(): pl.pallas_call(kernel, out_shape=outs, in_specs=[SMEM_IN] + [VMEM_IN] * 8...  24 us
    ppermute x6, waiting for transfers between devices, per_device(): hidden = lax.ppermute(current, 'section', pairs)  21.7 us
    pallas_call x6, Pallas kernels, first_half(): pl.pallas_call(kernel, out_shape=sums, in_specs=[SMEM_IN] + [VMEM_IN] * 4...  15.2 us
    pallas_call x7, Pallas kernels, own_down(): pl.pallas_call(kernel, out_shape=jax.ShapeDtypeStruct((rows * PARTS, widt...  14.2 us
  transfers between devices with their start and end apart: 20, of which 17 were waited for; matrix products, arithmetic and copies ran while one was open for 0% of the time, Pallas kernels for 7%

profile of v3, /device:TPU:97, one launch (start us, length us, event | category | flops | bytes accessed | tf_op | source)
XLA Modules:
  0.0 500.3 jit_solution(3085321228913336709)
XLA Ops:
  3.4 1.0 compare_convert_fusion.s_ref
  4.5 1.0 shard_map.91
  5.5 28.4 %all_to_all.154 = bf16[32,24,896]{2,1,0:T(8,128)(2,1)S(1)} all-to-all(bf16[32,24,896]{2,1,0:T(8,128)(2,1)S(1)} %bitcast.57), channel_id=1, replica_groups=mesh['section'=4,'expert'=32] {'expert'}, dimensions={0} | all-to-all | bytes 2752512 | tf_op jit(solution)/shard_map/all_to_all | solution.py:342
  34.2 6.2 %shard_map.92 = (f32[192,512]{1,0:T(8,128)S(1)}, f32[192,512]{1,0:T(8,128)S(1)}, bf16[1,7168,512]{2,1,0:T(8,128)(2,1)S(1)}, bf16[1,7168,512]{2,1,0:T(8,128)(2,1)S(1)}) custom-call(s32[2]{0:T(128)S(1)} %pad_add_fusion.place_ref, bf16[768,896]{1,0:T(8,128)(2,1)S(1)} %bitcast.70, bf16[192,192]{1,0:T(8,128)(2,1)S(1)} %get-tuple-element.46.p_ref, ...), custom_call_target="tpu_custom_call" | custom-call | flops 1409286144 | bytes 29360128 | tf_op jit(solution)/shard_map/pallas_call | solution.py:147
  40.4 5.1 %shard_map.93 = (bf16[768,896]{1,0:T(8,128)(2,1)S(1)}, bf16[192,512]{1,0:T(8,128)(2,1)S(1)}, bf16[1,512,7168]{2,1,0:T(8,128)(2,1)S(1)}) custom-call(s32[2]{0:T(128)S(1)} %pad_add_fusion.place_ref, bf16[768,896]{1,0:T(8,128)(2,1)S(1)} %collective-permute-done.a_ref, bf16[192,192]{1,0:T(8,128)(2,1)S(1)} %get-tuple-element.46.p_ref, ...), custom_call_target="tpu_custom_call" | custom-call | flops 2113929216 | bytes 11010048 | tf_op jit(solution)/shard_map/pallas_call | solution.py:203
  45.9 2.0 shard_map.94
  47.9 0.8 collective-permute-done.1
  49.1 24.4 %all_to_all.155 = bf16[32,24,896]{2,1,0:T(8,128)(2,1)S(1)} all-to-all(bf16[32,24,896]{2,1,0:T(8,128)(2,1)S(1)} %bitcast.83), channel_id=1, replica_groups=mesh['section'=4,'expert'=32] {'expert'}, dimensions={0} | all-to-all | bytes 2752512 | tf_op jit(solution)/shard_map/all_to_all | solution.py:352
  73.5 1.1 shard_map.95
  75.3 1.0 shard_map.96
  76.4 24.3 %all_to_all.156 = bf16[32,24,896]{2,1,0:T(8,128)(2,1)S(1)} all-to-all(bf16[32,24,896]{2,1,0:T(8,128)(2,1)S(1)} %bitcast.58), channel_id=1, replica_groups=mesh['section'=4,'expert'=32] {'expert'}, dimensions={0} | all-to-all | bytes 2752512 | tf_op jit(solution)/shard_map/all_to_all | solution.py:342
  101.4 2.5 shard_map.97
  104.3 4.0 shard_map.98
  108.7 2.0 shard_map.99
  110.7 0.8 collective-permute-done.4
  111.9 24.3 %all_to_all.157 = bf16[32,24,896]{2,1,0:T(8,128)(2,1)S(1)} all-to-all(bf16[32,24,896]{2,1,0:T(8,128)(2,1)S(1)} %bitcast.84), channel_id=1, replica_groups=mesh['section'=4,'expert'=32] {'expert'}, dimensions={0} | all-to-all | bytes 2752512 | tf_op jit(solution)/shard_map/all_to_all | solution.py:352
  136.2 1.1 shard_map.100
  138.0 1.0 shard_map.101
  139.1 24.3 %all_to_all.158 = bf16[32,24,896]{2,1,0:T(8,128)(2,1)S(1)} all-to-all(bf16[32,24,896]{2,1,0:T(8,128)(2,1)S(1)} %bitcast.59), channel_id=1, replica_groups=mesh['section'=4,'expert'=32] {'expert'}, dimensions={0} | all-to-all | bytes 2752512 | tf_op jit(solution)/shard_map/all_to_all | solution.py:342
  163.8 2.5 shard_map.102
  166.7 4.0 shard_map.103
  171.0 2.0 shard_map.104
  173.1 0.8 collective-permute-done.7
  174.2 24.3 %all_to_all.159 = bf16[32,24,896]{2,1,0:T(8,128)(2,1)S(1)} all-to-all(bf16[32,24,896]{2,1,0:T(8,128)(2,1)S(1)} %bitcast.85), channel_id=1, replica_groups=mesh['section'=4,'expert'=32] {'expert'}, dimensions={0} | all-to-all | bytes 2752512 | tf_op jit(solution)/shard_map/all_to_all | solution.py:352
  198.5 1.1 shard_map.105
  199.7 18.5 %collective-permute-start.8 = (bf16[16,7168]{1,0:T(8,128)(2,1)S(1)}, bf16[16,7168]{1,0:T(8,128)(2,1)S(1)}, u32[]{:S(2)}, u32[]{:S(2)}) collective-permute-start(bf16[16,7168]{1,0:T(8,128)(2,1)S(1)} %shard_map.105), channel_id=1, source_target_pairs={{0,32},{32,64},{64,96},{96,0},{1,33},{33,65},{65,97},{97,1},{2,34}... | collective-permute-start | bytes 688136 | tf_op jit(solution)/shard_map/ppermute | solution.py:338
  218.2 4.7 collective-permute-done.8.h_ref
  222.9 1.0 shard_map.106
  224.0 25.2 %all_to_all.160 = bf16[32,24,896]{2,1,0:T(8,128)(2,1)S(1)} all-to-all(bf16[32,24,896]{2,1,0:T(8,128)(2,1)S(1)} %bitcast.60), channel_id=1, replica_groups=mesh['section'=4,'expert'=32] {'expert'}, dimensions={0} | all-to-all | bytes 2752512 | tf_op jit(solution)/shard_map/all_to_all | solution.py:342
  249.6 2.5 shard_map.107
  252.5 4.0 shard_map.108
  256.8 2.0 shard_map.109
  258.9 0.8 collective-permute-done.10
  260.0 24.3 %all_to_all.161 = bf16[32,24,896]{2,1,0:T(8,128)(2,1)S(1)} all-to-all(bf16[32,24,896]{2,1,0:T(8,128)(2,1)S(1)} %bitcast.86), channel_id=1, replica_groups=mesh['section'=4,'expert'=32] {'expert'}, dimensions={0} | all-to-all | bytes 2752512 | tf_op jit(solution)/shard_map/all_to_all | solution.py:352
  284.4 1.1 shard_map.110
  285.5 3.5 collective-permute-start.11
  289.0 4.7 collective-permute-done.11.h_ref.rest_0_
  293.7 1.0 shard_map.111
  294.8 25.2 %all_to_all.162 = bf16[32,24,896]{2,1,0:T(8,128)(2,1)S(1)} all-to-all(bf16[32,24,896]{2,1,0:T(8,128)(2,1)S(1)} %bitcast.61), channel_id=1, replica_groups=mesh['section'=4,'expert'=32] {'expert'}, dimensions={0} | all-to-all | bytes 2752512 | tf_op jit(solution)/shard_map/all_to_all | solution.py:342
  320.4 2.5 shard_map.112
  323.3 4.0 shard_map.113
  327.7 2.0 shard_map.114
  330.8 24.4 %all_to_all.163 = bf16[32,24,896]{2,1,0:T(8,128)(2,1)S(1)} all-to-all(bf16[32,24,896]{2,1,0:T(8,128)(2,1)S(1)} %bitcast.87), channel_id=1, replica_groups=mesh['section'=4,'expert'=32] {'expert'}, dimensions={0} | all-to-all | bytes 2752512 | tf_op jit(solution)/shard_map/all_to_all | solution.py:352
  355.2 1.1 shard_map.115
  356.3 3.5 collective-permute-start.14
  359.8 5.3 %collective-permute-done.14.h_ref.rest_1_ = bf16[16,7168]{1,0:T(8,128)(2,1)S(1)} collective-permute-done((bf16[16,7168]{1,0:T(8,128)(2,1)S(1)}, bf16[16,7168]{1,0:T(8,128)(2,1)S(1)}, u32[]{:S(2)}, u32[]{:S(2)}) %collective-permute-start.14) | collective-permute-done | bytes 229408 | tf_op jit(solution)/shard_map/ppermute | solution.py:338
  365.2 1.0 shard_map.116
  366.2 25.2 %all_to_all.164 = bf16[32,24,896]{2,1,0:T(8,128)(2,1)S(1)} all-to-all(bf16[32,24,896]{2,1,0:T(8,128)(2,1)S(1)} %bitcast.62), channel_id=1, replica_groups=mesh['section'=4,'expert'=32] {'expert'}, dimensions={0} | all-to-all | bytes 2752512 | tf_op jit(solution)/shard_map/all_to_all | solution.py:342
  392.1 2.5 shard_map.117
  394.9 4.0 shard_map.118
  399.3 2.0 shard_map.119
  401.3 0.8 collective-permute-done.16
  402.5 24.4 %all_to_all.165 = bf16[32,24,896]{2,1,0:T(8,128)(2,1)S(1)} all-to-all(bf16[32,24,896]{2,1,0:T(8,128)(2,1)S(1)} %bitcast.88), channel_id=1, replica_groups=mesh['section'=4,'expert'=32] {'expert'}, dimensions={0} | all-to-all | bytes 2752512 | tf_op jit(solution)/shard_map/all_to_all | solution.py:352
  426.9 1.1 shard_map.120
  428.0 1.9 collective-permute-start.17
  429.9 6.9 %collective-permute-done.17.h_ref.rest_2_ = bf16[16,7168]{1,0:T(8,128)(2,1)S(1)} collective-permute-done((bf16[16,7168]{1,0:T(8,128)(2,1)S(1)}, bf16[16,7168]{1,0:T(8,128)(2,1)S(1)}, u32[]{:S(2)}, u32[]{:S(2)}) %collective-permute-start.17) | collective-permute-done | bytes 229408 | tf_op jit(solution)/shard_map/ppermute | solution.py:338
  436.8 1.0 shard_map.121
  437.9 25.2 %all_to_all.166 = bf16[32,24,896]{2,1,0:T(8,128)(2,1)S(1)} all-to-all(bf16[32,24,896]{2,1,0:T(8,128)(2,1)S(1)} %bitcast.56), channel_id=1, replica_groups=mesh['section'=4,'expert'=32] {'expert'}, dimensions={0} | all-to-all | bytes 2752512 | tf_op jit(solution)/shard_map/all_to_all | solution.py:342
  463.4 2.5 shard_map.122
  466.3 4.0 shard_map.123
  470.7 2.0 shard_map.124
  472.7 0.8 collective-permute-done.19
  473.9 24.3 %all_to_all.167 = bf16[32,24,896]{2,1,0:T(8,128)(2,1)S(1)} all-to-all(bf16[32,24,896]{2,1,0:T(8,128)(2,1)S(1)} %bitcast.89), channel_id=1, replica_groups=mesh['section'=4,'expert'=32] {'expert'}, dimensions={0} | all-to-all | bytes 2752512 | tf_op jit(solution)/shard_map/all_to_all | solution.py:352
  498.2 1.9 shard_map.125
  (66 shorter events, 16.0 us)
Async XLA Ops:
  0.0 4.5 copy-start.1
  0.0 4.5 copy-start
  0.0 4.5 copy-start.2
  33.9 6.5 %collective-permute-start = (bf16[768,896]{1,0:T(8,128)(2,1)S(1)}, bf16[768,896]{1,0:T(8,128)(2,1)S(1)}, u32[]{:S(2)}, u32[]{:S(2)}) collective-permute-start(bf16[768,896]{1,0:T(8,128)(2,1)S(1)} %bitcast.69), channel_id=1, source_target_pairs={{0,1},{1,0},{2,3},{3,2},{4,5},{5,4},{6,7},{7,6},{8,9},{9,8},{10,11... | collective-permute-start | bytes 4128776 | tf_op jit(solution)/shard_map/ppermute | solution.py:343
  45.6 3.2 collective-permute-start.1
  74.6 0.7 collective-permute-start.2
  100.7 3.6 collective-permute-start.3
  108.3 3.2 collective-permute-start.4
  137.3 0.7 collective-permute-start.5
  163.4 3.3 collective-permute-start.6
  170.7 3.2 collective-permute-start.7
  199.7 23.3 %collective-permute-start.8 = (bf16[16,7168]{1,0:T(8,128)(2,1)S(1)}, bf16[16,7168]{1,0:T(8,128)(2,1)S(1)}, u32[]{:S(2)}, u32[]{:S(2)}) collective-permute-start(bf16[16,7168]{1,0:T(8,128)(2,1)S(1)} %shard_map.105), channel_id=1, source_target_pairs={{0,32},{32,64},{64,96},{96,0},{1,33},{33,65},{65,97},{97,1},{2,34}... | collective-permute-start | bytes 688136 | tf_op jit(solution)/shard_map/ppermute | solution.py:338
  249.2 3.3 collective-permute-start.9
  256.5 3.2 collective-permute-start.10
  285.5 8.2 %collective-permute-start.11 = (bf16[16,7168]{1,0:T(8,128)(2,1)S(1)}, bf16[16,7168]{1,0:T(8,128)(2,1)S(1)}, u32[]{:S(2)}, u32[]{:S(2)}) collective-permute-start(bf16[16,7168]{1,0:T(8,128)(2,1)S(1)} %shard_map.110), channel_id=1, source_target_pairs={{0,32},{32,64},{64,96},{96,0},{1,33},{33,65},{65,97},{97,1},{2,34}... | collective-permute-start | bytes 688136 | tf_op jit(solution)/shard_map/ppermute | solution.py:338
  319.9 3.4 collective-permute-start.12
  327.3 3.2 collective-permute-start.13
  356.3 8.8 %collective-permute-start.14 = (bf16[16,7168]{1,0:T(8,128)(2,1)S(1)}, bf16[16,7168]{1,0:T(8,128)(2,1)S(1)}, u32[]{:S(2)}, u32[]{:S(2)}) collective-permute-start(bf16[16,7168]{1,0:T(8,128)(2,1)S(1)} %shard_map.115), channel_id=1, source_target_pairs={{32,64},{64,96},{96,32},{33,65},{65,97},{97,33},{34,66},{66,98},{9... | collective-permute-start | bytes 688136 | tf_op jit(solution)/shard_map/ppermute | solution.py:338
  391.4 3.6 collective-permute-start.15
  398.9 3.2 collective-permute-start.16
  428.0 8.8 %collective-permute-start.17 = (bf16[16,7168]{1,0:T(8,128)(2,1)S(1)}, bf16[16,7168]{1,0:T(8,128)(2,1)S(1)}, u32[]{:S(2)}, u32[]{:S(2)}) collective-permute-start(bf16[16,7168]{1,0:T(8,128)(2,1)S(1)} %shard_map.120), channel_id=1, source_target_pairs={{64,96},{96,64},{65,97},{97,65},{66,98},{98,66},{67,99},{99,67},{6... | collective-permute-start | bytes 688136 | tf_op jit(solution)/shard_map/ppermute | solution.py:338
  463.0 3.3 collective-permute-start.18
  470.3 3.2 collective-permute-start.19

commit v4 on v3

--- a/solution.py
+++ b/solution.py
@@ -13,6 +13,10 @@
 BF16 = jnp.bfloat16
 
 
+SMEM_IN = pl.BlockSpec(memory_space=pltpu.SMEM)
+VMEM_IN = pl.BlockSpec(memory_space=pltpu.VMEM)
+
+
 def params():
     return pltpu.CompilerParams(vmem_limit_bytes=12 * 1024 * 1024)
 
@@ -41,9 +45,10 @@
         scale = lax.rsqrt(jnp.mean(x * x, axis=-1, keepdims=True) + 1e-06)
         normed = (x * scale * g_ref[...]).astype(BF16)
         stack = jnp.concatenate([normed[:, b * width : (b + 1) * width] for b in range(blocks)], axis=0)
-        hit = r_ref[...] == k_ref[0, :1, :]
+        wanted = k_ref[batch_at(step, place_ref, batches)]
+        hit = r_ref[...] == wanted[:1]
         for k in range(1, routes_each):
-            hit |= r_ref[...] == k_ref[0, k : k + 1, :]
+            hit |= r_ref[...] == wanted[k : k + 1]
         out = mm(jnp.where(hit, 1.0, 0.0).astype(BF16), stack).astype(BF16)
         for e in range(experts):
             for chip in range(2):
@@ -53,17 +58,8 @@
     return pl.pallas_call(
         kernel,
         out_shape=jax.ShapeDtypeStruct((2 * rows, width), BF16),
-        grid_spec=pltpu.PrefetchScalarGridSpec(
-            num_scalar_prefetch=1,
-            grid=(1,),
-            in_specs=[
-                pl.BlockSpec((tok, full), lambda i, s: (0, 0)),
-                pl.BlockSpec((1, full), lambda i, s: (0, 0)),
-                pl.BlockSpec((1, routes_each, lanes), lambda i, s: (batch_at(step, s, batches), 0, 0)),
-                pl.BlockSpec((rows, lanes), lambda i, s: (0, 0)),
-            ],
-            out_specs=pl.BlockSpec((2 * rows, width), lambda i, s: (0, 0)),
-        ),
+        in_specs=[SMEM_IN] + [VMEM_IN] * 4,
+        out_specs=VMEM_IN,
         compiler_params=params(),
         cost_estimate=cost(2 * rows * lanes * width, 4 * rows * width),
     )(place, hidden, gain, keys, row_keys)
@@ -80,21 +76,6 @@
         moved = mm(perm, packed_ref[g * group : (g + 1) * group, :]).astype(BF16)
         for b in range(PARTS):
             xs[g * piece : (g + 1) * piece, b * width : (b + 1) * width] = moved[b * piece : (b + 1) * piece]
-
-
-def down_packed(inner, down_ref, half, perm, ys, out_ref):
-    group, width = perm.shape[0], out_ref.shape[1]
-    piece = group // PARTS
-    for b in range(PARTS):
-        cols = pl.ds(pl.multiple_of(half * (PARTS * width) + b * width, 128), width)
-        ys[b] = mm(inner, down_ref[0, :, cols]).astype(BF16)
-    for g in range(out_ref.shape[0] // group):
-        stack = jnp.concatenate([ys[b, g * piece : (g + 1) * piece, :] for b in range(PARTS)], axis=0)
-        out_ref[g * group : (g + 1) * group, :] = mm(perm, stack).astype(BF16)
-
-
-SMEM_IN = pl.BlockSpec(memory_space=pltpu.SMEM)
-VMEM_IN = pl.BlockSpec(memory_space=pltpu.VMEM)
 
 
 def halves(core, depth):
@@ -164,78 +145,102 @@
     )(place, arrived, perm, held(gate), held(up)) + (gate, up)
 
 
-def second_half(place, arrived, perm, back, gate, up, down, sum_gate, sum_up, stage):
+def second_half(place, arrived, perm, gate, up, sum_gate, sum_up, down, others_down, stage):
     all_rows, width = arrived.shape
     rows = all_rows // PARTS
     units = gate.shape[2]
     depth = PARTS * width
 
-    def hidden_units(core, a_ref, p_ref, g_ref, u_ref, sg_ref, su_ref, i_ref, xs):
+    def product(core, a_ref, p_ref, g_ref, u_ref, sg_ref, su_ref, i_ref, xs):
         unpack(a_ref, p_ref[...], xs, rows)
         _, other = halves(core, depth)
         pre = sg_ref[...] + mm(xs[...], g_ref[0, other, :])
         upper = su_ref[...] + mm(xs[...], u_ref[0, other, :])
         i_ref[...] = (pre * lax.logistic(pre) * upper).astype(BF16)
 
-    def kernel(place_ref, a_ref, p_ref, q_ref, g_ref, u_ref, sg_ref, su_ref, d_ref, o_ref, i_ref, xs, ys):
+    def kernel(place_ref, *refs):
+        product(place_ref[1], *refs)
+
+    def staging(place_ref, a_ref, p_ref, g_ref, u_ref, sg_ref, su_ref, own_hbm, other_hbm, i_ref, d_ref, xs, sems):
         core = place_ref[1]
-        hidden_units(core, a_ref, p_ref, g_ref, u_ref, sg_ref, su_ref, i_ref, xs)
-        down_packed(i_ref[...], d_ref, 1 - core, q_ref[...], ys, o_ref)
-
-    def staging(
-        place_ref, a_ref, p_ref, q_ref, g_ref, u_ref, sg_ref, su_ref, d_hbm, o_ref, i_ref, d_ref, xs, ys, sem
-    ):
-        core = place_ref[1]
-        copy = pltpu.make_async_copy(d_hbm, d_ref, sem)
-        copy.start()
-        hidden_units(core, a_ref, p_ref, g_ref, u_ref, sg_ref, su_ref, i_ref, xs)
-        copy.wait()
-        down_packed(i_ref[...], d_ref, 1 - core, q_ref[...], ys, o_ref)
-
-    outs = [
-        jax.ShapeDtypeStruct((all_rows, width), BF16),
-        jax.ShapeDtypeStruct((rows, units), BF16),
-    ]
-    scratch = [pltpu.VMEM((rows, depth), BF16), pltpu.VMEM((PARTS, rows, width), BF16)]
-    estimate = cost(6 * all_rows * width * units, 3 * gate.size)
-    operands = (place, arrived, perm, back, held(gate), held(up), sum_gate, sum_up)
+        own, _ = halves(core, depth)
+        copies = [
+            pltpu.make_async_copy(source.at[0, :, own], d_ref.at[n], sems.at[n])
+            for n, source in enumerate((own_hbm, other_hbm))
+        ]
+        for copy in copies:
+            copy.start()
+        product(core, a_ref, p_ref, g_ref, u_ref, sg_ref, su_ref, i_ref, xs)
+        for copy in copies:
+            copy.wait()
+
+    inner = jax.ShapeDtypeStruct((rows, units), BF16)
+    scratch = [pltpu.VMEM((rows, depth), BF16)]
+    estimate = cost(4 * all_rows * width * units, 2 * gate.size)
+    operands = (place, arrived, perm, held(gate), held(up), sum_gate, sum_up)
     if stage:
         return pl.pallas_call(
             staging,
-            out_shape=outs + [pltpu.VMEM(down.shape, BF16)],
-            in_specs=[SMEM_IN] + [VMEM_IN] * 7 + [HBM_IN],
-            out_specs=[VMEM_IN] * 3,
-            scratch_shapes=scratch + [pltpu.SemaphoreType.DMA],
+            out_shape=[inner, pltpu.VMEM((2, units, depth), BF16)],
+            in_specs=[SMEM_IN] + [VMEM_IN] * 6 + [HBM_IN] * 2,
+            out_specs=[VMEM_IN] * 2,
+            scratch_shapes=scratch + [pltpu.SemaphoreType.DMA((2,))],
             compiler_params=params(),
             cost_estimate=estimate,
-        )(*operands, in_hbm(down))
-    return pl.pallas_call(
-        kernel,
-        out_shape=outs,
-        in_specs=[SMEM_IN] + [VMEM_IN] * 8,
-        out_specs=[VMEM_IN] * 2,
+        )(*operands, in_hbm(down), in_hbm(others_down))
+    return pl.pallas_call(
+        kernel,
+        out_shape=inner,
+        in_specs=[SMEM_IN] + [VMEM_IN] * 6,
+        out_specs=VMEM_IN,
         scratch_shapes=scratch,
         compiler_params=params(),
         cost_estimate=estimate,
-    )(*operands, held(down)) + (down,)
-
-
-def own_down(place, inner, down, back):
+    )(*operands), down
+
+
+def own_units(inner, down):
     rows, units = inner.shape
-    width = down.shape[2] // (2 * PARTS)
-
-    def kernel(place_ref, i_ref, d_ref, q_ref, o_ref, ys):
-        down_packed(i_ref[...], d_ref, place_ref[1], q_ref[...], ys, o_ref)
+    depth = down.shape[2]
+    piece = depth // PARTS
+
+    def kernel(i_ref, d_ref, o_ref):
+        for b in range(PARTS):
+            cols = slice(b * piece, (b + 1) * piece)
+            o_ref[:, cols] = mm(i_ref[...], d_ref[0, :, cols])
+
+    return pl.pallas_call(
+        kernel,
+        out_shape=jax.ShapeDtypeStruct((rows, depth), F32),
+        in_specs=[VMEM_IN] * 2,
+        out_specs=VMEM_IN,
+        compiler_params=params(),
+        cost_estimate=cost(2 * rows * units * depth, 2 * units * depth),
+    )(inner, held(down))
+
+
+def other_units(inner, down, total, back, width):
+    rows = inner.shape[0]
+    group = back.shape[0]
+    piece = group // PARTS
+
+    def kernel(i_ref, d_ref, t_ref, q_ref, o_ref, ys):
+        for b in range(PARTS):
+            cols = slice(b * width, (b + 1) * width)
+            ys[b] = (t_ref[:, cols] + mm(i_ref[...], d_ref[1, :, cols])).astype(BF16)
+        for g in range(rows // piece):
+            stack = jnp.concatenate([ys[b, g * piece : (g + 1) * piece, :] for b in range(PARTS)], axis=0)
+            o_ref[g * group : (g + 1) * group, :] = mm(q_ref[...], stack).astype(BF16)
 
     return pl.pallas_call(
         kernel,
         out_shape=jax.ShapeDtypeStruct((rows * PARTS, width), BF16),
-        in_specs=[SMEM_IN] + [VMEM_IN] * 3,
+        in_specs=[VMEM_IN] * 4,
         out_specs=VMEM_IN,
         scratch_shapes=[pltpu.VMEM((PARTS, rows, width), BF16)],
         compiler_params=params(),
-        cost_estimate=cost(2 * rows * PARTS * width * units, 2 * PARTS * width * units),
-    )(place, inner, held(down), back)
+        cost_estimate=cost(2 * inner.size * PARTS * width, inner.size),
+    )(inner, held(down), total, back)
 
 
 def combine(place, returned, spread, scales, hidden, tokens, step, finished=()):
@@ -248,35 +253,26 @@
 
     def kernel(place_ref, r_ref, s_ref, w_ref, h_ref, t_ref, *rest):
         o_ref = rest[-1]
-        got = mm(s_ref[0], r_ref[...])
+        batch = batch_at(step, place_ref, batches)
+        got = mm(s_ref[batch], r_ref[...])
+        scale = w_ref[batch][:, :1]
         section = place_ref[0]
         for b in range(blocks):
             cols = slice(b * width, (b + 1) * width)
             total = h_ref[:, cols].astype(F32)
             for k in range(routes_each):
                 at = b * picks + k * tok
-                total += w_ref[0, k * tok : (k + 1) * tok, :1] * got[at : at + tok]
+                total += scale[k * tok : (k + 1) * tok] * got[at : at + tok]
             total = jnp.where(section <= step, total, t_ref[:, cols].astype(F32))
             for home, f_ref in enumerate(rest[:-1]):
                 total = jnp.where(section == home, f_ref[:, cols].astype(F32), total)
             o_ref[:, cols] = total.astype(BF16)
 
-    whole = lambda i, s: (0, 0)
-    chosen = lambda i, s: (batch_at(step, s, batches), 0, 0)
     return pl.pallas_call(
         kernel,
         out_shape=jax.ShapeDtypeStruct((tok, full), BF16),
-        grid_spec=pltpu.PrefetchScalarGridSpec(
-            num_scalar_prefetch=1,
-            grid=(1,),
-            in_specs=[
-                pl.BlockSpec((rows, width), whole),
-                pl.BlockSpec((1,) + spread.shape[1:], chosen),
-                pl.BlockSpec((1, picks, 128), chosen),
-            ]
-            + [pl.BlockSpec((tok, full), whole)] * (2 + len(finished)),
-            out_specs=pl.BlockSpec((tok, full), whole),
-        ),
+        in_specs=[SMEM_IN] + [VMEM_IN] * (5 + len(finished)),
+        out_specs=VMEM_IN,
         compiler_params=params(),
         cost_estimate=cost(2 * spread.shape[1] * rows * width, 2 * rows * width),
     )(place, returned, spread, scales, hidden, tokens, *finished)
@@ -325,6 +321,7 @@
         (place, keys, row_keys, spread, scales, perm, back)
     )
     gate, up, down = gate_weight, up_weight, down_weight
+    others_down = lax.ppermute(down_weight, "expert", swap)
     hidden = own
     finished = []
     for step in range(batches + sections - 1):
@@ -343,12 +340,12 @@
         others = lax.ppermute(arrived, "expert", swap)
         stage = step == 0
         sum_gate, sum_up, gate, up = first_half(place, arrived, perm, gate, up, stage)
-        leaving, inner, down = second_half(
-            place, others, perm, back, gate, up, down, sum_gate, sum_up, stage
+        inner, down = second_half(
+            place, others, perm, gate, up, sum_gate, sum_up, down, others_down, stage
         )
-        received = lax.ppermute(leaving, "expert", swap)
-        staying = own_down(place, inner, down, back)
-        partial_value = (staying.astype(F32) + received.astype(F32)).astype(BF16)
+        others_inner = lax.ppermute(inner, "expert", swap)
+        total = own_units(inner, down)
+        partial_value = other_units(others_inner, down, total, back, width)
         returned = lax.all_to_all(partial_value, "expert", split_axis=0, concat_axis=0, tiled=True)
         is_last = step == batches + sections - 2
         current = combine(

time: 508 us -> 495 us (0.974)
  Pallas kernels: 80.6 us -> 75.2 us
    pallas_call x14 -> x21, Pallas kernels: 43.3 us -> 37.9 us  [the longest x6 15.4 us: second_half(): pl.pallas_call(kernel, out_shape=inner, in_specs=[SMEM_IN] + [VMEM_IN] *...]
  transfers between devices with their start and end apart: 20 -> 21, of which waited for: 17 -> 17; matrix products, arithmetic and copies ran while one was open for 0% -> 1% of each run, Pallas kernels for 7% -> 6%
where the time goes in v4:
time: 495 us; the launch traced here: 488 us
  blocking collectives  347 us (70%)
  Pallas kernels  75.2 us (15%)
  starting transfers between devices  34.8 us (7%)
  waiting for transfers between devices  25.1 us (5%)
    all_to_all x7, blocking collectives, per_device(): lax.all_to_all(packed, 'expert', split_axis=0, concat_axis=0, tiled=True)  177 us
    all_to_all x7, blocking collectives, per_device(): lax.all_to_all(partial_value, 'expert', split_axis=0, concat_axis=0, tile...  170 us
    ppermute x6, starting transfers between devices, per_device(): hidden = lax.ppermute(current, 'section', pairs)  28.7 us
    ppermute x6, waiting for transfers between devices, per_device(): hidden = lax.ppermute(current, 'section', pairs)  21.8 us
    pallas_call x6, Pallas kernels, second_half(): pl.pallas_call(kernel, out_shape=inner, in_specs=[SMEM_IN] + [VMEM_IN] *...  15.4 us
    pallas_call x6, Pallas kernels, first_half(): pl.pallas_call(kernel, out_shape=sums, in_specs=[SMEM_IN] + [VMEM_IN] * 4...  15.2 us
    pallas_call x7, Pallas kernels, other_units(): pl.pallas_call(kernel, out_shape=jax.ShapeDtypeStruct((rows * PARTS, widt...  10.7 us
  transfers between devices with their start and end apart: 21, of which 17 were waited for; matrix products, arithmetic and copies ran while one was open for 1% of the time, Pallas kernels for 6%

profile of v4, /device:TPU:97, one launch (start us, length us, event | category | flops | bytes accessed | tf_op | source)
XLA Modules:
  0.0 487.7 jit_solution(7660491437912348335)
XLA Ops:
  4.1 1.0 compare_convert_fusion.s_ref
  5.2 1.0 shard_map.91
  6.2 27.8 %all_to_all.154 = bf16[32,24,896]{2,1,0:T(8,128)(2,1)S(1)} all-to-all(bf16[32,24,896]{2,1,0:T(8,128)(2,1)S(1)} %bitcast.57), channel_id=1, replica_groups=mesh['section'=4,'expert'=32] {'expert'}, dimensions={0} | all-to-all | bytes 2752512 | tf_op jit(solution)/shard_map/all_to_all | solution.py:339
  34.3 6.2 %shard_map.92 = (f32[192,512]{1,0:T(8,128)S(1)}, f32[192,512]{1,0:T(8,128)S(1)}, bf16[1,7168,512]{2,1,0:T(8,128)(2,1)S(1)}, bf16[1,7168,512]{2,1,0:T(8,128)(2,1)S(1)}) custom-call(s32[2]{0:T(128)S(1)} %pad_add_fusion.place_ref, bf16[768,896]{1,0:T(8,128)(2,1)S(1)} %bitcast.70, bf16[192,192]{1,0:T(8,128)(2,1)S(1)} %get-tuple-element.33.p_ref.refs_1_, ...), custom_call_target="tpu_custom_call" | custom-call | flops 1409286144 | bytes 29360128 | tf_op jit(solution)/shard_map/pallas_call | solution.py:128
  40.6 4.8 shard_map.93
  45.7 1.0 shard_map.94.t_ref
  46.9 1.5 shard_map.95
  48.4 24.3 %all_to_all.155 = bf16[32,24,896]{2,1,0:T(8,128)(2,1)S(1)} all-to-all(bf16[32,24,896]{2,1,0:T(8,128)(2,1)S(1)} %bitcast.84), channel_id=1, replica_groups=mesh['section'=4,'expert'=32] {'expert'}, dimensions={0} | all-to-all | bytes 2752512 | tf_op jit(solution)/shard_map/all_to_all | solution.py:349
  72.7 1.1 shard_map.96
  74.6 1.0 shard_map.97
  75.6 24.3 %all_to_all.156 = bf16[32,24,896]{2,1,0:T(8,128)(2,1)S(1)} all-to-all(bf16[32,24,896]{2,1,0:T(8,128)(2,1)S(1)} %bitcast.58), channel_id=1, replica_groups=mesh['section'=4,'expert'=32] {'expert'}, dimensions={0} | all-to-all | bytes 2752512 | tf_op jit(solution)/shard_map/all_to_all | solution.py:339
  100.6 2.5 shard_map.98
  103.5 2.6 shard_map.99.i_ref
  106.4 1.0 shard_map.100.t_ref
  107.6 1.5 shard_map.101
  109.2 24.3 %all_to_all.157 = bf16[32,24,896]{2,1,0:T(8,128)(2,1)S(1)} all-to-all(bf16[32,24,896]{2,1,0:T(8,128)(2,1)S(1)} %bitcast.85), channel_id=1, replica_groups=mesh['section'=4,'expert'=32] {'expert'}, dimensions={0} | all-to-all | bytes 2752512 | tf_op jit(solution)/shard_map/all_to_all | solution.py:349
  133.5 1.1 shard_map.102
  135.3 1.0 shard_map.103
  136.3 24.3 %all_to_all.158 = bf16[32,24,896]{2,1,0:T(8,128)(2,1)S(1)} all-to-all(bf16[32,24,896]{2,1,0:T(8,128)(2,1)S(1)} %bitcast.59), channel_id=1, replica_groups=mesh['section'=4,'expert'=32] {'expert'}, dimensions={0} | all-to-all | bytes 2752512 | tf_op jit(solution)/shard_map/all_to_all | solution.py:339
  160.9 2.5 shard_map.104
  163.8 2.6 shard_map.105.i_ref
  166.9 1.0 shard_map.106.t_ref
  168.1 1.5 shard_map.107
  169.6 24.3 %all_to_all.159 = bf16[32,24,896]{2,1,0:T(8,128)(2,1)S(1)} all-to-all(bf16[32,24,896]{2,1,0:T(8,128)(2,1)S(1)} %bitcast.86), channel_id=1, replica_groups=mesh['section'=4,'expert'=32] {'expert'}, dimensions={0} | all-to-all | bytes 2752512 | tf_op jit(solution)/shard_map/all_to_all | solution.py:349
  193.9 1.1 shard_map.108
  195.0 18.5 %collective-permute-start.9 = (bf16[16,7168]{1,0:T(8,128)(2,1)S(1)}, bf16[16,7168]{1,0:T(8,128)(2,1)S(1)}, u32[]{:S(2)}, u32[]{:S(2)}) collective-permute-start(bf16[16,7168]{1,0:T(8,128)(2,1)S(1)} %shard_map.108), channel_id=1, source_target_pairs={{0,32},{32,64},{64,96},{96,0},{1,33},{33,65},{65,97},{97,1},{2,34}... | collective-permute-start | bytes 688136 | tf_op jit(solution)/shard_map/ppermute | solution.py:335
  213.6 4.7 collective-permute-done.9.h_ref
  218.3 1.0 shard_map.109
  219.4 25.2 %all_to_all.160 = bf16[32,24,896]{2,1,0:T(8,128)(2,1)S(1)} all-to-all(bf16[32,24,896]{2,1,0:T(8,128)(2,1)S(1)} %bitcast.60), channel_id=1, replica_groups=mesh['section'=4,'expert'=32] {'expert'}, dimensions={0} | all-to-all | bytes 2752512 | tf_op jit(solution)/shard_map/all_to_all | solution.py:339
  244.8 2.5 shard_map.110
  247.7 2.6 shard_map.111.i_ref
  250.6 1.0 shard_map.112.t_ref
  251.8 1.5 shard_map.113
  253.3 24.3 %all_to_all.161 = bf16[32,24,896]{2,1,0:T(8,128)(2,1)S(1)} all-to-all(bf16[32,24,896]{2,1,0:T(8,128)(2,1)S(1)} %bitcast.87), channel_id=1, replica_groups=mesh['section'=4,'expert'=32] {'expert'}, dimensions={0} | all-to-all | bytes 2752512 | tf_op jit(solution)/shard_map/all_to_all | solution.py:349
  277.6 1.1 shard_map.114
  278.8 3.5 collective-permute-start.12
  282.3 4.7 collective-permute-done.12.h_ref.rest_0_
  287.0 1.0 shard_map.115
  288.0 25.2 %all_to_all.162 = bf16[32,24,896]{2,1,0:T(8,128)(2,1)S(1)} all-to-all(bf16[32,24,896]{2,1,0:T(8,128)(2,1)S(1)} %bitcast.61), channel_id=1, replica_groups=mesh['section'=4,'expert'=32] {'expert'}, dimensions={0} | all-to-all | bytes 2752512 | tf_op jit(solution)/shard_map/all_to_all | solution.py:339
  313.7 2.5 shard_map.116
  316.6 2.6 shard_map.117.i_ref
  320.7 1.5 shard_map.119
  322.3 24.3 %all_to_all.163 = bf16[32,24,896]{2,1,0:T(8,128)(2,1)S(1)} all-to-all(bf16[32,24,896]{2,1,0:T(8,128)(2,1)S(1)} %bitcast.88), channel_id=1, replica_groups=mesh['section'=4,'expert'=32] {'expert'}, dimensions={0} | all-to-all | bytes 2752512 | tf_op jit(solution)/shard_map/all_to_all | solution.py:349
  346.6 1.1 shard_map.120
  347.7 3.5 collective-permute-start.15
  351.2 5.4 %collective-permute-done.15.h_ref.rest_1_ = bf16[16,7168]{1,0:T(8,128)(2,1)S(1)} collective-permute-done((bf16[16,7168]{1,0:T(8,128)(2,1)S(1)}, bf16[16,7168]{1,0:T(8,128)(2,1)S(1)}, u32[]{:S(2)}, u32[]{:S(2)}) %collective-permute-start.15) | collective-permute-done | bytes 229408 | tf_op jit(solution)/shard_map/ppermute | solution.py:335
  356.5 1.0 shard_map.121
  357.6 25.2 %all_to_all.164 = bf16[32,24,896]{2,1,0:T(8,128)(2,1)S(1)} all-to-all(bf16[32,24,896]{2,1,0:T(8,128)(2,1)S(1)} %bitcast.62), channel_id=1, replica_groups=mesh['section'=4,'expert'=32] {'expert'}, dimensions={0} | all-to-all | bytes 2752512 | tf_op jit(solution)/shard_map/all_to_all | solution.py:339
  383.0 2.5 shard_map.122
  385.9 2.6 shard_map.123.i_ref
  389.0 1.0 shard_map.124.t_ref
  390.2 1.5 shard_map.125
  391.8 24.3 %all_to_all.165 = bf16[32,24,896]{2,1,0:T(8,128)(2,1)S(1)} all-to-all(bf16[32,24,896]{2,1,0:T(8,128)(2,1)S(1)} %bitcast.89), channel_id=1, replica_groups=mesh['section'=4,'expert'=32] {'expert'}, dimensions={0} | all-to-all | bytes 2752512 | tf_op jit(solution)/shard_map/all_to_all | solution.py:349
  416.1 1.1 shard_map.126
  417.2 1.9 collective-permute-start.18
  419.2 6.9 %collective-permute-done.18.h_ref.rest_2_ = bf16[16,7168]{1,0:T(8,128)(2,1)S(1)} collective-permute-done((bf16[16,7168]{1,0:T(8,128)(2,1)S(1)}, bf16[16,7168]{1,0:T(8,128)(2,1)S(1)}, u32[]{:S(2)}, u32[]{:S(2)}) %collective-permute-start.18) | collective-permute-done | bytes 229408 | tf_op jit(solution)/shard_map/ppermute | solution.py:335
  426.1 1.0 shard_map.127
  427.1 25.2 %all_to_all.166 = bf16[32,24,896]{2,1,0:T(8,128)(2,1)S(1)} all-to-all(bf16[32,24,896]{2,1,0:T(8,128)(2,1)S(1)} %bitcast.56), channel_id=1, replica_groups=mesh['section'=4,'expert'=32] {'expert'}, dimensions={0} | all-to-all | bytes 2752512 | tf_op jit(solution)/shard_map/all_to_all | solution.py:339
  452.5 2.5 shard_map.128
  455.4 2.6 shard_map.129.i_ref
  458.3 1.0 shard_map.130.t_ref
  459.5 1.5 shard_map.131
  461.1 24.3 %all_to_all.167 = bf16[32,24,896]{2,1,0:T(8,128)(2,1)S(1)} all-to-all(bf16[32,24,896]{2,1,0:T(8,128)(2,1)S(1)} %bitcast.83), channel_id=1, replica_groups=mesh['section'=4,'expert'=32] {'expert'}, dimensions={0} | all-to-all | bytes 2752512 | tf_op jit(solution)/shard_map/all_to_all | solution.py:349
  485.4 1.9 shard_map.132
  (68 shorter events, 15.1 us)
Async XLA Ops:
  0.0 5.2 %copy-start.1 = (s32[384,128]{1,0:T(8,128)S(1)}, s32[384,128]{1,0:T(8,128)}, u32[]{:S(2)}) copy-start(s32[384,128]{1,0:T(8,128)} %constant.62.clone.r_ref) | copy-start | bytes 589828
  0.0 5.2 %copy-start.2 = (f32[1,7168]{1,0:T(1,128)S(1)}, f32[1,7168]{1,0:T(1,128)}, u32[]{:S(2)}) copy-start(f32[1,7168]{1,0:T(1,128)} %g_ref.13) | copy-start | bytes 86020
  0.0 5.2 %copy-start = (bf16[1,16,7168]{2,1,0:T(8,128)(2,1)S(1)}, bf16[1,16,7168]{2,1,0:T(8,128)(2,1)}, u32[]{:S(2)}) copy-start(bf16[1,16,7168]{2,1,0:T(8,128)(2,1)} %param.9) | copy-start | bytes 688132
  0.0 40.5 %collective-permute-start.1 = (bf16[1,512,7168]{2,1,0:T(8,128)(2,1)}, bf16[1,512,7168]{2,1,0:T(8,128)(2,1)}, u32[]{:S(2)}, u32[]{:S(2)}) collective-permute-start(bf16[1,512,7168]{2,1,0:T(8,128)(2,1)} %own_hbm.1), channel_id=1, source_target_pairs={{0,1},{1,0},{2,3},{3,2},{4,5},{5,4},{6,7},{7,6},{8,9},{9,8},{10,11... | collective-permute-start | bytes 22020104 | tf_op jit(solution)/shard_map/ppermute | solution.py:324
  34.1 6.5 %collective-permute-start = (bf16[768,896]{1,0:T(8,128)(2,1)S(1)}, bf16[768,896]{1,0:T(8,128)(2,1)S(1)}, u32[]{:S(2)}, u32[]{:S(2)}) collective-permute-start(bf16[768,896]{1,0:T(8,128)(2,1)S(1)} %bitcast.69), channel_id=1, source_target_pairs={{0,1},{1,0},{2,3},{3,2},{4,5},{5,4},{6,7},{7,6},{8,9},{9,8},{10,11... | collective-permute-start | bytes 4128776 | tf_op jit(solution)/shard_map/ppermute | solution.py:340
  45.4 1.5 collective-permute-start.2
  73.9 0.7 collective-permute-start.3
  99.9 3.6 collective-permute-start.4
  106.1 1.5 collective-permute-start.5
  134.6 0.7 collective-permute-start.6
  160.6 3.1 collective-permute-start.7
  166.4 1.7 collective-permute-start.8
  195.0 23.3 %collective-permute-start.9 = (bf16[16,7168]{1,0:T(8,128)(2,1)S(1)}, bf16[16,7168]{1,0:T(8,128)(2,1)S(1)}, u32[]{:S(2)}, u32[]{:S(2)}) collective-permute-start(bf16[16,7168]{1,0:T(8,128)(2,1)S(1)} %shard_map.108), channel_id=1, source_target_pairs={{0,32},{32,64},{64,96},{96,0},{1,33},{33,65},{65,97},{97,1},{2,34}... | collective-permute-start | bytes 688136 | tf_op jit(solution)/shard_map/ppermute | solution.py:335
  244.5 3.1 collective-permute-start.10
  250.3 1.5 collective-permute-start.11
  278.8 8.2 %collective-permute-start.12 = (bf16[16,7168]{1,0:T(8,128)(2,1)S(1)}, bf16[16,7168]{1,0:T(8,128)(2,1)S(1)}, u32[]{:S(2)}, u32[]{:S(2)}) collective-permute-start(bf16[16,7168]{1,0:T(8,128)(2,1)S(1)} %shard_map.114), channel_id=1, source_target_pairs={{0,32},{32,64},{64,96},{96,0},{1,33},{33,65},{65,97},{97,1},{2,34}... | collective-permute-start | bytes 688136 | tf_op jit(solution)/shard_map/ppermute | solution.py:335
  313.2 3.4 collective-permute-start.13
  319.2 1.5 collective-permute-start.14
  347.7 8.8 %collective-permute-start.15 = (bf16[16,7168]{1,0:T(8,128)(2,1)S(1)}, bf16[16,7168]{1,0:T(8,128)(2,1)S(1)}, u32[]{:S(2)}, u32[]{:S(2)}) collective-permute-start(bf16[16,7168]{1,0:T(8,128)(2,1)S(1)} %shard_map.120), channel_id=1, source_target_pairs={{32,64},{64,96},{96,32},{33,65},{65,97},{97,33},{34,66},{66,98},{9... | collective-permute-start | bytes 688136 | tf_op jit(solution)/shard_map/ppermute | solution.py:335
  382.7 3.1 collective-permute-start.16
  388.5 1.8 collective-permute-start.17
  417.2 8.8 %collective-permute-start.18 = (bf16[16,7168]{1,0:T(8,128)(2,1)S(1)}, bf16[16,7168]{1,0:T(8,128)(2,1)S(1)}, u32[]{:S(2)}, u32[]{:S(2)}) collective-permute-start(bf16[16,7168]{1,0:T(8,128)(2,1)S(1)} %shard_map.126), channel_id=1, source_target_pairs={{64,96},{96,64},{65,97},{97,65},{66,98},{98,66},{67,99},{99,67},{6... | collective-permute-start | bytes 688136 | tf_op jit(solution)/shard_map/ppermute | solution.py:335
  452.3 3.1 collective-permute-start.19
  458.0 1.5 collective-permute-start.20

commit v5 on v4

--- a/solution.py
+++ b/solution.py
@@ -7,6 +7,7 @@
 from jax.sharding import PartitionSpec as P
 
 SHARDS = 4
+SECTIONS = 4
 PARTS = 4
 
 F32 = jnp.float32
@@ -17,6 +18,13 @@
 VMEM_IN = pl.BlockSpec(memory_space=pltpu.VMEM)
 
 
+HBM_IN = pl.BlockSpec(memory_space=pltpu.HBM)
+
+
+def in_hbm(array):
+    return pltpu.with_memory_space_constraint(array, pltpu.HBM)
+
+
 def params():
     return pltpu.CompilerParams(vmem_limit_bytes=12 * 1024 * 1024)
 
@@ -33,27 +41,108 @@
     return jnp.clip(step - place[0], 0, batches - 1)
 
 
+def plan(ids_ref, w_ref, sent_ref, k_ref, s_ref, c_ref, slots, capacity):
+    batches, routes_each, tok = ids_ref.shape
+    lanes = k_ref.shape[2]
+    picks = routes_each * tok
+    sub = lax.broadcasted_iota(jnp.int32, (tok, tok), 0)
+    lane = lax.broadcasted_iota(jnp.int32, (tok, tok), 1)
+    wide_sub = lax.broadcasted_iota(jnp.int32, (tok, lanes), 0)
+    wide_lane = lax.broadcasted_iota(jnp.int32, (tok, lanes), 1)
+
+    def column(values):
+        values = jnp.broadcast_to(values, (tok, tok))
+        return jnp.sum(jnp.where(sub == lane, values, jnp.zeros_like(values)), axis=1, keepdims=True)
+
+    for m in range(batches):
+        rows = [ids_ref[m, k : k + 1, :] for k in range(routes_each)]
+        for k in range(routes_each):
+            own = column(rows[k])
+            code = own * capacity
+            for before in range(k + 1):
+                same = own == rows[before]
+                if before == k:
+                    same &= lane < sub
+                code += jnp.sum(jnp.where(same, 1, 0), axis=1, keepdims=True)
+            lane_code = jnp.sum(jnp.where(wide_sub == wide_lane % tok, code, 0), axis=0, keepdims=True)
+            k_ref[m, k : k + 1, :] = lane_code + wide_lane[:1] // tok * slots
+            for b in range(2 * PARTS):
+                at = b * picks + k * tok
+                hit = code + b * slots == sent_ref[...]
+                s_ref[m, at : at + tok, :] = jnp.where(hit, 1.0, 0.0).astype(BF16)
+            scale = column(w_ref[m, k : k + 1, :])
+            c_ref[m, k * tok : (k + 1) * tok, :] = jnp.broadcast_to(scale, (tok, 128))
+
+
+def pack(batch, h_ref, g_ref, k_ref, r_ref, o_ref, experts):
+    rows = r_ref.shape[0]
+    width = o_ref.shape[1]
+    piece = rows // experts
+    x = h_ref[...].astype(F32)
+    scale = lax.rsqrt(jnp.mean(x * x, axis=-1, keepdims=True) + 1e-06)
+    normed = (x * scale * g_ref[...]).astype(BF16)
+    stack = jnp.concatenate([normed[:, b * width : (b + 1) * width] for b in range(2 * PARTS)], axis=0)
+    wanted = k_ref[batch]
+    hit = r_ref[...] == wanted[:1]
+    for k in range(1, wanted.shape[0]):
+        hit |= r_ref[...] == wanted[k : k + 1]
+    out = mm(jnp.where(hit, 1.0, 0.0).astype(BF16), stack).astype(BF16)
+    for e in range(experts):
+        for chip in range(2):
+            at = (2 * e + chip) * piece
+            o_ref[at : at + piece, :] = out[e * piece : (e + 1) * piece]
+
+
+def begin(place, tokens, gain, row_keys, ids, weights, sent, slots, capacity, experts):
+    batches, routes_each, tok = ids.shape
+    rows, lanes = row_keys.shape
+    picks = routes_each * tok
+    full = tokens.shape[1]
+
+    def kernel(place_ref, *refs):
+        sources, rest = refs[:6], refs[6:]
+        h_ref, g_ref, r_ref, k_ref, s_ref, c_ref, o_ref, ids_ref, w_ref, sent_ref, sems = rest
+        targets = (h_ref, g_ref, r_ref, ids_ref, w_ref, sent_ref)
+        copies = [pltpu.make_async_copy(sources[i], targets[i], sems.at[i]) for i in range(6)]
+        for copy in copies:
+            copy.start()
+        for copy in copies[3:]:
+            copy.wait()
+        plan(ids_ref, w_ref, sent_ref, k_ref, s_ref, c_ref, slots, capacity)
+        for copy in copies[:3]:
+            copy.wait()
+        pack(batch_at(0, place_ref, batches), h_ref, g_ref, k_ref, r_ref, o_ref, experts)
+
+    sources = (tokens, gain, row_keys, ids, weights, sent)
+    return pl.pallas_call(
+        kernel,
+        out_shape=[
+            pltpu.VMEM(tokens.shape, BF16),
+            pltpu.VMEM(gain.shape, F32),
+            pltpu.VMEM(row_keys.shape, jnp.int32),
+            jax.ShapeDtypeStruct((batches, routes_each, lanes), jnp.int32),
+            jax.ShapeDtypeStruct((batches, 2 * PARTS * picks, sent.shape[1]), BF16),
+            jax.ShapeDtypeStruct((batches, picks, 128), F32),
+            jax.ShapeDtypeStruct((2 * rows, full // (2 * PARTS)), BF16),
+        ],
+        in_specs=[SMEM_IN] + [HBM_IN] * 6,
+        out_specs=[VMEM_IN] * 7,
+        scratch_shapes=[
+            pltpu.VMEM(ids.shape, jnp.int32),
+            pltpu.VMEM(weights.shape, F32),
+            pltpu.VMEM(sent.shape, jnp.int32),
+            pltpu.SemaphoreType.DMA((6,)),
+        ],
+        compiler_params=params(),
+    )(place, *[in_hbm(array) for array in sources])
+
+
 def front(place, hidden, gain, keys, row_keys, step, *, width, experts):
-    tok, full = hidden.shape
-    batches, routes_each, lanes = keys.shape
-    rows = row_keys.shape[0]
-    blocks = full // width
-    piece = rows // experts
-
-    def kernel(place_ref, h_ref, g_ref, k_ref, r_ref, o_ref):
-        x = h_ref[...].astype(F32)
-        scale = lax.rsqrt(jnp.mean(x * x, axis=-1, keepdims=True) + 1e-06)
-        normed = (x * scale * g_ref[...]).astype(BF16)
-        stack = jnp.concatenate([normed[:, b * width : (b + 1) * width] for b in range(blocks)], axis=0)
-        wanted = k_ref[batch_at(step, place_ref, batches)]
-        hit = r_ref[...] == wanted[:1]
-        for k in range(1, routes_each):
-            hit |= r_ref[...] == wanted[k : k + 1]
-        out = mm(jnp.where(hit, 1.0, 0.0).astype(BF16), stack).astype(BF16)
-        for e in range(experts):
-            for chip in range(2):
-                at = (2 * e + chip) * piece
-                o_ref[at : at + piece, :] = out[e * piece : (e + 1) * piece]
+    batches = keys.shape[0]
+    rows, lanes = row_keys.shape
+
+    def kernel(place_ref, *refs):
+        pack(batch_at(step, place_ref, batches), *refs, experts)
 
     return pl.pallas_call(
         kernel,
@@ -82,13 +171,6 @@
     own = pl.ds(pl.multiple_of(core * depth, depth), depth)
     other = pl.ds(pl.multiple_of((1 - core) * depth, depth), depth)
     return own, other
-
-
-def in_hbm(array):
-    return pltpu.with_memory_space_constraint(array, pltpu.HBM)
-
-
-HBM_IN = pl.BlockSpec(memory_space=pltpu.HBM)
 
 
 def first_half(place, arrived, perm, gate, up, stage):
@@ -263,9 +345,14 @@
             for k in range(routes_each):
                 at = b * picks + k * tok
                 total += scale[k * tok : (k + 1) * tok] * got[at : at + tok]
-            total = jnp.where(section <= step, total, t_ref[:, cols].astype(F32))
-            for home, f_ref in enumerate(rest[:-1]):
-                total = jnp.where(section == home, f_ref[:, cols].astype(F32), total)
+            if step < SECTIONS - 1:
+                waiting = h_ref if step == 1 else t_ref
+                total = jnp.where(section > step, waiting[:, cols].astype(F32), total)
+            if step >= batches:
+                total = jnp.where(section <= step - batches, h_ref[:, cols].astype(F32), total)
+            if finished:
+                total = jnp.where(section < SECTIONS - 1, rest[1][:, cols].astype(F32), total)
+                total = jnp.where(section == 0, rest[0][:, cols].astype(F32), total)
             o_ref[:, cols] = total.astype(BF16)
 
     return pl.pallas_call(
@@ -289,26 +376,19 @@
     section = lax.axis_index("section")
     core = lax.axis_index("expert") % 2
     place = jnp.stack([section, core]).astype(jnp.int32)
-    own = tokens[0]
 
     slots = experts * capacity
-    ids = jnp.moveaxis(routes[0], 2, 1).reshape(batches, routes_each * tok)
-    order = jnp.arange(routes_each * tok)
-    same = (ids[:, :, None] == ids[:, None, :]) & (order[None, :] < order[:, None])
-    code = ids * capacity + jnp.sum(same.astype(jnp.int32), axis=2)
-    blocks = jnp.arange(2 * PARTS, dtype=jnp.int32)
-    keys = code.reshape(batches, routes_each, 1, tok) + (blocks * slots)[:, None]
-    keys = keys.reshape(batches, routes_each, -1)
     unit = PARTS * capacity
     row = np.arange(devices * unit // 2)
     row_keys = (row // unit % 2 * PARTS + row % unit // capacity) * slots
     row_keys = row_keys + row // (2 * unit) * capacity + row % capacity
-    sent = np.repeat(row_keys.reshape(experts, 1, 2 * unit), 2, axis=1).reshape(-1)
-    row_keys = jnp.asarray(np.repeat(row_keys[:, None], keys.shape[2], axis=1), jnp.int32)
-    wants = code[:, None, :] + (blocks * slots)[:, None]
-    spread = (wants[:, :, :, None] == jnp.asarray(sent, jnp.int32)).reshape(batches, -1, sent.size).astype(BF16)
-    scales = jnp.moveaxis(route_weights[0], 2, 1).reshape(batches, tok * routes_each, 1)
-    scales = jnp.broadcast_to(scales, scales.shape[:2] + (128,))
+    sent = np.repeat(row_keys.reshape(experts, 1, 2 * unit), 2, axis=1).reshape(1, -1)
+    row_keys = np.repeat(row_keys[:, None], 2 * PARTS * tok, axis=1)
+    row_keys, sent = jnp.asarray(row_keys, jnp.int32), jnp.asarray(sent, jnp.int32)
+    by_route = lambda array: jnp.moveaxis(array[0], 2, 1)
+    own, gain, row_keys, keys, spread, scales, packed = begin(
+        place, tokens[0], norm_gain, row_keys, by_route(routes), by_route(route_weights), sent, slots, capacity, experts
+    )
 
     group = 8 * PARTS * capacity
     at = jnp.arange(group, dtype=jnp.int32)
@@ -317,25 +397,22 @@
     back = (at[:, None] == wanted[None, :]).astype(BF16)
 
     swap = [(i, i ^ 1) for i in range(devices)]
-    place, keys, row_keys, spread, scales, perm, back = lax.optimization_barrier(
-        (place, keys, row_keys, spread, scales, perm, back)
-    )
+    perm, back = lax.optimization_barrier((perm, back))
     gate, up, down = gate_weight, up_weight, down_weight
     others_down = lax.ppermute(down_weight, "expert", swap)
     hidden = own
     finished = []
-    for step in range(batches + sections - 1):
+    steps = batches + sections - 1
+    for step in range(steps):
         if step > 0:
-            begins = max(0, step - batches)
-            pairs = [(i, i + 1) for i in range(begins, min(step, sections - 1))]
-            if step < batches:
-                pairs.append((step, 0))
+            if step in (1, steps - 1):
+                pairs = [(i, i ^ 1) for i in range(sections)]
             else:
-                pairs.append((sections - 1, step - batches))
+                pairs = [(i, (i + 1) % sections) for i in range(sections)]
             hidden = lax.ppermute(current, "section", pairs)
-            if step >= batches:
+            if step in (batches, steps - 1):
                 finished.append(hidden)
-        packed = front(place, hidden, norm_gain, keys, row_keys, step, width=width, experts=experts)
+            packed = front(place, hidden, gain, keys, row_keys, step, width=width, experts=experts)
         arrived = lax.all_to_all(packed, "expert", split_axis=0, concat_axis=0, tiled=True)
         others = lax.ppermute(arrived, "expert", swap)
         stage = step == 0
@@ -347,7 +424,7 @@
         total = own_units(inner, down)
         partial_value = other_units(others_inner, down, total, back, width)
         returned = lax.all_to_all(partial_value, "expert", split_axis=0, concat_axis=0, tiled=True)
-        is_last = step == batches + sections - 2
+        is_last = step == steps - 1
         current = combine(
             place, returned, spread, scales, hidden, own, step, finished if is_last else ()
         )

time: 495 us -> 492 us (level)
  the two profiles are of different devices: /device:TPU:97 before, /device:TPU:1 now
where the time goes in v5:
time: 492 us; the launch traced here: 485 us
  blocking collectives  348 us (71%)
  Pallas kernels  76.9 us (16%)
  waiting for transfers between devices  48.2 us (10%)
  starting transfers between devices  10.3 us (2%)
    all_to_all x7, blocking collectives, per_device(): lax.all_to_all(packed, 'expert', split_axis=0, concat_axis=0, tiled=True)  178 us
    all_to_all x7, blocking collectives, per_device(): lax.all_to_all(partial_value, 'expert', split_axis=0, concat_axis=0, tile...  170 us
    ppermute x6, waiting for transfers between devices, per_device(): hidden = lax.ppermute(current, 'section', pairs)  45 us
    pallas_call x6, Pallas kernels, second_half(): pl.pallas_call(kernel, out_shape=inner, in_specs=[SMEM_IN] + [VMEM_IN] *...  15.5 us
    pallas_call x6, Pallas kernels, first_half(): pl.pallas_call(kernel, out_shape=sums, in_specs=[SMEM_IN] + [VMEM_IN] * 4...  15.1 us
    pallas_call x7, Pallas kernels, other_units(): pl.pallas_call(kernel, out_shape=jax.ShapeDtypeStruct((rows * PARTS, widt...  10.9 us
  transfers between devices with their start and end apart: 21, of which 19 were waited for; matrix products, arithmetic and copies ran while one was open for 0% of the time, Pallas kernels for 6%

profile of v5, /device:TPU:1, one launch (start us, length us, event | category | flops | bytes accessed | tf_op | source)
XLA Modules:
  0.0 484.5 jit_solution(10189527157167910225)
XLA Ops:
  0.0 1.4 collective-permute-start.1
  1.5 2.5 shard_map.91
  4.0 27.9 %all_to_all.154 = bf16[32,24,896]{2,1,0:T(8,128)(2,1)S(1)} all-to-all(bf16[32,24,896]{2,1,0:T(8,128)(2,1)S(1)} %bitcast.72), channel_id=1, replica_groups=mesh['section'=4,'expert'=32] {'expert'}, dimensions={0} | all-to-all | bytes 2752512 | tf_op jit(solution)/shard_map/all_to_all | solution.py:416
  32.3 6.2 %shard_map.92 = (f32[192,512]{1,0:T(8,128)S(1)}, f32[192,512]{1,0:T(8,128)S(1)}, bf16[1,7168,512]{2,1,0:T(8,128)(2,1)S(1)}, bf16[1,7168,512]{2,1,0:T(8,128)(2,1)S(1)}) custom-call(s32[2]{0:T(128)S(1)} %pad_add_fusion.place_ref, bf16[768,896]{1,0:T(8,128)(2,1)S(1)} %bitcast.52, bf16[192,192]{1,0:T(8,128)(2,1)S(1)} %get-tuple-element.33.p_ref.refs_1_, ...), custom_call_target="tpu_custom_call" | custom-call | flops 1409286144 | bytes 29360128 | tf_op jit(solution)/shard_map/pallas_call | solution.py:210
  38.5 4.8 shard_map.93
  43.7 1.0 shard_map.94.t_ref
  44.9 1.6 shard_map.95
  46.4 24.4 %all_to_all.155 = bf16[32,24,896]{2,1,0:T(8,128)(2,1)S(1)} all-to-all(bf16[32,24,896]{2,1,0:T(8,128)(2,1)S(1)} %bitcast.66), channel_id=1, replica_groups=mesh['section'=4,'expert'=32] {'expert'}, dimensions={0} | all-to-all | bytes 2752512 | tf_op jit(solution)/shard_map/all_to_all | solution.py:426
  70.8 1.1 shard_map.96
  71.9 1.7 collective-permute-start.3
  73.6 5.7 %collective-permute-done.3.refs_0_.h_ref = bf16[16,7168]{1,0:T(8,128)(2,1)S(1)} collective-permute-done((bf16[16,7168]{1,0:T(8,128)(2,1)S(1)}, bf16[16,7168]{1,0:T(8,128)(2,1)S(1)}, u32[]{:S(2)}, u32[]{:S(2)}) %collective-permute-start.3) | collective-permute-done | bytes 229408 | tf_op jit(solution)/shard_map/ppermute | solution.py:412
  79.3 1.0 shard_map.97
  80.4 24.9 %all_to_all.156 = bf16[32,24,896]{2,1,0:T(8,128)(2,1)S(1)} all-to-all(bf16[32,24,896]{2,1,0:T(8,128)(2,1)S(1)} %bitcast.40), channel_id=1, replica_groups=mesh['section'=4,'expert'=32] {'expert'}, dimensions={0} | all-to-all | bytes 2752512 | tf_op jit(solution)/shard_map/all_to_all | solution.py:416
  105.9 2.5 shard_map.98
  108.8 2.6 shard_map.99.i_ref
  111.7 1.0 shard_map.100.t_ref
  112.9 1.5 shard_map.101
  114.5 24.3 %all_to_all.157 = bf16[32,24,896]{2,1,0:T(8,128)(2,1)S(1)} all-to-all(bf16[32,24,896]{2,1,0:T(8,128)(2,1)S(1)} %bitcast.67), channel_id=1, replica_groups=mesh['section'=4,'expert'=32] {'expert'}, dimensions={0} | all-to-all | bytes 2752512 | tf_op jit(solution)/shard_map/all_to_all | solution.py:426
  138.8 1.1 shard_map.102
  139.9 1.6 collective-permute-start.6
  141.5 7.9 %collective-permute-done.6.refs_0_.h_ref = bf16[16,7168]{1,0:T(8,128)(2,1)S(1)} collective-permute-done((bf16[16,7168]{1,0:T(8,128)(2,1)S(1)}, bf16[16,7168]{1,0:T(8,128)(2,1)S(1)}, u32[]{:S(2)}, u32[]{:S(2)}) %collective-permute-start.6) | collective-permute-done | bytes 229408 | tf_op jit(solution)/shard_map/ppermute | solution.py:412
  149.5 1.0 shard_map.103
  150.5 24.5 %all_to_all.158 = bf16[32,24,896]{2,1,0:T(8,128)(2,1)S(1)} all-to-all(bf16[32,24,896]{2,1,0:T(8,128)(2,1)S(1)} %bitcast.41), channel_id=1, replica_groups=mesh['section'=4,'expert'=32] {'expert'}, dimensions={0} | all-to-all | bytes 2752512 | tf_op jit(solution)/shard_map/all_to_all | solution.py:416
  175.3 2.5 shard_map.104
  178.2 2.6 shard_map.105.i_ref
  182.5 1.6 shard_map.107
  184.0 24.3 %all_to_all.159 = bf16[32,24,896]{2,1,0:T(8,128)(2,1)S(1)} all-to-all(bf16[32,24,896]{2,1,0:T(8,128)(2,1)S(1)} %bitcast.68), channel_id=1, replica_groups=mesh['section'=4,'expert'=32] {'expert'}, dimensions={0} | all-to-all | bytes 2752512 | tf_op jit(solution)/shard_map/all_to_all | solution.py:426
  208.3 1.1 shard_map.108
  209.5 8.1 %collective-permute-done.9.refs_0_.h_ref = bf16[16,7168]{1,0:T(8,128)(2,1)S(1)} collective-permute-done((bf16[16,7168]{1,0:T(8,128)(2,1)S(1)}, bf16[16,7168]{1,0:T(8,128)(2,1)S(1)}, u32[]{:S(2)}, u32[]{:S(2)}) %collective-permute-start.9) | collective-permute-done | bytes 229408 | tf_op jit(solution)/shard_map/ppermute | solution.py:412
  217.7 1.0 shard_map.109
  218.7 25.2 %all_to_all.160 = bf16[32,24,896]{2,1,0:T(8,128)(2,1)S(1)} all-to-all(bf16[32,24,896]{2,1,0:T(8,128)(2,1)S(1)} %bitcast.42), channel_id=1, replica_groups=mesh['section'=4,'expert'=32] {'expert'}, dimensions={0} | all-to-all | bytes 2752512 | tf_op jit(solution)/shard_map/all_to_all | solution.py:416
  244.1 2.5 shard_map.110
  247.0 2.6 shard_map.111.i_ref
  249.9 1.0 shard_map.112.t_ref
  251.1 1.6 shard_map.113
  252.7 24.3 %all_to_all.161 = bf16[32,24,896]{2,1,0:T(8,128)(2,1)S(1)} all-to-all(bf16[32,24,896]{2,1,0:T(8,128)(2,1)S(1)} %bitcast.69), channel_id=1, replica_groups=mesh['section'=4,'expert'=32] {'expert'}, dimensions={0} | all-to-all | bytes 2752512 | tf_op jit(solution)/shard_map/all_to_all | solution.py:426
  277.0 1.1 shard_map.114
  278.2 8.1 %collective-permute-done.12.refs_0_.h_ref.rest_0_ = bf16[16,7168]{1,0:T(8,128)(2,1)S(1)} collective-permute-done((bf16[16,7168]{1,0:T(8,128)(2,1)S(1)}, bf16[16,7168]{1,0:T(8,128)(2,1)S(1)}, u32[]{:S(2)}, u32[]{:S(2)}) %collective-permute-start.12) | collective-permute-done | bytes 229408 | tf_op jit(solution)/shard_map/ppermute | solution.py:412
  286.3 1.0 shard_map.115
  287.4 25.2 %all_to_all.162 = bf16[32,24,896]{2,1,0:T(8,128)(2,1)S(1)} all-to-all(bf16[32,24,896]{2,1,0:T(8,128)(2,1)S(1)} %bitcast.43), channel_id=1, replica_groups=mesh['section'=4,'expert'=32] {'expert'}, dimensions={0} | all-to-all | bytes 2752512 | tf_op jit(solution)/shard_map/all_to_all | solution.py:416
  313.0 2.5 shard_map.116
  315.9 2.6 shard_map.117.i_ref
  318.8 1.0 shard_map.118.t_ref
  320.0 1.5 shard_map.119
  321.5 24.3 %all_to_all.163 = bf16[32,24,896]{2,1,0:T(8,128)(2,1)S(1)} all-to-all(bf16[32,24,896]{2,1,0:T(8,128)(2,1)S(1)} %bitcast.70), channel_id=1, replica_groups=mesh['section'=4,'expert'=32] {'expert'}, dimensions={0} | all-to-all | bytes 2752512 | tf_op jit(solution)/shard_map/all_to_all | solution.py:426
  345.8 1.1 shard_map.120
  347.0 8.1 %collective-permute-done.15.refs_0_.h_ref = bf16[16,7168]{1,0:T(8,128)(2,1)S(1)} collective-permute-done((bf16[16,7168]{1,0:T(8,128)(2,1)S(1)}, bf16[16,7168]{1,0:T(8,128)(2,1)S(1)}, u32[]{:S(2)}, u32[]{:S(2)}) %collective-permute-start.15) | collective-permute-done | bytes 229408 | tf_op jit(solution)/shard_map/ppermute | solution.py:412
  355.2 1.0 shard_map.121
  356.2 25.2 %all_to_all.164 = bf16[32,24,896]{2,1,0:T(8,128)(2,1)S(1)} all-to-all(bf16[32,24,896]{2,1,0:T(8,128)(2,1)S(1)} %bitcast.44), channel_id=1, replica_groups=mesh['section'=4,'expert'=32] {'expert'}, dimensions={0} | all-to-all | bytes 2752512 | tf_op jit(solution)/shard_map/all_to_all | solution.py:416
  381.7 2.5 shard_map.122
  384.5 2.6 shard_map.123.i_ref
  387.7 1.0 shard_map.124.t_ref
  388.9 1.5 shard_map.125
  390.4 24.3 %all_to_all.165 = bf16[32,24,896]{2,1,0:T(8,128)(2,1)S(1)} all-to-all(bf16[32,24,896]{2,1,0:T(8,128)(2,1)S(1)} %bitcast.71), channel_id=1, replica_groups=mesh['section'=4,'expert'=32] {'expert'}, dimensions={0} | all-to-all | bytes 2752512 | tf_op jit(solution)/shard_map/all_to_all | solution.py:426
  414.8 1.1 shard_map.126
  416.0 6.9 %collective-permute-done.18.refs_0_.h_ref.rest_1_ = bf16[16,7168]{1,0:T(8,128)(2,1)S(1)} collective-permute-done((bf16[16,7168]{1,0:T(8,128)(2,1)S(1)}, bf16[16,7168]{1,0:T(8,128)(2,1)S(1)}, u32[]{:S(2)}, u32[]{:S(2)}) %collective-permute-start.18) | collective-permute-done | bytes 229408 | tf_op jit(solution)/shard_map/ppermute | solution.py:412
  422.9 1.0 shard_map.127
  424.0 25.2 %all_to_all.166 = bf16[32,24,896]{2,1,0:T(8,128)(2,1)S(1)} all-to-all(bf16[32,24,896]{2,1,0:T(8,128)(2,1)S(1)} %bitcast.39), channel_id=1, replica_groups=mesh['section'=4,'expert'=32] {'expert'}, dimensions={0} | all-to-all | bytes 2752512 | tf_op jit(solution)/shard_map/all_to_all | solution.py:416
  449.4 2.5 shard_map.128
  452.3 2.6 shard_map.129.i_ref
  455.2 1.0 shard_map.130.t_ref
  456.4 1.6 shard_map.131
  457.9 24.3 %all_to_all.167 = bf16[32,24,896]{2,1,0:T(8,128)(2,1)S(1)} all-to-all(bf16[32,24,896]{2,1,0:T(8,128)(2,1)S(1)} %bitcast.65), channel_id=1, replica_groups=mesh['section'=4,'expert'=32] {'expert'}, dimensions={0} | all-to-all | bytes 2752512 | tf_op jit(solution)/shard_map/all_to_all | solution.py:426
  482.2 1.9 shard_map.132
  (37 shorter events, 10.0 us)
Async XLA Ops:
  0.0 38.5 %collective-permute-start.1 = (bf16[1,512,7168]{2,1,0:T(8,128)(2,1)}, bf16[1,512,7168]{2,1,0:T(8,128)(2,1)}, u32[]{:S(2)}, u32[]{:S(2)}) collective-permute-start(bf16[1,512,7168]{2,1,0:T(8,128)(2,1)} %own_hbm.1), channel_id=1, source_target_pairs={{0,1},{1,0},{2,3},{3,2},{4,5},{5,4},{6,7},{7,6},{8,9},{9,8},{10,11... | collective-permute-start | bytes 22020104 | tf_op jit(solution)/shard_map/ppermute | solution.py:402
  31.9 6.6 %collective-permute-start = (bf16[768,896]{1,0:T(8,128)(2,1)S(1)}, bf16[768,896]{1,0:T(8,128)(2,1)S(1)}, u32[]{:S(2)}, u32[]{:S(2)}) collective-permute-start(bf16[768,896]{1,0:T(8,128)(2,1)S(1)} %bitcast.51), channel_id=1, source_target_pairs={{0,1},{1,0},{2,3},{3,2},{4,5},{5,4},{6,7},{7,6},{8,9},{9,8},{10,11... | collective-permute-start | bytes 4128776 | tf_op jit(solution)/shard_map/ppermute | solution.py:417
  43.4 1.5 collective-permute-start.2
  71.9 7.4 %collective-permute-start.3 = (bf16[16,7168]{1,0:T(8,128)(2,1)S(1)}, bf16[16,7168]{1,0:T(8,128)(2,1)S(1)}, u32[]{:S(2)}, u32[]{:S(2)}) collective-permute-start(bf16[16,7168]{1,0:T(8,128)(2,1)S(1)} %shard_map.96), channel_id=1, source_target_pairs={{0,32},{32,0},{64,96},{96,64},{1,33},{33,1},{65,97},{97,65},{2,34}... | collective-permute-start | bytes 688136 | tf_op jit(solution)/shard_map/ppermute | solution.py:412
  105.2 3.6 collective-permute-start.4
  111.4 1.5 collective-permute-start.5
  139.9 9.6 %collective-permute-start.6 = (bf16[16,7168]{1,0:T(8,128)(2,1)S(1)}, bf16[16,7168]{1,0:T(8,128)(2,1)S(1)}, u32[]{:S(2)}, u32[]{:S(2)}) collective-permute-start(bf16[16,7168]{1,0:T(8,128)(2,1)S(1)} %shard_map.102), channel_id=1, source_target_pairs={{0,32},{32,64},{64,96},{96,0},{1,33},{33,65},{65,97},{97,1},{2,34}... | collective-permute-start | bytes 688136 | tf_op jit(solution)/shard_map/ppermute | solution.py:412
  175.0 3.1 collective-permute-start.7
  180.8 1.7 collective-permute-start.8
  209.4 8.2 %collective-permute-start.9 = (bf16[16,7168]{1,0:T(8,128)(2,1)S(1)}, bf16[16,7168]{1,0:T(8,128)(2,1)S(1)}, u32[]{:S(2)}, u32[]{:S(2)}) collective-permute-start(bf16[16,7168]{1,0:T(8,128)(2,1)S(1)} %shard_map.108), channel_id=1, source_target_pairs={{0,32},{32,64},{64,96},{96,0},{1,33},{33,65},{65,97},{97,1},{2,34}... | collective-permute-start | bytes 688136 | tf_op jit(solution)/shard_map/ppermute | solution.py:412
  243.9 3.1 collective-permute-start.10
  249.6 1.5 collective-permute-start.11
  278.1 8.2 %collective-permute-start.12 = (bf16[16,7168]{1,0:T(8,128)(2,1)S(1)}, bf16[16,7168]{1,0:T(8,128)(2,1)S(1)}, u32[]{:S(2)}, u32[]{:S(2)}) collective-permute-start(bf16[16,7168]{1,0:T(8,128)(2,1)S(1)} %shard_map.114), channel_id=1, source_target_pairs={{0,32},{32,64},{64,96},{96,0},{1,33},{33,65},{65,97},{97,1},{2,34}... | collective-permute-start | bytes 688136 | tf_op jit(solution)/shard_map/ppermute | solution.py:412
  312.5 3.3 collective-permute-start.13
  318.4 1.5 collective-permute-start.14
  347.0 8.2 %collective-permute-start.15 = (bf16[16,7168]{1,0:T(8,128)(2,1)S(1)}, bf16[16,7168]{1,0:T(8,128)(2,1)S(1)}, u32[]{:S(2)}, u32[]{:S(2)}) collective-permute-start(bf16[16,7168]{1,0:T(8,128)(2,1)S(1)} %shard_map.120), channel_id=1, source_target_pairs={{0,32},{32,64},{64,96},{96,0},{1,33},{33,65},{65,97},{97,1},{2,34}... | collective-permute-start | bytes 688136 | tf_op jit(solution)/shard_map/ppermute | solution.py:412
  381.4 3.1 collective-permute-start.16
  387.1 1.8 collective-permute-start.17
  415.9 7.0 %collective-permute-start.18 = (bf16[16,7168]{1,0:T(8,128)(2,1)S(1)}, bf16[16,7168]{1,0:T(8,128)(2,1)S(1)}, u32[]{:S(2)}, u32[]{:S(2)}) collective-permute-start(bf16[16,7168]{1,0:T(8,128)(2,1)S(1)} %shard_map.126), channel_id=1, source_target_pairs={{0,32},{32,0},{64,96},{96,64},{1,33},{33,1},{65,97},{97,65},{2,34}... | collective-permute-start | bytes 688136 | tf_op jit(solution)/shard_map/ppermute | solution.py:412
  449.1 3.1 collective-permute-start.19
  454.8 1.5 collective-permute-start.20

commit v6 on v5

v6 whole, which is shorter than its diff:
```python
import jax
import jax.numpy as jnp
import numpy as np
from jax import lax
from jax.experimental import pallas as pl
from jax.experimental.pallas import tpu as pltpu
from jax.sharding import PartitionSpec as P

SHARDS = 4
COMPUTED, TOKENS, SENT, FIRST, NEXT = range(5)
SECTIONS = 4
PARTS = 4

F32 = jnp.float32
BF16 = jnp.bfloat16


SMEM_IN = pl.BlockSpec(memory_space=pltpu.SMEM)
VMEM_IN = pl.BlockSpec(memory_space=pltpu.VMEM)


HBM_IN = pl.BlockSpec(memory_space=pltpu.HBM)


def in_hbm(array):
    return pltpu.with_memory_space_constraint(array, pltpu.HBM)


def params():
    return pltpu.CompilerParams(vmem_limit_bytes=12 * 1024 * 1024)


def cost(flops, bytes_accessed):
    return pl.CostEstimate(flops=int(flops), bytes_accessed=int(bytes_accessed), transcendentals=0)


def mm(a, b):
    return jnp.dot(a, b, preferred_element_type=F32)


def plan(section, steps, ids_ref, w_ref, sent_ref, k_ref, s_ref, c_ref, m_ref, slots, capacity):
    batches, routes_each, tok = ids_ref.shape
    lanes = k_ref.shape[2]
    picks = routes_each * tok
    sub = lax.broadcasted_iota(jnp.int32, (tok, tok), 0)
    lane = lax.broadcasted_iota(jnp.int32, (tok, tok), 1)
    wide_sub = lax.broadcasted_iota(jnp.int32, (tok, lanes), 0)
    wide_lane = lax.broadcasted_iota(jnp.int32, (tok, lanes), 1)

    def column(values):
        values = jnp.broadcast_to(values, (tok, tok))
        return jnp.sum(jnp.where(sub == lane, values, jnp.zeros_like(values)), axis=1, keepdims=True)

    for step in range(steps):
        m = jnp.clip(step - section, 0, batches - 1)
        ids, weights = ids_ref[m], w_ref[m]
        rows = [ids[k : k + 1] for k in range(routes_each)]
        for k in range(routes_each):
            own = column(rows[k])
            code = own * capacity
            for before in range(k + 1):
                same = own == rows[before]
                if before == k:
                    same &= lane < sub
                code += jnp.sum(jnp.where(same, 1, 0), axis=1, keepdims=True)
            lane_code = jnp.sum(jnp.where(wide_sub == wide_lane % tok, code, 0), axis=0, keepdims=True)
            k_ref[step, k : k + 1, :] = lane_code + wide_lane[:1] // tok * slots
            for b in range(2 * PARTS):
                at = b * picks + k * tok
                hit = code + b * slots == sent_ref[...]
                s_ref[step, at : at + tok, :] = jnp.where(hit, 1.0, 0.0).astype(BF16)
            scale = column(weights[k : k + 1])
            c_ref[step, k * tok : (k + 1) * tok, :] = jnp.broadcast_to(scale, (tok, 128))
        mode = jnp.where(section > step, SENT if step == 1 else TOKENS, COMPUTED)
        mode = jnp.where(section <= step - batches, SENT, mode)
        if step == steps - 1:
            mode = jnp.where(section < SECTIONS - 1, jnp.where(section == 0, FIRST, NEXT), COMPUTED)
        m_ref[step] = jnp.full(m_ref.shape[1:], mode, jnp.int32)


def pack(step, h_ref, g_ref, k_ref, r_ref, o_ref, experts):
    rows = r_ref.shape[0]
    width = o_ref.shape[1]
    piece = rows // experts
    x = h_ref[...].astype(F32)
    scale = lax.rsqrt(jnp.mean(x * x, axis=-1, keepdims=True) + 1e-06)
    normed = (x * scale * g_ref[...]).astype(BF16)
    stack = jnp.concatenate([normed[:, b * width : (b + 1) * width] for b in range(2 * PARTS)], axis=0)
    wanted = k_ref[step]
    hit = r_ref[...] == wanted[:1]
    for k in range(1, wanted.shape[0]):
        hit |= r_ref[...] == wanted[k : k + 1]
    out = mm(jnp.where(hit, 1.0, 0.0).astype(BF16), stack).astype(BF16)
    for e in range(experts):
        for chip in range(2):
            at = (2 * e + chip) * piece
            o_ref[at : at + piece, :] = out[e * piece : (e + 1) * piece]


def begin(place, tokens, gain, row_keys, ids, weights, sent, slots, capacity, experts, steps):
    batches, routes_each, tok = ids.shape
    rows, lanes = row_keys.shape
    picks = routes_each * tok
    full = tokens.shape[1]

    def kernel(place_ref, *refs):
        sources, rest = refs[:6], refs[6:]
        h_ref, g_ref, r_ref, k_ref, s_ref, c_ref, m_ref, o_ref, ids_ref, w_ref, sent_ref, sems = rest
        targets = (h_ref, g_ref, r_ref, ids_ref, w_ref, sent_ref)
        copies = [pltpu.make_async_copy(sources[i], targets[i], sems.at[i]) for i in range(6)]
        for copy in copies:
            copy.start()
        for copy in copies[3:]:
            copy.wait()
        plan(place_ref[0], steps, ids_ref, w_ref, sent_ref, k_ref, s_ref, c_ref, m_ref, slots, capacity)
        for copy in copies[:3]:
            copy.wait()
        pack(0, h_ref, g_ref, k_ref, r_ref, o_ref, experts)

    sources = (tokens, gain, row_keys, ids, weights, sent)
    return pl.pallas_call(
        kernel,
        out_shape=[
            pltpu.VMEM(tokens.shape, BF16),
            pltpu.VMEM(gain.shape, F32),
            pltpu.VMEM(row_keys.shape, jnp.int32),
            pltpu.VMEM((steps, routes_each, lanes), jnp.int32),
            pltpu.VMEM((steps, 2 * PARTS * picks, sent.shape[1]), BF16),
            pltpu.VMEM((steps, picks, 128), F32),
            pltpu.VMEM((steps, 8, 128), jnp.int32),
            jax.ShapeDtypeStruct((2 * rows, full // (2 * PARTS)), BF16),
        ],
        in_specs=[SMEM_IN] + [HBM_IN] * 6,
        out_specs=[VMEM_IN] * 8,
        scratch_shapes=[
            pltpu.VMEM(ids.shape, jnp.int32),
            pltpu.VMEM(weights.shape, F32),
            pltpu.VMEM(sent.shape, jnp.int32),
            pltpu.SemaphoreType.DMA((6,)),
        ],
        compiler_params=params(),
    )(place, *[in_hbm(array) for array in sources])


def front(hidden, gain, keys, row_keys, step, *, width, experts):
    rows, lanes = row_keys.shape

    def kernel(*refs):
        pack(step, *refs, experts)

    return pl.pallas_call(
        kernel,
        out_shape=jax.ShapeDtypeStruct((2 * rows, width), BF16),
        in_specs=[VMEM_IN] * 4,
        out_specs=VMEM_IN,
        compiler_params=params(),
        cost_estimate=cost(2 * rows * lanes * width, 4 * rows * width),
    )(hidden, held(gain), held(keys), held(row_keys))


def held(array):
    return pltpu.with_memory_space_constraint(array, pltpu.VMEM)


def unpack(packed_ref, perm, xs, rows):
    group, width = perm.shape[0], packed_ref.shape[1]
    piece = group // PARTS
    for g in range(rows // piece):
        moved = mm(perm, packed_ref[g * group : (g + 1) * group, :]).astype(BF16)
        for b in range(PARTS):
            xs[g * piece : (g + 1) * piece, b * width : (b + 1) * width] = moved[b * piece : (b + 1) * piece]


def halves(core, depth):
    own = pl.ds(pl.multiple_of(core * depth, depth), depth)
    other = pl.ds(pl.multiple_of((1 - core) * depth, depth), depth)
    return own, other


def times(xs, weight_ref):
    return mm(xs[...], weight_ref[...])


def first_half(place, arrived, perm, gate, up, stage):
    all_rows, width = arrived.shape
    rows = all_rows // PARTS
    depth = PARTS * width
    units = gate.shape[-1]

    def kernel(a_ref, p_ref, g_ref, u_ref, og_ref, ou_ref, xs):
        unpack(a_ref, p_ref[...], xs, rows)
        og_ref[...] = times(xs, g_ref)
        ou_ref[...] = times(xs, u_ref)

    def staging(place_ref, a_ref, p_ref, g_hbm, u_hbm, og_ref, ou_ref, g_ref, u_ref, g_other, u_other, xs, sems):
        copies = []
        for part, targets in zip(halves(place_ref[1], depth), ((g_ref, u_ref), (g_other, u_other))):
            for source, target in zip((g_hbm, u_hbm), targets):
                copy = pltpu.make_async_copy(source.at[0, part, :], target, sems.at[len(copies)])
                copy.start()
                copies.append(copy)
        unpack(a_ref, p_ref[...], xs, rows)
        copies[0].wait()
        og_ref[...] = times(xs, g_ref)
        copies[1].wait()
        ou_ref[...] = times(xs, u_ref)
        copies[2].wait()
        copies[3].wait()

    sums = [jax.ShapeDtypeStruct((rows, units), F32)] * 2
    scratch = [pltpu.VMEM((rows, depth), BF16)]
    estimate = cost(4 * all_rows * width * units, 4 * depth * units)
    if stage:
        return pl.pallas_call(
            staging,
            out_shape=sums + [pltpu.VMEM((depth, units), BF16)] * 4,
            in_specs=[SMEM_IN] + [VMEM_IN] * 2 + [HBM_IN] * 2,
            out_specs=[VMEM_IN] * 6,
            scratch_shapes=scratch + [pltpu.SemaphoreType.DMA((4,))],
            compiler_params=params(),
            cost_estimate=estimate,
        )(place, arrived, perm, in_hbm(gate), in_hbm(up))
    return pl.pallas_call(
        kernel,
        out_shape=sums,
        in_specs=[VMEM_IN] * 4,
        out_specs=[VMEM_IN] * 2,
        scratch_shapes=scratch,
        compiler_params=params(),
        cost_estimate=estimate,
    )(arrived, perm, held(gate), held(up))


def second_half(place, arrived, perm, gate, up, sum_gate, sum_up, down, others_down, stage):
    all_rows, width = arrived.shape
    rows = all_rows // PARTS
    depth, units = gate.shape

    def kernel(a_ref, p_ref, g_ref, u_ref, sg_ref, su_ref, i_ref, xs):
        unpack(a_ref, p_ref[...], xs, rows)
        pre = sg_ref[...] + times(xs, g_ref)
        upper = su_ref[...] + times(xs, u_ref)
        i_ref[...] = (pre * lax.logistic(pre) * upper).astype(BF16)

    def staging(place_ref, a_ref, p_ref, g_ref, u_ref, sg_ref, su_ref, own_hbm, other_hbm, i_ref, d_ref, xs, sems):
        own, _ = halves(place_ref[1], depth)
        copies = [
            pltpu.make_async_copy(source.at[0, :, own], d_ref.at[n], sems.at[n])
            for n, source in enumerate((own_hbm, other_hbm))
        ]
        for copy in copies:
            copy.start()
        kernel(a_ref, p_ref, g_ref, u_ref, sg_ref, su_ref, i_ref, xs)
        for copy in copies:
            copy.wait()

    inner = jax.ShapeDtypeStruct((rows, units), BF16)
    scratch = [pltpu.VMEM((rows, depth), BF16)]
    estimate = cost(4 * all_rows * width * units, 4 * depth * units)
    operands = (arrived, perm, held(gate), held(up), sum_gate, sum_up)
    if stage:
        return pl.pallas_call(
            staging,
            out_shape=[inner, pltpu.VMEM((2, units, depth), BF16)],
            in_specs=[SMEM_IN] + [VMEM_IN] * 6 + [HBM_IN] * 2,
            out_specs=[VMEM_IN] * 2,
            scratch_shapes=scratch + [pltpu.SemaphoreType.DMA((2,))],
            compiler_params=params(),
            cost_estimate=estimate,
        )(place, *operands, in_hbm(down), in_hbm(others_down))
    return pl.pallas_call(
        kernel,
        out_shape=inner,
        in_specs=[VMEM_IN] * 6,
        out_specs=VMEM_IN,
        scratch_shapes=scratch,
        compiler_params=params(),
        cost_estimate=estimate,
    )(*operands), down


def own_units(inner, down):
    rows, units = inner.shape
    depth = down.shape[2]
    piece = depth // PARTS

    def kernel(i_ref, d_ref, o_ref):
        for b in range(PARTS):
            cols = slice(b * piece, (b + 1) * piece)
            o_ref[:, cols] = mm(i_ref[...], d_ref[0, :, cols])

    return pl.pallas_call(
        kernel,
        out_shape=jax.ShapeDtypeStruct((rows, depth), F32),
        in_specs=[VMEM_IN] * 2,
        out_specs=VMEM_IN,
        compiler_params=params(),
        cost_estimate=cost(2 * rows * units * depth, 2 * units * depth),
    )(inner, held(down))


def other_units(inner, down, total, back, width):
    rows = inner.shape[0]
    group = back.shape[0]
    piece = group // PARTS

    def kernel(i_ref, d_ref, t_ref, q_ref, o_ref, ys):
        for b in range(PARTS):
            cols = slice(b * width, (b + 1) * width)
            ys[b] = (t_ref[:, cols] + mm(i_ref[...], d_ref[1, :, cols])).astype(BF16)
        for g in range(rows // piece):
            stack = jnp.concatenate([ys[b, g * piece : (g + 1) * piece, :] for b in range(PARTS)], axis=0)
            o_ref[g * group : (g + 1) * group, :] = mm(q_ref[...], stack).astype(BF16)

    return pl.pallas_call(
        kernel,
        out_shape=jax.ShapeDtypeStruct((rows * PARTS, width), BF16),
        in_specs=[VMEM_IN] * 4,
        out_specs=VMEM_IN,
        scratch_shapes=[pltpu.VMEM((PARTS, rows, width), BF16)],
        compiler_params=params(),
        cost_estimate=cost(2 * inner.size * PARTS * width, inner.size),
    )(inner, held(down), total, back)


def combine(returned, spread, scales, modes, hidden, tokens, step, finished=()):
    rows, width = returned.shape
    tok, full = hidden.shape
    blocks = full // width
    picks = spread.shape[1] // blocks
    routes_each = picks // tok

    def kernel(r_ref, s_ref, w_ref, m_ref, h_ref, t_ref, *rest):
        o_ref = rest[-1]
        got = mm(s_ref[step], r_ref[...])
        scale = w_ref[step][:, :1]
        mode = jnp.broadcast_to(m_ref[step, :1, :1], (tok, 1))
        others = {TOKENS: t_ref, SENT: h_ref, **dict(zip((FIRST, NEXT), rest[:-1]))}
        for b in range(blocks):
            cols = slice(b * width, (b + 1) * width)
            total = h_ref[:, cols].astype(F32)
            for k in range(routes_each):
                at = b * picks + k * tok
                total += scale[k * tok : (k + 1) * tok] * got[at : at + tok]
            for kind, ref in others.items():
                total = jnp.where(mode == kind, ref[:, cols].astype(F32), total)
            o_ref[:, cols] = total.astype(BF16)

    return pl.pallas_call(
        kernel,
        out_shape=jax.ShapeDtypeStruct((tok, full), BF16),
        in_specs=[VMEM_IN] * (6 + len(finished)),
        out_specs=VMEM_IN,
        compiler_params=params(),
        cost_estimate=cost(2 * spread.shape[1] * rows * width, 2 * rows * width),
    )(returned, held(spread), held(scales), held(modes), hidden, held(tokens), *finished)


def per_device(tokens, norm_gain, gate_weight, up_weight, down_weight, routes, route_weights):
    sections = lax.axis_size("section")
    devices = lax.axis_size("expert")
    experts = devices // SHARDS
    _, batches, tok, routes_each = routes.shape
    full = tokens.shape[2]
    capacity = min(tok, tok * routes_each * 3 // (2 * experts))
    width = full // (2 * PARTS)
    section = lax.axis_index("section")
    core = lax.axis_index("expert") % 2
    place = jnp.stack([section, core]).astype(jnp.int32)

    slots = experts * capacity
    unit = PARTS * capacity
    row = np.arange(devices * unit // 2)
    row_keys = (row // unit % 2 * PARTS + row % unit // capacity) * slots
    row_keys = row_keys + row // (2 * unit) * capacity + row % capacity
    sent = np.repeat(row_keys.reshape(experts, 1, 2 * unit), 2, axis=1).reshape(1, -1)
    row_keys = np.repeat(row_keys[:, None], 2 * PARTS * tok, axis=1)
    row_keys, sent = jnp.asarray(row_keys, jnp.int32), jnp.asarray(sent, jnp.int32)
    by_route = lambda array: jnp.moveaxis(array[0], 2, 1)
    steps = batches + sections - 1
    own, gain, row_keys, keys, spread, scales, modes, packed = begin(
        place, tokens[0], norm_gain, row_keys, by_route(routes), by_route(route_weights), sent, slots, capacity, experts, steps
    )

    group = 8 * PARTS * capacity
    at = jnp.arange(group, dtype=jnp.int32)
    wanted = (at % (8 * capacity)) // capacity * (PARTS * capacity) + at // (8 * capacity) * capacity + at % capacity
    perm = (wanted[:, None] == at[None, :]).astype(BF16)
    back = (at[:, None] == wanted[None, :]).astype(BF16)

    swap = [(i, i ^ 1) for i in range(devices)]
    perm, back = lax.optimization_barrier((perm, back))
    gate, up, down = gate_weight, up_weight, down_weight
    others_down = lax.ppermute(down_weight, "expert", swap)
    hidden = own
    finished = []
    for step in range(steps):
        if step > 0:
            if step in (1, steps - 1):
                pairs = [(i, i ^ 1) for i in range(sections)]
            else:
                pairs = [(i, (i + 1) % sections) for i in range(sections)]
            hidden = lax.ppermute(current, "section", pairs)
            if step in (batches, steps - 1):
                finished.append(hidden)
            packed = front(hidden, gain, keys, row_keys, step, width=width, experts=experts)
        arrived = lax.all_to_all(packed, "expert", split_axis=0, concat_axis=0, tiled=True)
        others = lax.ppermute(arrived, "expert", swap)
        stage = step == 0
        sum_gate, sum_up, *staged = first_half(place, arrived, perm, gate, up, stage)
        if stage:
            gate, up, other_gate, other_up = staged
        inner, down = second_half(
            place, others, perm, other_gate, other_up, sum_gate, sum_up, down, others_down, stage
        )
        others_inner = lax.ppermute(inner, "expert", swap)
        total = own_units(inner, down)
        partial_value = other_units(others_inner, down, total, back, width)
        returned = lax.all_to_all(partial_value, "expert", split_axis=0, concat_axis=0, tiled=True)
        is_last = step == steps - 1
        current = combine(
            returned, spread, scales, modes, hidden, own, step, finished if is_last else ()
        )
    return current[None]


def solution(mesh):
    return jax.shard_map(
        per_device,
        mesh=mesh,
        in_specs=(
            P("section", "expert", None),
            P("section", None),
            P("section", None, "expert"),
            P("section", None, "expert"),
            P("section", "expert", None),
            P("section", None, "expert", None),
            P("section", None, "expert", None),
        ),
        out_specs=P("section", "expert", None),
        check_vma=False,
    )
```

time: 492 us -> 481 us (0.978)
  Pallas kernels: 76.9 us -> 62.6 us
    pallas_call x13, Pallas kernels: 36.8 us -> 30 us  [the longest x6 11.9 us: second_half(): pl.pallas_call(kernel, out_shape=inner, in_specs=[VMEM_IN] * 6, out_specs...]
where the time goes in v6:
time: 481 us; the launch traced here: 474 us
  blocking collectives  348 us (72%)
  Pallas kernels  62.6 us (13%)
  waiting for transfers between devices  51.5 us (11%)
  starting transfers between devices  10.4 us (2%)
    all_to_all x7, blocking collectives, per_device(): lax.all_to_all(packed, 'expert', split_axis=0, concat_axis=0, tiled=True)  178 us
    all_to_all x7, blocking collectives, per_device(): lax.all_to_all(partial_value, 'expert', split_axis=0, concat_axis=0, tile...  170 us
    ppermute x6, waiting for transfers between devices, per_device(): hidden = lax.ppermute(current, 'section', pairs)  45 us
    pallas_call x6, Pallas kernels, second_half(): pl.pallas_call(kernel, out_shape=inner, in_specs=[VMEM_IN] * 6, out_specs...  11.9 us
    pallas_call x6, Pallas kernels, first_half(): pl.pallas_call(kernel, out_shape=sums, in_specs=[VMEM_IN] * 4, out_specs=...  11.8 us
    pallas_call x7, Pallas kernels, other_units(): pl.pallas_call(kernel, out_shape=jax.ShapeDtypeStruct((rows * PARTS, widt...  10.8 us
  transfers between devices with their start and end apart: 21, of which 19 were waited for; matrix products, arithmetic and copies ran while one was open for 0% of the time, Pallas kernels for 6%

profile of v6, /device:TPU:1, one launch (start us, length us, event | category | flops | bytes accessed | tf_op | source)
XLA Modules:
  0.0 473.7 jit_solution(13171177053716850776)
XLA Ops:
  0.0 1.4 collective-permute-start.1
  1.5 2.8 shard_map.91
  4.3 27.9 %all_to_all.154 = bf16[32,24,896]{2,1,0:T(8,128)(2,1)S(1)} all-to-all(bf16[32,24,896]{2,1,0:T(8,128)(2,1)S(1)} %bitcast.72), channel_id=1, replica_groups=mesh['section'=4,'expert'=32] {'expert'}, dimensions={0} | all-to-all | bytes 2752512 | tf_op jit(solution)/shard_map/all_to_all | solution.py:407
  32.6 6.2 %shard_map.92 = (f32[192,512]{1,0:T(8,128)S(1)}, f32[192,512]{1,0:T(8,128)S(1)}, bf16[3584,512]{1,0:T(8,128)(2,1)S(1)}, bf16[3584,512]{1,0:T(8,128)(2,1)S(1)}, b...) custom-call(s32[2]{0:T(128)S(1)} %pad_add_fusion.place_ref, bf16[768,896]{1,0:T(8,128)(2,1)S(1)} %bitcast.52, ...), custom_call_target="tpu_custom_call" | custom-call | flops 1409286144 | bytes 7340032 | tf_op jit(solution)/shard_map/pallas_call | solution.py:214
  38.9 4.2 shard_map.93
  43.4 1.0 shard_map.94.t_ref
  44.5 1.5 shard_map.95
  46.1 24.3 %all_to_all.155 = bf16[32,24,896]{2,1,0:T(8,128)(2,1)S(1)} all-to-all(bf16[32,24,896]{2,1,0:T(8,128)(2,1)S(1)} %bitcast.66), channel_id=1, replica_groups=mesh['section'=4,'expert'=32] {'expert'}, dimensions={0} | all-to-all | bytes 2752512 | tf_op jit(solution)/shard_map/all_to_all | solution.py:419
  70.4 0.6 shard_map.96
  71.0 1.7 collective-permute-start.3
  72.8 5.7 %collective-permute-done.3.refs_0_.h_ref = bf16[16,7168]{1,0:T(8,128)(2,1)S(1)} collective-permute-done((bf16[16,7168]{1,0:T(8,128)(2,1)S(1)}, bf16[16,7168]{1,0:T(8,128)(2,1)S(1)}, u32[]{:S(2)}, u32[]{:S(2)}) %collective-permute-start.3) | collective-permute-done | bytes 229408 | tf_op jit(solution)/shard_map/ppermute | solution.py:403
  79.0 24.8 %all_to_all.156 = bf16[32,24,896]{2,1,0:T(8,128)(2,1)S(1)} all-to-all(bf16[32,24,896]{2,1,0:T(8,128)(2,1)S(1)} %bitcast.46), channel_id=1, replica_groups=mesh['section'=4,'expert'=32] {'expert'}, dimensions={0} | all-to-all | bytes 2752512 | tf_op jit(solution)/shard_map/all_to_all | solution.py:407
  103.8 0.7 collective-permute-start.4
  104.5 2.0 shard_map.98
  106.5 0.9 collective-permute-done.4.a_ref
  107.3 2.0 shard_map.99.i_ref
  109.7 1.0 shard_map.100.t_ref
  110.9 1.5 shard_map.101
  112.4 24.3 %all_to_all.157 = bf16[32,24,896]{2,1,0:T(8,128)(2,1)S(1)} all-to-all(bf16[32,24,896]{2,1,0:T(8,128)(2,1)S(1)} %bitcast.67), channel_id=1, replica_groups=mesh['section'=4,'expert'=32] {'expert'}, dimensions={0} | all-to-all | bytes 2752512 | tf_op jit(solution)/shard_map/all_to_all | solution.py:419
  136.7 0.6 shard_map.102
  137.3 1.7 collective-permute-start.6
  139.0 7.9 %collective-permute-done.6.refs_0_.h_ref = bf16[16,7168]{1,0:T(8,128)(2,1)S(1)} collective-permute-done((bf16[16,7168]{1,0:T(8,128)(2,1)S(1)}, bf16[16,7168]{1,0:T(8,128)(2,1)S(1)}, u32[]{:S(2)}, u32[]{:S(2)}) %collective-permute-start.6) | collective-permute-done | bytes 229408 | tf_op jit(solution)/shard_map/ppermute | solution.py:403
  147.4 24.5 %all_to_all.158 = bf16[32,24,896]{2,1,0:T(8,128)(2,1)S(1)} all-to-all(bf16[32,24,896]{2,1,0:T(8,128)(2,1)S(1)} %bitcast.47), channel_id=1, replica_groups=mesh['section'=4,'expert'=32] {'expert'}, dimensions={0} | all-to-all | bytes 2752512 | tf_op jit(solution)/shard_map/all_to_all | solution.py:407
  172.2 2.0 shard_map.104
  174.2 0.9 collective-permute-done.7.a_ref
  175.1 2.0 shard_map.105.i_ref
  177.6 1.0 shard_map.106.t_ref
  178.8 1.5 shard_map.107
  180.3 24.3 %all_to_all.159 = bf16[32,24,896]{2,1,0:T(8,128)(2,1)S(1)} all-to-all(bf16[32,24,896]{2,1,0:T(8,128)(2,1)S(1)} %bitcast.68), channel_id=1, replica_groups=mesh['section'=4,'expert'=32] {'expert'}, dimensions={0} | all-to-all | bytes 2752512 | tf_op jit(solution)/shard_map/all_to_all | solution.py:419
  204.6 0.6 shard_map.108
  205.3 8.1 %collective-permute-done.9.refs_0_.h_ref = bf16[16,7168]{1,0:T(8,128)(2,1)S(1)} collective-permute-done((bf16[16,7168]{1,0:T(8,128)(2,1)S(1)}, bf16[16,7168]{1,0:T(8,128)(2,1)S(1)}, u32[]{:S(2)}, u32[]{:S(2)}) %collective-permute-start.9) | collective-permute-done | bytes 229408 | tf_op jit(solution)/shard_map/ppermute | solution.py:403
  214.0 25.2 %all_to_all.160 = bf16[32,24,896]{2,1,0:T(8,128)(2,1)S(1)} all-to-all(bf16[32,24,896]{2,1,0:T(8,128)(2,1)S(1)} %bitcast.48), channel_id=1, replica_groups=mesh['section'=4,'expert'=32] {'expert'}, dimensions={0} | all-to-all | bytes 2752512 | tf_op jit(solution)/shard_map/all_to_all | solution.py:407
  239.4 2.0 shard_map.110
  241.4 0.9 collective-permute-done.10.a_ref
  242.3 2.0 shard_map.111.i_ref
  244.6 1.0 shard_map.112.t_ref
  245.8 1.5 shard_map.113
  247.3 24.3 %all_to_all.161 = bf16[32,24,896]{2,1,0:T(8,128)(2,1)S(1)} all-to-all(bf16[32,24,896]{2,1,0:T(8,128)(2,1)S(1)} %bitcast.69), channel_id=1, replica_groups=mesh['section'=4,'expert'=32] {'expert'}, dimensions={0} | all-to-all | bytes 2752512 | tf_op jit(solution)/shard_map/all_to_all | solution.py:419
  271.6 0.6 shard_map.114
  272.3 8.1 %collective-permute-done.12.refs_0_.h_ref.rest_0_ = bf16[16,7168]{1,0:T(8,128)(2,1)S(1)} collective-permute-done((bf16[16,7168]{1,0:T(8,128)(2,1)S(1)}, bf16[16,7168]{1,0:T(8,128)(2,1)S(1)}, u32[]{:S(2)}, u32[]{:S(2)}) %collective-permute-start.12) | collective-permute-done | bytes 229408 | tf_op jit(solution)/shard_map/ppermute | solution.py:403
  281.0 25.2 %all_to_all.162 = bf16[32,24,896]{2,1,0:T(8,128)(2,1)S(1)} all-to-all(bf16[32,24,896]{2,1,0:T(8,128)(2,1)S(1)} %bitcast.49), channel_id=1, replica_groups=mesh['section'=4,'expert'=32] {'expert'}, dimensions={0} | all-to-all | bytes 2752512 | tf_op jit(solution)/shard_map/all_to_all | solution.py:407
  306.6 2.0 shard_map.116
  308.6 0.9 collective-permute-done.13.a_ref
  309.4 2.0 shard_map.117.i_ref
  311.8 1.0 shard_map.118.t_ref
  313.0 1.5 shard_map.119
  314.5 24.3 %all_to_all.163 = bf16[32,24,896]{2,1,0:T(8,128)(2,1)S(1)} all-to-all(bf16[32,24,896]{2,1,0:T(8,128)(2,1)S(1)} %bitcast.70), channel_id=1, replica_groups=mesh['section'=4,'expert'=32] {'expert'}, dimensions={0} | all-to-all | bytes 2752512 | tf_op jit(solution)/shard_map/all_to_all | solution.py:419
  339.5 8.1 %collective-permute-done.15.refs_0_.h_ref = bf16[16,7168]{1,0:T(8,128)(2,1)S(1)} collective-permute-done((bf16[16,7168]{1,0:T(8,128)(2,1)S(1)}, bf16[16,7168]{1,0:T(8,128)(2,1)S(1)}, u32[]{:S(2)}, u32[]{:S(2)}) %collective-permute-start.15) | collective-permute-done | bytes 229408 | tf_op jit(solution)/shard_map/ppermute | solution.py:403
  348.2 25.2 %all_to_all.164 = bf16[32,24,896]{2,1,0:T(8,128)(2,1)S(1)} all-to-all(bf16[32,24,896]{2,1,0:T(8,128)(2,1)S(1)} %bitcast.50), channel_id=1, replica_groups=mesh['section'=4,'expert'=32] {'expert'}, dimensions={0} | all-to-all | bytes 2752512 | tf_op jit(solution)/shard_map/all_to_all | solution.py:407
  373.6 2.0 shard_map.122
  375.6 0.9 collective-permute-done.16.a_ref
  376.5 2.0 shard_map.123.i_ref
  379.0 1.0 shard_map.124.t_ref
  380.2 1.5 shard_map.125
  381.8 24.3 %all_to_all.165 = bf16[32,24,896]{2,1,0:T(8,128)(2,1)S(1)} all-to-all(bf16[32,24,896]{2,1,0:T(8,128)(2,1)S(1)} %bitcast.71), channel_id=1, replica_groups=mesh['section'=4,'expert'=32] {'expert'}, dimensions={0} | all-to-all | bytes 2752512 | tf_op jit(solution)/shard_map/all_to_all | solution.py:419
  406.8 6.9 %collective-permute-done.18.refs_0_.h_ref.rest_1_ = bf16[16,7168]{1,0:T(8,128)(2,1)S(1)} collective-permute-done((bf16[16,7168]{1,0:T(8,128)(2,1)S(1)}, bf16[16,7168]{1,0:T(8,128)(2,1)S(1)}, u32[]{:S(2)}, u32[]{:S(2)}) %collective-permute-start.18) | collective-permute-done | bytes 229408 | tf_op jit(solution)/shard_map/ppermute | solution.py:403
  414.2 25.2 %all_to_all.166 = bf16[32,24,896]{2,1,0:T(8,128)(2,1)S(1)} all-to-all(bf16[32,24,896]{2,1,0:T(8,128)(2,1)S(1)} %bitcast.39), channel_id=1, replica_groups=mesh['section'=4,'expert'=32] {'expert'}, dimensions={0} | all-to-all | bytes 2752512 | tf_op jit(solution)/shard_map/all_to_all | solution.py:407
  439.6 2.0 shard_map.128
  441.6 0.9 collective-permute-done.19.a_ref
  442.5 2.0 shard_map.129.i_ref
  444.8 1.0 shard_map.130.t_ref
  446.0 1.5 shard_map.131
  447.6 24.3 %all_to_all.167 = bf16[32,24,896]{2,1,0:T(8,128)(2,1)S(1)} all-to-all(bf16[32,24,896]{2,1,0:T(8,128)(2,1)S(1)} %bitcast.65), channel_id=1, replica_groups=mesh['section'=4,'expert'=32] {'expert'}, dimensions={0} | all-to-all | bytes 2752512 | tf_op jit(solution)/shard_map/all_to_all | solution.py:419
  471.9 1.4 shard_map.132
  (37 shorter events, 10.4 us)
Async XLA Ops:
  0.0 38.9 %collective-permute-start.1 = (bf16[1,512,7168]{2,1,0:T(8,128)(2,1)}, bf16[1,512,7168]{2,1,0:T(8,128)(2,1)}, u32[]{:S(2)}, u32[]{:S(2)}) collective-permute-start(bf16[1,512,7168]{2,1,0:T(8,128)(2,1)} %own_hbm.1), channel_id=1, source_target_pairs={{0,1},{1,0},{2,3},{3,2},{4,5},{5,4},{6,7},{7,6},{8,9},{9,8},{10,11... | collective-permute-start | bytes 22020104 | tf_op jit(solution)/shard_map/ppermute | solution.py:394
  32.2 6.6 %collective-permute-start = (bf16[768,896]{1,0:T(8,128)(2,1)S(1)}, bf16[768,896]{1,0:T(8,128)(2,1)S(1)}, u32[]{:S(2)}, u32[]{:S(2)}) collective-permute-start(bf16[768,896]{1,0:T(8,128)(2,1)S(1)} %bitcast.51), channel_id=1, source_target_pairs={{0,1},{1,0},{2,3},{3,2},{4,5},{5,4},{6,7},{7,6},{8,9},{9,8},{10,11... | collective-permute-start | bytes 4128776 | tf_op jit(solution)/shard_map/ppermute | solution.py:408
  43.0 1.5 collective-permute-start.2
  71.0 7.4 %collective-permute-start.3 = (bf16[16,7168]{1,0:T(8,128)(2,1)S(1)}, bf16[16,7168]{1,0:T(8,128)(2,1)S(1)}, u32[]{:S(2)}, u32[]{:S(2)}) collective-permute-start(bf16[16,7168]{1,0:T(8,128)(2,1)S(1)} %shard_map.96), channel_id=1, source_target_pairs={{0,32},{32,0},{64,96},{96,64},{1,33},{33,1},{65,97},{97,65},{2,34}... | collective-permute-start | bytes 688136 | tf_op jit(solution)/shard_map/ppermute | solution.py:403
  103.8 3.6 collective-permute-start.4
  109.3 1.5 collective-permute-start.5
  137.3 9.6 %collective-permute-start.6 = (bf16[16,7168]{1,0:T(8,128)(2,1)S(1)}, bf16[16,7168]{1,0:T(8,128)(2,1)S(1)}, u32[]{:S(2)}, u32[]{:S(2)}) collective-permute-start(bf16[16,7168]{1,0:T(8,128)(2,1)S(1)} %shard_map.102), channel_id=1, source_target_pairs={{0,32},{32,64},{64,96},{96,0},{1,33},{33,65},{65,97},{97,1},{2,34}... | collective-permute-start | bytes 688136 | tf_op jit(solution)/shard_map/ppermute | solution.py:403
  172.0 3.1 collective-permute-start.7
  177.1 1.7 collective-permute-start.8
  205.2 8.2 %collective-permute-start.9 = (bf16[16,7168]{1,0:T(8,128)(2,1)S(1)}, bf16[16,7168]{1,0:T(8,128)(2,1)S(1)}, u32[]{:S(2)}, u32[]{:S(2)}) collective-permute-start(bf16[16,7168]{1,0:T(8,128)(2,1)S(1)} %shard_map.108), channel_id=1, source_target_pairs={{0,32},{32,64},{64,96},{96,0},{1,33},{33,65},{65,97},{97,1},{2,34}... | collective-permute-start | bytes 688136 | tf_op jit(solution)/shard_map/ppermute | solution.py:403
  239.1 3.1 collective-permute-start.10
  244.2 1.5 collective-permute-start.11
  272.2 8.2 %collective-permute-start.12 = (bf16[16,7168]{1,0:T(8,128)(2,1)S(1)}, bf16[16,7168]{1,0:T(8,128)(2,1)S(1)}, u32[]{:S(2)}, u32[]{:S(2)}) collective-permute-start(bf16[16,7168]{1,0:T(8,128)(2,1)S(1)} %shard_map.114), channel_id=1, source_target_pairs={{0,32},{32,64},{64,96},{96,0},{1,33},{33,65},{65,97},{97,1},{2,34}... | collective-permute-start | bytes 688136 | tf_op jit(solution)/shard_map/ppermute | solution.py:403
  306.1 3.3 collective-permute-start.13
  311.4 1.5 collective-permute-start.14
  339.4 8.2 %collective-permute-start.15 = (bf16[16,7168]{1,0:T(8,128)(2,1)S(1)}, bf16[16,7168]{1,0:T(8,128)(2,1)S(1)}, u32[]{:S(2)}, u32[]{:S(2)}) collective-permute-start(bf16[16,7168]{1,0:T(8,128)(2,1)S(1)} %shard_map.120), channel_id=1, source_target_pairs={{0,32},{32,64},{64,96},{96,0},{1,33},{33,65},{65,97},{97,1},{2,34}... | collective-permute-start | bytes 688136 | tf_op jit(solution)/shard_map/ppermute | solution.py:403
  373.3 3.1 collective-permute-start.16
  378.5 1.8 collective-permute-start.17
  406.7 7.0 %collective-permute-start.18 = (bf16[16,7168]{1,0:T(8,128)(2,1)S(1)}, bf16[16,7168]{1,0:T(8,128)(2,1)S(1)}, u32[]{:S(2)}, u32[]{:S(2)}) collective-permute-start(bf16[16,7168]{1,0:T(8,128)(2,1)S(1)} %shard_map.126), channel_id=1, source_target_pairs={{0,32},{32,0},{64,96},{96,64},{1,33},{33,1},{65,97},{97,65},{2,34}... | collective-permute-start | bytes 688136 | tf_op jit(solution)/shard_map/ppermute | solution.py:403
  439.4 3.1 collective-permute-start.19
  444.5 1.5 collective-permute-start.20

commit v7 on v6

--- a/solution.py
+++ b/solution.py
@@ -7,7 +7,7 @@
 from jax.sharding import PartitionSpec as P
 
 SHARDS = 4
-COMPUTED, TOKENS, SENT, FIRST, NEXT = range(5)
+COMPUTED, TOKENS, SENT = range(3)
 SECTIONS = 4
 PARTS = 4
 
@@ -74,7 +74,7 @@
         mode = jnp.where(section > step, SENT if step == 1 else TOKENS, COMPUTED)
         mode = jnp.where(section <= step - batches, SENT, mode)
         if step == steps - 1:
-            mode = jnp.where(section < SECTIONS - 1, jnp.where(section == 0, FIRST, NEXT), COMPUTED)
+            mode = jnp.where(section < SECTIONS - 1, jnp.where(section == 0, TOKENS, SENT), COMPUTED)
         m_ref[step] = jnp.full(m_ref.shape[1:], mode, jnp.int32)
 
 
@@ -162,13 +162,27 @@
     return pltpu.with_memory_space_constraint(array, pltpu.VMEM)
 
 
-def unpack(packed_ref, perm, xs, rows):
-    group, width = perm.shape[0], packed_ref.shape[1]
+def unpack(arrived, perm, part):
+    all_rows, width = arrived.shape
+    group = perm.shape[0]
     piece = group // PARTS
-    for g in range(rows // piece):
-        moved = mm(perm, packed_ref[g * group : (g + 1) * group, :]).astype(BF16)
-        for b in range(PARTS):
-            xs[g * piece : (g + 1) * piece, b * width : (b + 1) * width] = moved[b * piece : (b + 1) * piece]
+    some = PARTS // 2
+
+    def kernel(a_ref, p_ref, x_ref):
+        chosen = p_ref[part * some * piece : (part + 1) * some * piece, :]
+        for g in range(all_rows // group):
+            moved = mm(chosen, a_ref[g * group : (g + 1) * group, :]).astype(BF16)
+            for b in range(some):
+                x_ref[g * piece : (g + 1) * piece, b * width : (b + 1) * width] = moved[b * piece : (b + 1) * piece]
+
+    return pl.pallas_call(
+        kernel,
+        out_shape=jax.ShapeDtypeStruct((all_rows // PARTS, some * width), BF16),
+        in_specs=[VMEM_IN] * 2,
+        out_specs=VMEM_IN,
+        compiler_params=params(),
+        cost_estimate=cost(all_rows * group * width, 3 * all_rows * width),
+    )(arrived, perm)
 
 
 def halves(core, depth):
@@ -177,117 +191,107 @@
     return own, other
 
 
-def times(xs, weight_ref):
-    return mm(xs[...], weight_ref[...])
-
-
-def first_half(place, arrived, perm, gate, up, stage):
-    all_rows, width = arrived.shape
-    rows = all_rows // PARTS
-    depth = PARTS * width
-    units = gate.shape[-1]
-
-    def kernel(a_ref, p_ref, g_ref, u_ref, og_ref, ou_ref, xs):
-        unpack(a_ref, p_ref[...], xs, rows)
-        og_ref[...] = times(xs, g_ref)
-        ou_ref[...] = times(xs, u_ref)
-
-    def staging(place_ref, a_ref, p_ref, g_hbm, u_hbm, og_ref, ou_ref, g_ref, u_ref, g_other, u_other, xs, sems):
-        copies = []
-        for part, targets in zip(halves(place_ref[1], depth), ((g_ref, u_ref), (g_other, u_other))):
-            for source, target in zip((g_hbm, u_hbm), targets):
-                copy = pltpu.make_async_copy(source.at[0, part, :], target, sems.at[len(copies)])
-                copy.start()
-                copies.append(copy)
-        unpack(a_ref, p_ref[...], xs, rows)
-        copies[0].wait()
-        og_ref[...] = times(xs, g_ref)
-        copies[1].wait()
-        ou_ref[...] = times(xs, u_ref)
-        copies[2].wait()
-        copies[3].wait()
-
-    sums = [jax.ShapeDtypeStruct((rows, units), F32)] * 2
-    scratch = [pltpu.VMEM((rows, depth), BF16)]
-    estimate = cost(4 * all_rows * width * units, 4 * depth * units)
-    if stage:
-        return pl.pallas_call(
-            staging,
-            out_shape=sums + [pltpu.VMEM((depth, units), BF16)] * 4,
-            in_specs=[SMEM_IN] + [VMEM_IN] * 2 + [HBM_IN] * 2,
-            out_specs=[VMEM_IN] * 6,
-            scratch_shapes=scratch + [pltpu.SemaphoreType.DMA((4,))],
-            compiler_params=params(),
-            cost_estimate=estimate,
-        )(place, arrived, perm, in_hbm(gate), in_hbm(up))
-    return pl.pallas_call(
-        kernel,
-        out_shape=sums,
+def own_half(left, right, gate, up):
+    rows, part = left.shape
+    units = gate.shape[1]
+
+    def kernel(l_ref, r_ref, g_ref, u_ref, og_ref, ou_ref):
+        own_sums(l_ref, r_ref, g_ref, og_ref)
+        own_sums(l_ref, r_ref, u_ref, ou_ref)
+
+    return pl.pallas_call(
+        kernel,
+        out_shape=[jax.ShapeDtypeStruct((rows, units), F32)] * 2,
         in_specs=[VMEM_IN] * 4,
         out_specs=[VMEM_IN] * 2,
-        scratch_shapes=scratch,
-        compiler_params=params(),
-        cost_estimate=estimate,
-    )(arrived, perm, held(gate), held(up))
-
-
-def second_half(place, arrived, perm, gate, up, sum_gate, sum_up, down, others_down, stage):
-    all_rows, width = arrived.shape
-    rows = all_rows // PARTS
-    depth, units = gate.shape
-
-    def kernel(a_ref, p_ref, g_ref, u_ref, sg_ref, su_ref, i_ref, xs):
-        unpack(a_ref, p_ref[...], xs, rows)
-        pre = sg_ref[...] + times(xs, g_ref)
-        upper = su_ref[...] + times(xs, u_ref)
-        i_ref[...] = (pre * lax.logistic(pre) * upper).astype(BF16)
-
-    def staging(place_ref, a_ref, p_ref, g_ref, u_ref, sg_ref, su_ref, own_hbm, other_hbm, i_ref, d_ref, xs, sems):
-        own, _ = halves(place_ref[1], depth)
-        copies = [
-            pltpu.make_async_copy(source.at[0, :, own], d_ref.at[n], sems.at[n])
-            for n, source in enumerate((own_hbm, other_hbm))
-        ]
+        compiler_params=params(),
+        cost_estimate=cost(8 * rows * part * units, 8 * part * units),
+    )(left, right, held(gate), held(up))
+
+
+def own_sums(l_ref, r_ref, w_ref, o_ref):
+    part = l_ref.shape[1]
+    o_ref[...] = mm(l_ref[...], w_ref[:part, :]) + mm(r_ref[...], w_ref[part:, :])
+
+
+def own_half_staging(place, left, right, gate, up, down, others_down):
+    rows, part = left.shape
+    depth, units = 2 * part, gate.shape[2]
+
+    def kernel(place_ref, l_ref, r_ref, g_hbm, u_hbm, d_hbm, e_hbm, og_ref, ou_ref, *rest):
+        targets, sems = rest[:-1], rest[-1]
+        own, other = halves(place_ref[1], depth)
+        sources = [hbm.at[0, half, :] for half in (own, other) for hbm in (g_hbm, u_hbm)]
+        sources += [hbm.at[0, :, own] for hbm in (d_hbm, e_hbm)]
+        copies = [pltpu.make_async_copy(sources[i], targets[i], sems.at[i]) for i in range(6)]
         for copy in copies:
             copy.start()
-        kernel(a_ref, p_ref, g_ref, u_ref, sg_ref, su_ref, i_ref, xs)
-        for copy in copies:
+        copies[0].wait()
+        own_sums(l_ref, r_ref, targets[0], og_ref)
+        copies[1].wait()
+        own_sums(l_ref, r_ref, targets[1], ou_ref)
+        for copy in copies[2:]:
             copy.wait()
 
-    inner = jax.ShapeDtypeStruct((rows, units), BF16)
-    scratch = [pltpu.VMEM((rows, depth), BF16)]
-    estimate = cost(4 * all_rows * width * units, 4 * depth * units)
-    operands = (arrived, perm, held(gate), held(up), sum_gate, sum_up)
-    if stage:
-        return pl.pallas_call(
-            staging,
-            out_shape=[inner, pltpu.VMEM((2, units, depth), BF16)],
-            in_specs=[SMEM_IN] + [VMEM_IN] * 6 + [HBM_IN] * 2,
-            out_specs=[VMEM_IN] * 2,
-            scratch_shapes=scratch + [pltpu.SemaphoreType.DMA((2,))],
-            compiler_params=params(),
-            cost_estimate=estimate,
-        )(place, *operands, in_hbm(down), in_hbm(others_down))
-    return pl.pallas_call(
-        kernel,
-        out_shape=inner,
-        in_specs=[VMEM_IN] * 6,
-        out_specs=VMEM_IN,
-        scratch_shapes=scratch,
-        compiler_params=params(),
-        cost_estimate=estimate,
-    )(*operands), down
+    return pl.pallas_call(
+        kernel,
+        out_shape=[jax.ShapeDtypeStruct((rows, units), F32)] * 2
+        + [pltpu.VMEM((depth, units), BF16)] * 4
+        + [pltpu.VMEM((units, depth), BF16)] * 2,
+        in_specs=[SMEM_IN] + [VMEM_IN] * 2 + [HBM_IN] * 4,
+        out_specs=[VMEM_IN] * 8,
+        scratch_shapes=[pltpu.SemaphoreType.DMA((6,))],
+        compiler_params=params(),
+        cost_estimate=cost(8 * rows * part * units, 24 * depth * units),
+    )(place, left, right, *map(in_hbm, (gate, up, down, others_down)))
+
+
+def third_quarter(left, gate, up, sum_gate, sum_up):
+    rows, part = left.shape
+    units = gate.shape[1]
+
+    def kernel(l_ref, g_ref, u_ref, sg_ref, su_ref, og_ref, ou_ref):
+        og_ref[...] = sg_ref[...] + mm(l_ref[...], g_ref[:part, :])
+        ou_ref[...] = su_ref[...] + mm(l_ref[...], u_ref[:part, :])
+
+    return pl.pallas_call(
+        kernel,
+        out_shape=[jax.ShapeDtypeStruct((rows, units), F32)] * 2,
+        in_specs=[VMEM_IN] * 5,
+        out_specs=[VMEM_IN] * 2,
+        compiler_params=params(),
+        cost_estimate=cost(4 * rows * part * units, 4 * part * units),
+    )(left, held(gate), held(up), sum_gate, sum_up)
+
+
+def last_quarter(right, gate, up, sum_gate, sum_up):
+    rows, part = right.shape
+    units = gate.shape[1]
+
+    def kernel(r_ref, g_ref, u_ref, sg_ref, su_ref, i_ref):
+        pre = sg_ref[...] + mm(r_ref[...], g_ref[part:, :])
+        upper = su_ref[...] + mm(r_ref[...], u_ref[part:, :])
+        i_ref[...] = (pre * lax.logistic(pre) * upper).astype(BF16)
+
+    return pl.pallas_call(
+        kernel,
+        out_shape=jax.ShapeDtypeStruct((rows, units), BF16),
+        in_specs=[VMEM_IN] * 5,
+        out_specs=VMEM_IN,
+        compiler_params=params(),
+        cost_estimate=cost(4 * rows * part * units, 4 * part * units),
+    )(right, held(gate), held(up), sum_gate, sum_up)
 
 
 def own_units(inner, down):
     rows, units = inner.shape
-    depth = down.shape[2]
+    depth = down.shape[1]
     piece = depth // PARTS
 
     def kernel(i_ref, d_ref, o_ref):
         for b in range(PARTS):
             cols = slice(b * piece, (b + 1) * piece)
-            o_ref[:, cols] = mm(i_ref[...], d_ref[0, :, cols])
+            o_ref[:, cols] = mm(i_ref[...], d_ref[:, cols])
 
     return pl.pallas_call(
         kernel,
@@ -307,7 +311,7 @@
     def kernel(i_ref, d_ref, t_ref, q_ref, o_ref, ys):
         for b in range(PARTS):
             cols = slice(b * width, (b + 1) * width)
-            ys[b] = (t_ref[:, cols] + mm(i_ref[...], d_ref[1, :, cols])).astype(BF16)
+            ys[b] = (t_ref[:, cols] + mm(i_ref[...], d_ref[:, cols])).astype(BF16)
         for g in range(rows // piece):
             stack = jnp.concatenate([ys[b, g * piece : (g + 1) * piece, :] for b in range(PARTS)], axis=0)
             o_ref[g * group : (g + 1) * group, :] = mm(q_ref[...], stack).astype(BF16)
@@ -323,37 +327,35 @@
     )(inner, held(down), total, back)
 
 
-def combine(returned, spread, scales, modes, hidden, tokens, step, finished=()):
+def combine(returned, spread, scales, modes, hidden, tokens, step):
     rows, width = returned.shape
     tok, full = hidden.shape
     blocks = full // width
     picks = spread.shape[1] // blocks
     routes_each = picks // tok
 
-    def kernel(r_ref, s_ref, w_ref, m_ref, h_ref, t_ref, *rest):
-        o_ref = rest[-1]
+    def kernel(r_ref, s_ref, w_ref, m_ref, h_ref, t_ref, o_ref):
         got = mm(s_ref[step], r_ref[...])
         scale = w_ref[step][:, :1]
         mode = jnp.broadcast_to(m_ref[step, :1, :1], (tok, 1))
-        others = {TOKENS: t_ref, SENT: h_ref, **dict(zip((FIRST, NEXT), rest[:-1]))}
         for b in range(blocks):
             cols = slice(b * width, (b + 1) * width)
             total = h_ref[:, cols].astype(F32)
             for k in range(routes_each):
                 at = b * picks + k * tok
                 total += scale[k * tok : (k + 1) * tok] * got[at : at + tok]
-            for kind, ref in others.items():
+            for kind, ref in ((TOKENS, t_ref), (SENT, h_ref)):
                 total = jnp.where(mode == kind, ref[:, cols].astype(F32), total)
             o_ref[:, cols] = total.astype(BF16)
 
     return pl.pallas_call(
         kernel,
         out_shape=jax.ShapeDtypeStruct((tok, full), BF16),
-        in_specs=[VMEM_IN] * (6 + len(finished)),
+        in_specs=[VMEM_IN] * 6,
         out_specs=VMEM_IN,
         compiler_params=params(),
         cost_estimate=cost(2 * spread.shape[1] * rows * width, 2 * rows * width),
-    )(returned, held(spread), held(scales), held(modes), hidden, held(tokens), *finished)
+    )(returned, held(spread), held(scales), held(modes), hidden, tokens)
 
 
 def per_device(tokens, norm_gain, gate_weight, up_weight, down_weight, routes, route_weights):
@@ -367,6 +369,13 @@
     section = lax.axis_index("section")
     core = lax.axis_index("expert") % 2
     place = jnp.stack([section, core]).astype(jnp.int32)
+
+    group = 8 * PARTS * capacity
+    at = jnp.arange(group, dtype=jnp.int32)
+    wanted = (at % (8 * capacity)) // capacity * (PARTS * capacity) + at // (8 * capacity) * capacity + at % capacity
+    perm = (wanted[:, None] == at[None, :]).astype(BF16)
+    back = (at[:, None] == wanted[None, :]).astype(BF16)
+    place, perm, back = lax.optimization_barrier((place, perm, back))
 
     slots = experts * capacity
     unit = PARTS * capacity
@@ -382,18 +391,9 @@
         place, tokens[0], norm_gain, row_keys, by_route(routes), by_route(route_weights), sent, slots, capacity, experts, steps
     )
 
-    group = 8 * PARTS * capacity
-    at = jnp.arange(group, dtype=jnp.int32)
-    wanted = (at % (8 * capacity)) // capacity * (PARTS * capacity) + at // (8 * capacity) * capacity + at % capacity
-    perm = (wanted[:, None] == at[None, :]).astype(BF16)
-    back = (at[:, None] == wanted[None, :]).astype(BF16)
-
     swap = [(i, i ^ 1) for i in range(devices)]
-    perm, back = lax.optimization_barrier((perm, back))
-    gate, up, down = gate_weight, up_weight, down_weight
     others_down = lax.ppermute(down_weight, "expert", swap)
     hidden = own
-    finished = []
     for step in range(steps):
         if step > 0:
             if step in (1, steps - 1):
@@ -401,26 +401,27 @@
             else:
                 pairs = [(i, (i + 1) % sections) for i in range(sections)]
             hidden = lax.ppermute(current, "section", pairs)
-            if step in (batches, steps - 1):
-                finished.append(hidden)
+            if step == batches:
+                own = hidden
             packed = front(hidden, gain, keys, row_keys, step, width=width, experts=experts)
         arrived = lax.all_to_all(packed, "expert", split_axis=0, concat_axis=0, tiled=True)
-        others = lax.ppermute(arrived, "expert", swap)
-        stage = step == 0
-        sum_gate, sum_up, *staged = first_half(place, arrived, perm, gate, up, stage)
-        if stage:
-            gate, up, other_gate, other_up = staged
-        inner, down = second_half(
-            place, others, perm, other_gate, other_up, sum_gate, sum_up, down, others_down, stage
-        )
+        left = unpack(arrived, perm, 0)
+        others_left = lax.ppermute(left, "expert", swap)
+        right = unpack(arrived, perm, 1)
+        others_right = lax.ppermute(right, "expert", swap)
+        if step == 0:
+            sum_gate, sum_up, gate, up, other_gate, other_up, down, other_down = own_half_staging(
+                place, left, right, gate_weight, up_weight, down_weight, others_down
+            )
+        else:
+            sum_gate, sum_up = own_half(left, right, gate, up)
+        sum_gate, sum_up = third_quarter(others_left, other_gate, other_up, sum_gate, sum_up)
+        inner = last_quarter(others_right, other_gate, other_up, sum_gate, sum_up)
         others_inner = lax.ppermute(inner, "expert", swap)
         total = own_units(inner, down)
-        partial_value = other_units(others_inner, down, total, back, width)
+        partial_value = other_units(others_inner, other_down, total, back, width)
         returned = lax.all_to_all(partial_value, "expert", split_axis=0, concat_axis=0, tiled=True)
-        is_last = step == steps - 1
-        current = combine(
-            returned, spread, scales, modes, hidden, own, step, finished if is_last else ()
-        )
+        current = combine(returned, spread, scales, modes, hidden, own, step)
     return current[None]
 
 

time: 481 us -> 480 us (level)
  waiting for transfers between devices: 51.5 us -> 46.3 us
    ppermute x7 -> x14, waiting for transfers between devices: 5.35 us -> 0.04 us  [the longest x7 0.02 us: per_device(): others_right = lax.ppermute(right, 'expert', swap)]
    pallas_call x14 -> x35, Pallas kernels: 34.1 us -> 34.9 us  [the longest x6 9.48 us: own_half(): pl.pallas_call(kernel, out_shape=[jax.ShapeDtypeStruct((rows, units), F32...]
  transfers between devices with their start and end apart: 21 -> 28, of which waited for: 19 -> 13; matrix products, arithmetic and copies ran while one was open for 0% -> 0% of each run, Pallas kernels for 6% -> 8%
where the time goes in v7:
time: 480 us; the launch traced here: 472 us
  blocking collectives  348 us (72%)
  Pallas kernels  63.2 us (13%)
  waiting for transfers between devices  46.3 us (10%)
  starting transfers between devices  13.1 us (3%)
    all_to_all x7, blocking collectives, per_device(): lax.all_to_all(packed, 'expert', split_axis=0, concat_axis=0, tiled=True)  178 us
    all_to_all x7, blocking collectives, per_device(): lax.all_to_all(partial_value, 'expert', split_axis=0, concat_axis=0, tile...  170 us
    ppermute x6, waiting for transfers between devices, per_device(): hidden = lax.ppermute(current, 'section', pairs)  45 us
    pallas_call x7, Pallas kernels, other_units(): pl.pallas_call(kernel, out_shape=jax.ShapeDtypeStruct((rows * PARTS, widt...  10.7 us
  transfers between devices with their start and end apart: 28, of which 13 were waited for; matrix products, arithmetic and copies ran while one was open for 0% of the time, Pallas kernels for 8%

profile of v7, /device:TPU:1, one launch (start us, length us, event | category | flops | bytes accessed | tf_op | source)
XLA Modules:
  0.0 472.1 jit_solution(7140641406615920324)
XLA Ops:
  0.0 1.4 collective-permute-start.1
  1.6 2.8 shard_map.91
  4.5 27.9 %all_to_all.154 = bf16[32,24,896]{2,1,0:T(8,128)(2,1)S(1)} all-to-all(bf16[32,24,896]{2,1,0:T(8,128)(2,1)S(1)} %bitcast.72), channel_id=1, replica_groups=mesh['section'=4,'expert'=32] {'expert'}, dimensions={0} | all-to-all | bytes 2752512 | tf_op jit(solution)/shard_map/all_to_all | solution.py:407
  33.8 7.9 %shard_map.94 = (f32[192,512]{1,0:T(8,128)S(1)}, f32[192,512]{1,0:T(8,128)S(1)}, bf16[3584,512]{1,0:T(8,128)(2,1)S(1)}, bf16[3584,512]{1,0:T(8,128)(2,1)S(1)}, b...) custom-call(s32[2]{0:T(128)S(1)} %pad_add_fusion.place_ref, ...), custom_call_target="tpu_custom_call" | custom-call | flops 1409286144 | bytes 44040192 | tf_op jit(solution)/shard_map/pallas_call | solution.py:236
  41.7 0.9 shard_map.95
  42.6 0.9 shard_map.96.i_ref
  43.9 1.0 shard_map.97.t_ref
  45.1 1.5 shard_map.98
  46.6 24.3 %all_to_all.155 = bf16[32,24,896]{2,1,0:T(8,128)(2,1)S(1)} all-to-all(bf16[32,24,896]{2,1,0:T(8,128)(2,1)S(1)} %bitcast.66), channel_id=1, replica_groups=mesh['section'=4,'expert'=32] {'expert'}, dimensions={0} | all-to-all | bytes 2752512 | tf_op jit(solution)/shard_map/all_to_all | solution.py:423
  71.5 1.7 collective-permute-start.4
  73.2 5.7 %collective-permute-done.4.refs_0_.h_ref = bf16[16,7168]{1,0:T(8,128)(2,1)S(1)} collective-permute-done((bf16[16,7168]{1,0:T(8,128)(2,1)S(1)}, bf16[16,7168]{1,0:T(8,128)(2,1)S(1)}, u32[]{:S(2)}, u32[]{:S(2)}) %collective-permute-start.4) | collective-permute-done | bytes 229408 | tf_op jit(solution)/shard_map/ppermute | solution.py:403
  79.4 24.8 %all_to_all.156 = bf16[32,24,896]{2,1,0:T(8,128)(2,1)S(1)} all-to-all(bf16[32,24,896]{2,1,0:T(8,128)(2,1)S(1)} %bitcast.60), channel_id=1, replica_groups=mesh['section'=4,'expert'=32] {'expert'}, dimensions={0} | all-to-all | bytes 2752512 | tf_op jit(solution)/shard_map/all_to_all | solution.py:407
  105.3 0.8 collective-permute-start.5
  106.1 1.6 shard_map.103
  107.7 0.9 shard_map.104
  108.6 0.9 shard_map.105.i_ref
  109.9 1.0 shard_map.106.t_ref
  111.1 1.5 shard_map.107
  112.6 24.3 %all_to_all.157 = bf16[32,24,896]{2,1,0:T(8,128)(2,1)S(1)} all-to-all(bf16[32,24,896]{2,1,0:T(8,128)(2,1)S(1)} %bitcast.67), channel_id=1, replica_groups=mesh['section'=4,'expert'=32] {'expert'}, dimensions={0} | all-to-all | bytes 2752512 | tf_op jit(solution)/shard_map/all_to_all | solution.py:423
  136.9 0.6 shard_map.108
  137.5 1.7 collective-permute-start.8
  139.2 7.9 %collective-permute-done.8.refs_0_.h_ref = bf16[16,7168]{1,0:T(8,128)(2,1)S(1)} collective-permute-done((bf16[16,7168]{1,0:T(8,128)(2,1)S(1)}, bf16[16,7168]{1,0:T(8,128)(2,1)S(1)}, u32[]{:S(2)}, u32[]{:S(2)}) %collective-permute-start.8) | collective-permute-done | bytes 229408 | tf_op jit(solution)/shard_map/ppermute | solution.py:403
  147.6 24.5 %all_to_all.158 = bf16[32,24,896]{2,1,0:T(8,128)(2,1)S(1)} all-to-all(bf16[32,24,896]{2,1,0:T(8,128)(2,1)S(1)} %bitcast.61), channel_id=1, replica_groups=mesh['section'=4,'expert'=32] {'expert'}, dimensions={0} | all-to-all | bytes 2752512 | tf_op jit(solution)/shard_map/all_to_all | solution.py:407
  173.6 1.6 shard_map.112
  175.2 0.9 shard_map.113
  176.1 0.9 shard_map.114.i_ref
  177.5 1.0 shard_map.115.t_ref
  178.7 1.5 shard_map.116
  180.2 24.3 %all_to_all.159 = bf16[32,24,896]{2,1,0:T(8,128)(2,1)S(1)} all-to-all(bf16[32,24,896]{2,1,0:T(8,128)(2,1)S(1)} %bitcast.68), channel_id=1, replica_groups=mesh['section'=4,'expert'=32] {'expert'}, dimensions={0} | all-to-all | bytes 2752512 | tf_op jit(solution)/shard_map/all_to_all | solution.py:423
  204.5 0.6 shard_map.117
  205.2 8.1 %collective-permute-done.12.refs_0_.h_ref = bf16[16,7168]{1,0:T(8,128)(2,1)S(1)} collective-permute-done((bf16[16,7168]{1,0:T(8,128)(2,1)S(1)}, bf16[16,7168]{1,0:T(8,128)(2,1)S(1)}, u32[]{:S(2)}, u32[]{:S(2)}) %collective-permute-start.12) | collective-permute-done | bytes 229408 | tf_op jit(solution)/shard_map/ppermute | solution.py:403
  213.8 25.2 %all_to_all.160 = bf16[32,24,896]{2,1,0:T(8,128)(2,1)S(1)} all-to-all(bf16[32,24,896]{2,1,0:T(8,128)(2,1)S(1)} %bitcast.62), channel_id=1, replica_groups=mesh['section'=4,'expert'=32] {'expert'}, dimensions={0} | all-to-all | bytes 2752512 | tf_op jit(solution)/shard_map/all_to_all | solution.py:407
  240.4 1.6 shard_map.121
  242.0 0.9 shard_map.122
  242.9 0.9 shard_map.123.i_ref
  244.2 1.0 shard_map.124.t_ref
  245.3 1.5 shard_map.125
  246.9 24.3 %all_to_all.161 = bf16[32,24,896]{2,1,0:T(8,128)(2,1)S(1)} all-to-all(bf16[32,24,896]{2,1,0:T(8,128)(2,1)S(1)} %bitcast.69), channel_id=1, replica_groups=mesh['section'=4,'expert'=32] {'expert'}, dimensions={0} | all-to-all | bytes 2752512 | tf_op jit(solution)/shard_map/all_to_all | solution.py:423
  271.2 0.6 shard_map.126
  271.9 8.1 %collective-permute-done.16.refs_0_.h_ref.t_ref = bf16[16,7168]{1,0:T(8,128)(2,1)S(1)} collective-permute-done((bf16[16,7168]{1,0:T(8,128)(2,1)S(1)}, bf16[16,7168]{1,0:T(8,128)(2,1)S(1)}, u32[]{:S(2)}, u32[]{:S(2)}) %collective-permute-start.16) | collective-permute-done | bytes 229408 | tf_op jit(solution)/shard_map/ppermute | solution.py:403
  280.5 25.3 %all_to_all.162 = bf16[32,24,896]{2,1,0:T(8,128)(2,1)S(1)} all-to-all(bf16[32,24,896]{2,1,0:T(8,128)(2,1)S(1)} %bitcast.63), channel_id=1, replica_groups=mesh['section'=4,'expert'=32] {'expert'}, dimensions={0} | all-to-all | bytes 2752512 | tf_op jit(solution)/shard_map/all_to_all | solution.py:407
  307.3 1.6 shard_map.130
  308.9 0.9 shard_map.131
  309.8 0.9 shard_map.132.i_ref
  311.1 1.0 shard_map.133.t_ref
  312.2 1.5 shard_map.134
  313.7 24.3 %all_to_all.163 = bf16[32,24,896]{2,1,0:T(8,128)(2,1)S(1)} all-to-all(bf16[32,24,896]{2,1,0:T(8,128)(2,1)S(1)} %bitcast.70), channel_id=1, replica_groups=mesh['section'=4,'expert'=32] {'expert'}, dimensions={0} | all-to-all | bytes 2752512 | tf_op jit(solution)/shard_map/all_to_all | solution.py:423
  338.7 8.1 %collective-permute-done.20.refs_0_.h_ref = bf16[16,7168]{1,0:T(8,128)(2,1)S(1)} collective-permute-done((bf16[16,7168]{1,0:T(8,128)(2,1)S(1)}, bf16[16,7168]{1,0:T(8,128)(2,1)S(1)}, u32[]{:S(2)}, u32[]{:S(2)}) %collective-permute-start.20) | collective-permute-done | bytes 229408 | tf_op jit(solution)/shard_map/ppermute | solution.py:403
  347.4 25.2 %all_to_all.164 = bf16[32,24,896]{2,1,0:T(8,128)(2,1)S(1)} all-to-all(bf16[32,24,896]{2,1,0:T(8,128)(2,1)S(1)} %bitcast.64), channel_id=1, replica_groups=mesh['section'=4,'expert'=32] {'expert'}, dimensions={0} | all-to-all | bytes 2752512 | tf_op jit(solution)/shard_map/all_to_all | solution.py:407
  374.0 1.6 shard_map.139
  375.6 0.9 shard_map.140
  376.5 0.9 shard_map.141.i_ref
  378.0 1.0 shard_map.142.t_ref
  379.1 1.5 shard_map.143
  380.7 24.3 %all_to_all.165 = bf16[32,24,896]{2,1,0:T(8,128)(2,1)S(1)} all-to-all(bf16[32,24,896]{2,1,0:T(8,128)(2,1)S(1)} %bitcast.71), channel_id=1, replica_groups=mesh['section'=4,'expert'=32] {'expert'}, dimensions={0} | all-to-all | bytes 2752512 | tf_op jit(solution)/shard_map/all_to_all | solution.py:423
  405.7 6.9 %collective-permute-done.24.refs_0_.h_ref = bf16[16,7168]{1,0:T(8,128)(2,1)S(1)} collective-permute-done((bf16[16,7168]{1,0:T(8,128)(2,1)S(1)}, bf16[16,7168]{1,0:T(8,128)(2,1)S(1)}, u32[]{:S(2)}, u32[]{:S(2)}) %collective-permute-start.24) | collective-permute-done | bytes 229408 | tf_op jit(solution)/shard_map/ppermute | solution.py:403
  413.1 25.2 %all_to_all.166 = bf16[32,24,896]{2,1,0:T(8,128)(2,1)S(1)} all-to-all(bf16[32,24,896]{2,1,0:T(8,128)(2,1)S(1)} %bitcast.54), channel_id=1, replica_groups=mesh['section'=4,'expert'=32] {'expert'}, dimensions={0} | all-to-all | bytes 2752512 | tf_op jit(solution)/shard_map/all_to_all | solution.py:407
  439.7 1.6 shard_map.148
  441.3 0.9 shard_map.149
  442.2 0.9 shard_map.150.i_ref
  443.4 1.0 shard_map.151.t_ref
  444.6 1.5 shard_map.152
  446.1 24.3 %all_to_all.167 = bf16[32,24,896]{2,1,0:T(8,128)(2,1)S(1)} all-to-all(bf16[32,24,896]{2,1,0:T(8,128)(2,1)S(1)} %bitcast.65), channel_id=1, replica_groups=mesh['section'=4,'expert'=32] {'expert'}, dimensions={0} | all-to-all | bytes 2752512 | tf_op jit(solution)/shard_map/all_to_all | solution.py:423
  470.4 1.3 shard_map.153
  (72 shorter events, 18.9 us)
Async XLA Ops:
  0.0 33.8 %collective-permute-start.1 = (bf16[1,512,7168]{2,1,0:T(8,128)(2,1)}, bf16[1,512,7168]{2,1,0:T(8,128)(2,1)}, u32[]{:S(2)}, u32[]{:S(2)}) collective-permute-start(bf16[1,512,7168]{2,1,0:T(8,128)(2,1)} %d_hbm.1), channel_id=1, source_target_pairs={{0,1},{1,0},{2,3},{3,2},{4,5},{5,4},{6,7},{7,6},{8,9},{9,8},{10,11... | collective-permute-start | bytes 22020104 | tf_op jit(solution)/shard_map/ppermute | solution.py:395
  32.7 9.0 %collective-permute-start.2 = (bf16[192,1792]{1,0:T(8,128)(2,1)S(1)}, bf16[192,1792]{1,0:T(8,128)(2,1)S(1)}, u32[]{:S(2)}, u32[]{:S(2)}) collective-permute-start(bf16[192,1792]{1,0:T(8,128)(2,1)S(1)} %shard_map.93.l_ref), channel_id=1, source_target_pairs={{0,1},{1,0},{2,3},{3,2},{4,5},{5,4},{6,7},{7,6},{8,9},{9,8},{10,11... | collective-permute-start | bytes 2064392 | tf_op jit(solution)/shard_map/ppermute | solution.py:409
  33.4 9.2 %collective-permute-start = (bf16[192,1792]{1,0:T(8,128)(2,1)S(1)}, bf16[192,1792]{1,0:T(8,128)(2,1)S(1)}, u32[]{:S(2)}, u32[]{:S(2)}) collective-permute-start(bf16[192,1792]{1,0:T(8,128)(2,1)S(1)} %shard_map.92.r_ref), channel_id=1, source_target_pairs={{0,1},{1,0},{2,3},{3,2},{4,5},{5,4},{6,7},{7,6},{8,9},{9,8},{10,11... | collective-permute-start | bytes 2064392 | tf_op jit(solution)/shard_map/ppermute | solution.py:411
  43.5 1.5 collective-permute-start.3
  71.5 7.4 %collective-permute-start.4 = (bf16[16,7168]{1,0:T(8,128)(2,1)S(1)}, bf16[16,7168]{1,0:T(8,128)(2,1)S(1)}, u32[]{:S(2)}, u32[]{:S(2)}) collective-permute-start(bf16[16,7168]{1,0:T(8,128)(2,1)S(1)} %shard_map.99), channel_id=1, source_target_pairs={{0,32},{32,0},{64,96},{96,64},{1,33},{33,1},{65,97},{97,65},{2,34}... | collective-permute-start | bytes 688136 | tf_op jit(solution)/shard_map/ppermute | solution.py:403
  104.6 3.1 collective-permute-start.6
  105.3 3.3 collective-permute-start.5
  109.5 1.5 collective-permute-start.7
  137.5 9.6 %collective-permute-start.8 = (bf16[16,7168]{1,0:T(8,128)(2,1)S(1)}, bf16[16,7168]{1,0:T(8,128)(2,1)S(1)}, u32[]{:S(2)}, u32[]{:S(2)}) collective-permute-start(bf16[16,7168]{1,0:T(8,128)(2,1)S(1)} %shard_map.108), channel_id=1, source_target_pairs={{0,32},{32,64},{64,96},{96,0},{1,33},{33,65},{65,97},{97,1},{2,34}... | collective-permute-start | bytes 688136 | tf_op jit(solution)/shard_map/ppermute | solution.py:403
  172.5 2.6 collective-permute-start.10
  173.2 2.8 collective-permute-start.9
  177.0 1.7 collective-permute-start.11
  205.1 8.2 %collective-permute-start.12 = (bf16[16,7168]{1,0:T(8,128)(2,1)S(1)}, bf16[16,7168]{1,0:T(8,128)(2,1)S(1)}, u32[]{:S(2)}, u32[]{:S(2)}) collective-permute-start(bf16[16,7168]{1,0:T(8,128)(2,1)S(1)} %shard_map.117), channel_id=1, source_target_pairs={{0,32},{32,64},{64,96},{96,0},{1,33},{33,65},{65,97},{97,1},{2,34}... | collective-permute-start | bytes 688136 | tf_op jit(solution)/shard_map/ppermute | solution.py:403
  239.4 2.6 collective-permute-start.14
  240.1 2.8 collective-permute-start.13
  243.8 1.5 collective-permute-start.15
  271.8 8.2 %collective-permute-start.16 = (bf16[16,7168]{1,0:T(8,128)(2,1)S(1)}, bf16[16,7168]{1,0:T(8,128)(2,1)S(1)}, u32[]{:S(2)}, u32[]{:S(2)}) collective-permute-start(bf16[16,7168]{1,0:T(8,128)(2,1)S(1)} %shard_map.126), channel_id=1, source_target_pairs={{0,32},{32,64},{64,96},{96,0},{1,33},{33,65},{65,97},{97,1},{2,34}... | collective-permute-start | bytes 688136 | tf_op jit(solution)/shard_map/ppermute | solution.py:403
  306.2 2.6 collective-permute-start.18
  307.0 2.8 collective-permute-start.17
  310.7 1.5 collective-permute-start.19
  338.7 8.2 %collective-permute-start.20 = (bf16[16,7168]{1,0:T(8,128)(2,1)S(1)}, bf16[16,7168]{1,0:T(8,128)(2,1)S(1)}, u32[]{:S(2)}, u32[]{:S(2)}) collective-permute-start(bf16[16,7168]{1,0:T(8,128)(2,1)S(1)} %shard_map.135), channel_id=1, source_target_pairs={{0,32},{32,64},{64,96},{96,0},{1,33},{33,65},{65,97},{97,1},{2,34}... | collective-permute-start | bytes 688136 | tf_op jit(solution)/shard_map/ppermute | solution.py:403
  372.9 2.6 collective-permute-start.22
  373.6 2.8 collective-permute-start.21
  377.4 1.8 collective-permute-start.23
  405.6 7.0 %collective-permute-start.24 = (bf16[16,7168]{1,0:T(8,128)(2,1)S(1)}, bf16[16,7168]{1,0:T(8,128)(2,1)S(1)}, u32[]{:S(2)}, u32[]{:S(2)}) collective-permute-start(bf16[16,7168]{1,0:T(8,128)(2,1)S(1)} %shard_map.144), channel_id=1, source_target_pairs={{0,32},{32,0},{64,96},{96,64},{1,33},{33,1},{65,97},{97,65},{2,34}... | collective-permute-start | bytes 688136 | tf_op jit(solution)/shard_map/ppermute | solution.py:403
  438.7 2.6 collective-permute-start.26
  439.4 2.8 collective-permute-start.25
  443.1 1.5 collective-permute-start.27

commit v8 on v7

--- a/solution.py
+++ b/solution.py
@@ -38,33 +38,49 @@
     return jnp.dot(a, b, preferred_element_type=F32)
 
 
-def plan(section, steps, ids_ref, w_ref, sent_ref, k_ref, s_ref, c_ref, m_ref, slots, capacity):
+def slot_codes(section, step, ids_ref, capacity):
     batches, routes_each, tok = ids_ref.shape
-    lanes = k_ref.shape[2]
-    picks = routes_each * tok
     sub = lax.broadcasted_iota(jnp.int32, (tok, tok), 0)
     lane = lax.broadcasted_iota(jnp.int32, (tok, tok), 1)
-    wide_sub = lax.broadcasted_iota(jnp.int32, (tok, lanes), 0)
-    wide_lane = lax.broadcasted_iota(jnp.int32, (tok, lanes), 1)
-
-    def column(values):
-        values = jnp.broadcast_to(values, (tok, tok))
-        return jnp.sum(jnp.where(sub == lane, values, jnp.zeros_like(values)), axis=1, keepdims=True)
-
+    ids = ids_ref[jnp.clip(step - section, 0, batches - 1)]
+    rows = [ids[k : k + 1] for k in range(routes_each)]
+    codes = []
+    for k in range(routes_each):
+        own = column(rows[k])
+        code = own * capacity
+        for before in range(k + 1):
+            same = own == rows[before]
+            if before == k:
+                same &= lane < sub
+            code += jnp.sum(jnp.where(same, 1, 0), axis=1, keepdims=True)
+        codes.append(code)
+    return codes
+
+
+def column(row):
+    tok = row.shape[1]
+    sub = lax.broadcasted_iota(jnp.int32, (tok, tok), 0)
+    lane = lax.broadcasted_iota(jnp.int32, (tok, tok), 1)
+    values = jnp.broadcast_to(row, (tok, tok))
+    return jnp.sum(jnp.where(sub == lane, values, jnp.zeros_like(values)), axis=1, keepdims=True)
+
+
+def plan_pack(section, steps, ids_ref, k_ref, slots, capacity):
+    tok, lanes = ids_ref.shape[2], k_ref.shape[2]
+    sub = lax.broadcasted_iota(jnp.int32, (tok, lanes), 0)
+    lane = lax.broadcasted_iota(jnp.int32, (tok, lanes), 1)
     for step in range(steps):
-        m = jnp.clip(step - section, 0, batches - 1)
-        ids, weights = ids_ref[m], w_ref[m]
-        rows = [ids[k : k + 1] for k in range(routes_each)]
-        for k in range(routes_each):
-            own = column(rows[k])
-            code = own * capacity
-            for before in range(k + 1):
-                same = own == rows[before]
-                if before == k:
-                    same &= lane < sub
-                code += jnp.sum(jnp.where(same, 1, 0), axis=1, keepdims=True)
-            lane_code = jnp.sum(jnp.where(wide_sub == wide_lane % tok, code, 0), axis=0, keepdims=True)
-            k_ref[step, k : k + 1, :] = lane_code + wide_lane[:1] // tok * slots
+        for k, code in enumerate(slot_codes(section, step, ids_ref, capacity)):
+            lane_code = jnp.sum(jnp.where(sub == lane % tok, code, 0), axis=0, keepdims=True)
+            k_ref[step, k : k + 1, :] = lane_code + lane[:1] // tok * slots
+
+
+def plan_combine(section, steps, ids_ref, w_ref, sent_ref, s_ref, c_ref, m_ref, slots, capacity):
+    batches, routes_each, tok = ids_ref.shape
+    picks = routes_each * tok
+    for step in range(steps):
+        weights = w_ref[jnp.clip(step - section, 0, batches - 1)]
+        for k, code in enumerate(slot_codes(section, step, ids_ref, capacity)):
             for b in range(2 * PARTS):
                 at = b * picks + k * tok
                 hit = code + b * slots == sent_ref[...]
@@ -97,27 +113,34 @@
             o_ref[at : at + piece, :] = out[e * piece : (e + 1) * piece]
 
 
-def begin(place, tokens, gain, row_keys, ids, weights, sent, slots, capacity, experts, steps):
-    batches, routes_each, tok = ids.shape
+def halves(core, depth):
+    own = pl.ds(pl.multiple_of(core * depth, depth), depth)
+    other = pl.ds(pl.multiple_of((1 - core) * depth, depth), depth)
+    return own, other
+
+
+def begin(place, tokens, gain, row_keys, ids, gate, slots, capacity, experts, steps):
+    routes_each = ids.shape[1]
     rows, lanes = row_keys.shape
-    picks = routes_each * tok
     full = tokens.shape[1]
 
     def kernel(place_ref, *refs):
-        sources, rest = refs[:6], refs[6:]
-        h_ref, g_ref, r_ref, k_ref, s_ref, c_ref, m_ref, o_ref, ids_ref, w_ref, sent_ref, sems = rest
-        targets = (h_ref, g_ref, r_ref, ids_ref, w_ref, sent_ref)
-        copies = [pltpu.make_async_copy(sources[i], targets[i], sems.at[i]) for i in range(6)]
+        sources, gate_hbm, rest = refs[:4], refs[4], refs[5:]
+        h_ref, g_ref, r_ref, k_ref, o_ref, gate_ref, ids_ref, sems = rest
+        own, _ = halves(place_ref[1], full // 2)
+        sources += (gate_hbm.at[0, own, :],)
+        targets = (h_ref, g_ref, r_ref, ids_ref, gate_ref)
+        copies = [pltpu.make_async_copy(sources[i], targets[i], sems.at[i]) for i in range(5)]
         for copy in copies:
             copy.start()
-        for copy in copies[3:]:
-            copy.wait()
-        plan(place_ref[0], steps, ids_ref, w_ref, sent_ref, k_ref, s_ref, c_ref, m_ref, slots, capacity)
+        copies[3].wait()
+        plan_pack(place_ref[0], steps, ids_ref, k_ref, slots, capacity)
         for copy in copies[:3]:
             copy.wait()
         pack(0, h_ref, g_ref, k_ref, r_ref, o_ref, experts)
-
-    sources = (tokens, gain, row_keys, ids, weights, sent)
+        copies[4].wait()
+
+    sources = (tokens, gain, row_keys, ids, gate)
     return pl.pallas_call(
         kernel,
         out_shape=[
@@ -125,19 +148,12 @@
             pltpu.VMEM(gain.shape, F32),
             pltpu.VMEM(row_keys.shape, jnp.int32),
             pltpu.VMEM((steps, routes_each, lanes), jnp.int32),
-            pltpu.VMEM((steps, 2 * PARTS * picks, sent.shape[1]), BF16),
-            pltpu.VMEM((steps, picks, 128), F32),
-            pltpu.VMEM((steps, 8, 128), jnp.int32),
             jax.ShapeDtypeStruct((2 * rows, full // (2 * PARTS)), BF16),
+            pltpu.VMEM((full // 2, gate.shape[2]), BF16),
         ],
-        in_specs=[SMEM_IN] + [HBM_IN] * 6,
-        out_specs=[VMEM_IN] * 8,
-        scratch_shapes=[
-            pltpu.VMEM(ids.shape, jnp.int32),
-            pltpu.VMEM(weights.shape, F32),
-            pltpu.VMEM(sent.shape, jnp.int32),
-            pltpu.SemaphoreType.DMA((6,)),
-        ],
+        in_specs=[SMEM_IN] + [HBM_IN] * 5,
+        out_specs=[VMEM_IN] * 6,
+        scratch_shapes=[pltpu.VMEM(ids.shape, jnp.int32), pltpu.SemaphoreType.DMA((5,))],
         compiler_params=params(),
     )(place, *[in_hbm(array) for array in sources])
 
@@ -185,12 +201,6 @@
     )(arrived, perm)
 
 
-def halves(core, depth):
-    own = pl.ds(pl.multiple_of(core * depth, depth), depth)
-    other = pl.ds(pl.multiple_of((1 - core) * depth, depth), depth)
-    return own, other
-
-
 def own_half(left, right, gate, up):
     rows, part = left.shape
     units = gate.shape[1]
@@ -214,36 +224,51 @@
     o_ref[...] = mm(l_ref[...], w_ref[:part, :]) + mm(r_ref[...], w_ref[part:, :])
 
 
-def own_half_staging(place, left, right, gate, up, down, others_down):
+def own_half_staging(place, left, right, own_gate, gate, up, down, others_down, ids, weights, sent, slots, capacity, steps):
     rows, part = left.shape
     depth, units = 2 * part, gate.shape[2]
-
-    def kernel(place_ref, l_ref, r_ref, g_hbm, u_hbm, d_hbm, e_hbm, og_ref, ou_ref, *rest):
-        targets, sems = rest[:-1], rest[-1]
+    picks = ids.shape[1] * ids.shape[2]
+
+    def kernel(place_ref, l_ref, r_ref, own_ref, g_hbm, u_hbm, d_hbm, e_hbm, ids_hbm, w_hbm, sent_hbm, *rest):
+        og_ref, ou_ref, *targets, s_ref, c_ref, m_ref, ids_ref, w_ref, sent_ref, sems = rest
         own, other = halves(place_ref[1], depth)
-        sources = [hbm.at[0, half, :] for half in (own, other) for hbm in (g_hbm, u_hbm)]
+        sources = [ids_hbm, w_hbm, sent_hbm]
+        sources += [u_hbm.at[0, own, :], g_hbm.at[0, other, :], u_hbm.at[0, other, :]]
         sources += [hbm.at[0, :, own] for hbm in (d_hbm, e_hbm)]
-        copies = [pltpu.make_async_copy(sources[i], targets[i], sems.at[i]) for i in range(6)]
+        targets = [ids_ref, w_ref, sent_ref] + targets
+        copies = [pltpu.make_async_copy(sources[i], targets[i], sems.at[i]) for i in range(8)]
         for copy in copies:
             copy.start()
-        copies[0].wait()
-        own_sums(l_ref, r_ref, targets[0], og_ref)
-        copies[1].wait()
-        own_sums(l_ref, r_ref, targets[1], ou_ref)
-        for copy in copies[2:]:
+        own_sums(l_ref, r_ref, own_ref, og_ref)
+        for copy in copies[:3]:
             copy.wait()
+        plan_combine(place_ref[0], steps, ids_ref, w_ref, sent_ref, s_ref, c_ref, m_ref, slots, capacity)
+        copies[3].wait()
+        own_sums(l_ref, r_ref, targets[3], ou_ref)
+        for copy in copies[4:]:
+            copy.wait()
 
     return pl.pallas_call(
         kernel,
         out_shape=[jax.ShapeDtypeStruct((rows, units), F32)] * 2
-        + [pltpu.VMEM((depth, units), BF16)] * 4
-        + [pltpu.VMEM((units, depth), BF16)] * 2,
-        in_specs=[SMEM_IN] + [VMEM_IN] * 2 + [HBM_IN] * 4,
-        out_specs=[VMEM_IN] * 8,
-        scratch_shapes=[pltpu.SemaphoreType.DMA((6,))],
-        compiler_params=params(),
-        cost_estimate=cost(8 * rows * part * units, 24 * depth * units),
-    )(place, left, right, *map(in_hbm, (gate, up, down, others_down)))
+        + [pltpu.VMEM((depth, units), BF16)] * 3
+        + [pltpu.VMEM((units, depth), BF16)] * 2
+        + [
+            pltpu.VMEM((steps, 2 * PARTS * picks, sent.shape[1]), BF16),
+            pltpu.VMEM((steps, picks, 128), F32),
+            pltpu.VMEM((steps, 8, 128), jnp.int32),
+        ],
+        in_specs=[SMEM_IN] + [VMEM_IN] * 3 + [HBM_IN] * 7,
+        out_specs=[VMEM_IN] * 10,
+        scratch_shapes=[
+            pltpu.VMEM(ids.shape, jnp.int32),
+            pltpu.VMEM(weights.shape, F32),
+            pltpu.VMEM(sent.shape, jnp.int32),
+            pltpu.SemaphoreType.DMA((8,)),
+        ],
+        compiler_params=params(),
+        cost_estimate=cost(8 * rows * part * units, 22 * depth * units),
+    )(place, left, right, held(own_gate), *map(in_hbm, (gate, up, down, others_down, ids, weights, sent)))
 
 
 def third_quarter(left, gate, up, sum_gate, sum_up):
@@ -387,8 +412,9 @@
     row_keys, sent = jnp.asarray(row_keys, jnp.int32), jnp.asarray(sent, jnp.int32)
     by_route = lambda array: jnp.moveaxis(array[0], 2, 1)
     steps = batches + sections - 1
-    own, gain, row_keys, keys, spread, scales, modes, packed = begin(
-        place, tokens[0], norm_gain, row_keys, by_route(routes), by_route(route_weights), sent, slots, capacity, experts, steps
+    ids, weights = by_route(routes), by_route(route_weights)
+    own, gain, row_keys, keys, packed, gate = begin(
+        place, tokens[0], norm_gain, row_keys, ids, gate_weight, slots, capacity, experts, steps
     )
 
     swap = [(i, i ^ 1) for i in range(devices)]
@@ -410,9 +436,23 @@
         right = unpack(arrived, perm, 1)
         others_right = lax.ppermute(right, "expert", swap)
         if step == 0:
-            sum_gate, sum_up, gate, up, other_gate, other_up, down, other_down = own_half_staging(
-                place, left, right, gate_weight, up_weight, down_weight, others_down
+            results = own_half_staging(
+                place,
+                left,
+                right,
+                gate,
+                gate_weight,
+                up_weight,
+                down_weight,
+                others_down,
+                ids,
+                weights,
+                sent,
+                slots,
+                capacity,
+                steps,
             )
+            sum_gate, sum_up, up, other_gate, other_up, down, other_down, spread, scales, modes = results
         else:
             sum_gate, sum_up = own_half(left, right, gate, up)
         sum_gate, sum_up = third_quarter(others_left, other_gate, other_up, sum_gate, sum_up)

time: 480 us -> 480 us (level)
  no operation moved by 1% of the time
where the time goes in v8:
time: 480 us; the launch traced here: 471 us
  blocking collectives  348 us (72%)
  Pallas kernels  62.5 us (13%)
  waiting for transfers between devices  46.2 us (10%)
  starting transfers between devices  13.1 us (3%)
    all_to_all x7, blocking collectives, per_device(): lax.all_to_all(packed, 'expert', split_axis=0, concat_axis=0, tiled=True)  178 us
    all_to_all x7, blocking collectives, per_device(): lax.all_to_all(partial_value, 'expert', split_axis=0, concat_axis=0, tile...  170 us
    ppermute x6, waiting for transfers between devices, per_device(): hidden = lax.ppermute(current, 'section', pairs)  45 us
    pallas_call x7, Pallas kernels, other_units(): pl.pallas_call(kernel, out_shape=jax.ShapeDtypeStruct((rows * PARTS, widt...  10.3 us
  transfers between devices with their start and end apart: 28, of which 13 were waited for; matrix products, arithmetic and copies ran while one was open for 0% of the time, Pallas kernels for 8%

profile of v8, /device:TPU:1, one launch (start us, length us, event | category | flops | bytes accessed | tf_op | source)
XLA Modules:
  0.0 471.3 jit_solution(3473480820297210923)
XLA Ops:
  0.0 1.4 collective-permute-start.1
  1.6 2.9 shard_map.91
  4.5 27.9 %all_to_all.154 = bf16[32,24,896]{2,1,0:T(8,128)(2,1)S(1)} all-to-all(bf16[32,24,896]{2,1,0:T(8,128)(2,1)S(1)} %bitcast.72), channel_id=1, replica_groups=mesh['section'=4,'expert'=32] {'expert'}, dimensions={0} | all-to-all | bytes 2752512 | tf_op jit(solution)/shard_map/all_to_all | solution.py:433
  33.8 7.6 %shard_map.94 = (f32[192,512]{1,0:T(8,128)S(1)}, f32[192,512]{1,0:T(8,128)S(1)}, bf16[3584,512]{1,0:T(8,128)(2,1)S(1)}, bf16[3584,512]{1,0:T(8,128)(2,1)S(1)}, b...) custom-call(s32[2]{0:T(128)S(1)} %pad_add_fusion.place_ref, ...), custom_call_target="tpu_custom_call" | custom-call | flops 1409286144 | bytes 40370176 | tf_op jit(solution)/shard_map/pallas_call | solution.py:251
  41.5 0.9 shard_map.95
  42.4 0.9 shard_map.96.i_ref
  43.6 1.0 shard_map.97.t_ref
  44.8 1.5 shard_map.98
  46.2 24.3 %all_to_all.155 = bf16[32,24,896]{2,1,0:T(8,128)(2,1)S(1)} all-to-all(bf16[32,24,896]{2,1,0:T(8,128)(2,1)S(1)} %bitcast.66), channel_id=1, replica_groups=mesh['section'=4,'expert'=32] {'expert'}, dimensions={0} | all-to-all | bytes 2752512 | tf_op jit(solution)/shard_map/all_to_all | solution.py:463
  70.5 0.6 shard_map.99
  71.1 1.7 collective-permute-start.4
  72.9 5.7 %collective-permute-done.4.refs_0_.h_ref = bf16[16,7168]{1,0:T(8,128)(2,1)S(1)} collective-permute-done((bf16[16,7168]{1,0:T(8,128)(2,1)S(1)}, bf16[16,7168]{1,0:T(8,128)(2,1)S(1)}, u32[]{:S(2)}, u32[]{:S(2)}) %collective-permute-start.4) | collective-permute-done | bytes 229408 | tf_op jit(solution)/shard_map/ppermute | solution.py:429
  79.1 24.8 %all_to_all.156 = bf16[32,24,896]{2,1,0:T(8,128)(2,1)S(1)} all-to-all(bf16[32,24,896]{2,1,0:T(8,128)(2,1)S(1)} %bitcast.60), channel_id=1, replica_groups=mesh['section'=4,'expert'=32] {'expert'}, dimensions={0} | all-to-all | bytes 2752512 | tf_op jit(solution)/shard_map/all_to_all | solution.py:433
  105.0 0.8 collective-permute-start.5
  105.8 1.6 shard_map.103
  107.4 0.9 shard_map.104
  108.3 0.9 shard_map.105.i_ref
  109.5 1.0 shard_map.106.t_ref
  110.7 1.5 shard_map.107
  112.1 24.3 %all_to_all.157 = bf16[32,24,896]{2,1,0:T(8,128)(2,1)S(1)} all-to-all(bf16[32,24,896]{2,1,0:T(8,128)(2,1)S(1)} %bitcast.67), channel_id=1, replica_groups=mesh['section'=4,'expert'=32] {'expert'}, dimensions={0} | all-to-all | bytes 2752512 | tf_op jit(solution)/shard_map/all_to_all | solution.py:463
  137.1 1.7 collective-permute-start.8
  138.7 7.9 %collective-permute-done.8.refs_0_.h_ref = bf16[16,7168]{1,0:T(8,128)(2,1)S(1)} collective-permute-done((bf16[16,7168]{1,0:T(8,128)(2,1)S(1)}, bf16[16,7168]{1,0:T(8,128)(2,1)S(1)}, u32[]{:S(2)}, u32[]{:S(2)}) %collective-permute-start.8) | collective-permute-done | bytes 229408 | tf_op jit(solution)/shard_map/ppermute | solution.py:429
  147.2 24.5 %all_to_all.158 = bf16[32,24,896]{2,1,0:T(8,128)(2,1)S(1)} all-to-all(bf16[32,24,896]{2,1,0:T(8,128)(2,1)S(1)} %bitcast.61), channel_id=1, replica_groups=mesh['section'=4,'expert'=32] {'expert'}, dimensions={0} | all-to-all | bytes 2752512 | tf_op jit(solution)/shard_map/all_to_all | solution.py:433
  173.1 1.6 shard_map.112
  174.7 0.9 shard_map.113
  175.6 0.9 shard_map.114.i_ref
  177.0 1.0 shard_map.115.t_ref
  178.2 1.5 shard_map.116
  179.7 24.3 %all_to_all.159 = bf16[32,24,896]{2,1,0:T(8,128)(2,1)S(1)} all-to-all(bf16[32,24,896]{2,1,0:T(8,128)(2,1)S(1)} %bitcast.68), channel_id=1, replica_groups=mesh['section'=4,'expert'=32] {'expert'}, dimensions={0} | all-to-all | bytes 2752512 | tf_op jit(solution)/shard_map/all_to_all | solution.py:463
  204.0 0.6 shard_map.117
  204.6 8.1 %collective-permute-done.12.refs_0_.h_ref = bf16[16,7168]{1,0:T(8,128)(2,1)S(1)} collective-permute-done((bf16[16,7168]{1,0:T(8,128)(2,1)S(1)}, bf16[16,7168]{1,0:T(8,128)(2,1)S(1)}, u32[]{:S(2)}, u32[]{:S(2)}) %collective-permute-start.12) | collective-permute-done | bytes 229408 | tf_op jit(solution)/shard_map/ppermute | solution.py:429
  213.3 25.2 %all_to_all.160 = bf16[32,24,896]{2,1,0:T(8,128)(2,1)S(1)} all-to-all(bf16[32,24,896]{2,1,0:T(8,128)(2,1)S(1)} %bitcast.62), channel_id=1, replica_groups=mesh['section'=4,'expert'=32] {'expert'}, dimensions={0} | all-to-all | bytes 2752512 | tf_op jit(solution)/shard_map/all_to_all | solution.py:433
  239.9 1.6 shard_map.121
  241.5 0.9 shard_map.122
  242.4 0.9 shard_map.123.i_ref
  243.6 1.0 shard_map.124.t_ref
  244.8 1.5 shard_map.125
  246.3 24.3 %all_to_all.161 = bf16[32,24,896]{2,1,0:T(8,128)(2,1)S(1)} all-to-all(bf16[32,24,896]{2,1,0:T(8,128)(2,1)S(1)} %bitcast.69), channel_id=1, replica_groups=mesh['section'=4,'expert'=32] {'expert'}, dimensions={0} | all-to-all | bytes 2752512 | tf_op jit(solution)/shard_map/all_to_all | solution.py:463
  271.2 8.1 %collective-permute-done.16.refs_0_.h_ref.t_ref = bf16[16,7168]{1,0:T(8,128)(2,1)S(1)} collective-permute-done((bf16[16,7168]{1,0:T(8,128)(2,1)S(1)}, bf16[16,7168]{1,0:T(8,128)(2,1)S(1)}, u32[]{:S(2)}, u32[]{:S(2)}) %collective-permute-start.16) | collective-permute-done | bytes 229408 | tf_op jit(solution)/shard_map/ppermute | solution.py:429
  279.9 25.3 %all_to_all.162 = bf16[32,24,896]{2,1,0:T(8,128)(2,1)S(1)} all-to-all(bf16[32,24,896]{2,1,0:T(8,128)(2,1)S(1)} %bitcast.63), channel_id=1, replica_groups=mesh['section'=4,'expert'=32] {'expert'}, dimensions={0} | all-to-all | bytes 2752512 | tf_op jit(solution)/shard_map/all_to_all | solution.py:433
  306.6 1.6 shard_map.130
  308.2 0.9 shard_map.131
  309.1 0.9 shard_map.132.i_ref
  310.4 1.0 shard_map.133.t_ref
  311.6 1.5 shard_map.134
  313.0 24.3 %all_to_all.163 = bf16[32,24,896]{2,1,0:T(8,128)(2,1)S(1)} all-to-all(bf16[32,24,896]{2,1,0:T(8,128)(2,1)S(1)} %bitcast.70), channel_id=1, replica_groups=mesh['section'=4,'expert'=32] {'expert'}, dimensions={0} | all-to-all | bytes 2752512 | tf_op jit(solution)/shard_map/all_to_all | solution.py:463
  337.4 0.6 shard_map.135
  338.0 8.1 %collective-permute-done.20.refs_0_.h_ref = bf16[16,7168]{1,0:T(8,128)(2,1)S(1)} collective-permute-done((bf16[16,7168]{1,0:T(8,128)(2,1)S(1)}, bf16[16,7168]{1,0:T(8,128)(2,1)S(1)}, u32[]{:S(2)}, u32[]{:S(2)}) %collective-permute-start.20) | collective-permute-done | bytes 229408 | tf_op jit(solution)/shard_map/ppermute | solution.py:429
  346.7 25.2 %all_to_all.164 = bf16[32,24,896]{2,1,0:T(8,128)(2,1)S(1)} all-to-all(bf16[32,24,896]{2,1,0:T(8,128)(2,1)S(1)} %bitcast.64), channel_id=1, replica_groups=mesh['section'=4,'expert'=32] {'expert'}, dimensions={0} | all-to-all | bytes 2752512 | tf_op jit(solution)/shard_map/all_to_all | solution.py:433
  373.3 1.6 shard_map.139
  374.9 0.9 shard_map.140
  375.8 0.9 shard_map.141.i_ref
  377.2 1.0 shard_map.142.t_ref
  378.4 1.5 shard_map.143
  379.9 24.3 %all_to_all.165 = bf16[32,24,896]{2,1,0:T(8,128)(2,1)S(1)} all-to-all(bf16[32,24,896]{2,1,0:T(8,128)(2,1)S(1)} %bitcast.71), channel_id=1, replica_groups=mesh['section'=4,'expert'=32] {'expert'}, dimensions={0} | all-to-all | bytes 2752512 | tf_op jit(solution)/shard_map/all_to_all | solution.py:463
  404.9 6.9 %collective-permute-done.24.refs_0_.h_ref = bf16[16,7168]{1,0:T(8,128)(2,1)S(1)} collective-permute-done((bf16[16,7168]{1,0:T(8,128)(2,1)S(1)}, bf16[16,7168]{1,0:T(8,128)(2,1)S(1)}, u32[]{:S(2)}, u32[]{:S(2)}) %collective-permute-start.24) | collective-permute-done | bytes 229408 | tf_op jit(solution)/shard_map/ppermute | solution.py:429
  412.4 25.2 %all_to_all.166 = bf16[32,24,896]{2,1,0:T(8,128)(2,1)S(1)} all-to-all(bf16[32,24,896]{2,1,0:T(8,128)(2,1)S(1)} %bitcast.54), channel_id=1, replica_groups=mesh['section'=4,'expert'=32] {'expert'}, dimensions={0} | all-to-all | bytes 2752512 | tf_op jit(solution)/shard_map/all_to_all | solution.py:433
  438.9 1.6 shard_map.148
  440.5 0.9 shard_map.149
  441.4 0.9 shard_map.150.i_ref
  442.7 1.0 shard_map.151.t_ref
  443.8 1.5 shard_map.152
  445.3 24.3 %all_to_all.167 = bf16[32,24,896]{2,1,0:T(8,128)(2,1)S(1)} all-to-all(bf16[32,24,896]{2,1,0:T(8,128)(2,1)S(1)} %bitcast.65), channel_id=1, replica_groups=mesh['section'=4,'expert'=32] {'expert'}, dimensions={0} | all-to-all | bytes 2752512 | tf_op jit(solution)/shard_map/all_to_all | solution.py:463
  469.6 1.3 shard_map.153
  (72 shorter events, 18.8 us)
Async XLA Ops:
  0.0 33.8 %collective-permute-start.1 = (bf16[1,512,7168]{2,1,0:T(8,128)(2,1)}, bf16[1,512,7168]{2,1,0:T(8,128)(2,1)}, u32[]{:S(2)}, u32[]{:S(2)}) collective-permute-start(bf16[1,512,7168]{2,1,0:T(8,128)(2,1)} %d_hbm.1), channel_id=1, source_target_pairs={{0,1},{1,0},{2,3},{3,2},{4,5},{5,4},{6,7},{7,6},{8,9},{9,8},{10,11... | collective-permute-start | bytes 22020104 | tf_op jit(solution)/shard_map/ppermute | solution.py:421
  32.8 8.7 %collective-permute-start.2 = (bf16[192,1792]{1,0:T(8,128)(2,1)S(1)}, bf16[192,1792]{1,0:T(8,128)(2,1)S(1)}, u32[]{:S(2)}, u32[]{:S(2)}) collective-permute-start(bf16[192,1792]{1,0:T(8,128)(2,1)S(1)} %shard_map.93.l_ref), channel_id=1, source_target_pairs={{0,1},{1,0},{2,3},{3,2},{4,5},{5,4},{6,7},{7,6},{8,9},{9,8},{10,11... | collective-permute-start | bytes 2064392 | tf_op jit(solution)/shard_map/ppermute | solution.py:435
  33.5 8.8 %collective-permute-start = (bf16[192,1792]{1,0:T(8,128)(2,1)S(1)}, bf16[192,1792]{1,0:T(8,128)(2,1)S(1)}, u32[]{:S(2)}, u32[]{:S(2)}) collective-permute-start(bf16[192,1792]{1,0:T(8,128)(2,1)S(1)} %shard_map.92.r_ref), channel_id=1, source_target_pairs={{0,1},{1,0},{2,3},{3,2},{4,5},{5,4},{6,7},{7,6},{8,9},{9,8},{10,11... | collective-permute-start | bytes 2064392 | tf_op jit(solution)/shard_map/ppermute | solution.py:437
  43.2 1.5 collective-permute-start.3
  71.1 7.4 %collective-permute-start.4 = (bf16[16,7168]{1,0:T(8,128)(2,1)S(1)}, bf16[16,7168]{1,0:T(8,128)(2,1)S(1)}, u32[]{:S(2)}, u32[]{:S(2)}) collective-permute-start(bf16[16,7168]{1,0:T(8,128)(2,1)S(1)} %shard_map.99), channel_id=1, source_target_pairs={{0,32},{32,0},{64,96},{96,64},{1,33},{33,1},{65,97},{97,65},{2,34}... | collective-permute-start | bytes 688136 | tf_op jit(solution)/shard_map/ppermute | solution.py:429
  104.3 3.1 collective-permute-start.6
  105.0 3.3 collective-permute-start.5
  109.2 1.5 collective-permute-start.7
  137.1 9.6 %collective-permute-start.8 = (bf16[16,7168]{1,0:T(8,128)(2,1)S(1)}, bf16[16,7168]{1,0:T(8,128)(2,1)S(1)}, u32[]{:S(2)}, u32[]{:S(2)}) collective-permute-start(bf16[16,7168]{1,0:T(8,128)(2,1)S(1)} %shard_map.108), channel_id=1, source_target_pairs={{0,32},{32,64},{64,96},{96,0},{1,33},{33,65},{65,97},{97,1},{2,34}... | collective-permute-start | bytes 688136 | tf_op jit(solution)/shard_map/ppermute | solution.py:429
  172.1 2.6 collective-permute-start.10
  172.8 2.8 collective-permute-start.9
  176.5 1.7 collective-permute-start.11
  204.6 8.2 %collective-permute-start.12 = (bf16[16,7168]{1,0:T(8,128)(2,1)S(1)}, bf16[16,7168]{1,0:T(8,128)(2,1)S(1)}, u32[]{:S(2)}, u32[]{:S(2)}) collective-permute-start(bf16[16,7168]{1,0:T(8,128)(2,1)S(1)} %shard_map.117), channel_id=1, source_target_pairs={{0,32},{32,64},{64,96},{96,0},{1,33},{33,65},{65,97},{97,1},{2,34}... | collective-permute-start | bytes 688136 | tf_op jit(solution)/shard_map/ppermute | solution.py:429
  238.8 2.6 collective-permute-start.14
  239.5 2.8 collective-permute-start.13
  243.3 1.5 collective-permute-start.15
  271.2 8.2 %collective-permute-start.16 = (bf16[16,7168]{1,0:T(8,128)(2,1)S(1)}, bf16[16,7168]{1,0:T(8,128)(2,1)S(1)}, u32[]{:S(2)}, u32[]{:S(2)}) collective-permute-start(bf16[16,7168]{1,0:T(8,128)(2,1)S(1)} %shard_map.126), channel_id=1, source_target_pairs={{0,32},{32,64},{64,96},{96,0},{1,33},{33,65},{65,97},{97,1},{2,34}... | collective-permute-start | bytes 688136 | tf_op jit(solution)/shard_map/ppermute | solution.py:429
  305.6 2.6 collective-permute-start.18
  306.4 2.8 collective-permute-start.17
  310.0 1.5 collective-permute-start.19
  338.0 8.2 %collective-permute-start.20 = (bf16[16,7168]{1,0:T(8,128)(2,1)S(1)}, bf16[16,7168]{1,0:T(8,128)(2,1)S(1)}, u32[]{:S(2)}, u32[]{:S(2)}) collective-permute-start(bf16[16,7168]{1,0:T(8,128)(2,1)S(1)} %shard_map.135), channel_id=1, source_target_pairs={{0,32},{32,64},{64,96},{96,0},{1,33},{33,65},{65,97},{97,1},{2,34}... | collective-permute-start | bytes 688136 | tf_op jit(solution)/shard_map/ppermute | solution.py:429
  372.2 2.6 collective-permute-start.22
  372.9 2.8 collective-permute-start.21
  376.7 1.8 collective-permute-start.23
  404.8 7.0 %collective-permute-start.24 = (bf16[16,7168]{1,0:T(8,128)(2,1)S(1)}, bf16[16,7168]{1,0:T(8,128)(2,1)S(1)}, u32[]{:S(2)}, u32[]{:S(2)}) collective-permute-start(bf16[16,7168]{1,0:T(8,128)(2,1)S(1)} %shard_map.144), channel_id=1, source_target_pairs={{0,32},{32,0},{64,96},{96,64},{1,33},{33,1},{65,97},{97,65},{2,34}... | collective-permute-start | bytes 688136 | tf_op jit(solution)/shard_map/ppermute | solution.py:429
  437.9 2.6 collective-permute-start.26
  438.6 2.8 collective-permute-start.25
  442.3 1.5 collective-permute-start.27

commit v9 on v8

--- a/solution.py
+++ b/solution.py
@@ -119,18 +119,16 @@
     return own, other
 
 
-def begin(place, tokens, gain, row_keys, ids, gate, slots, capacity, experts, steps):
+def begin(place, tokens, gain, row_keys, ids, slots, capacity, experts, steps):
     routes_each = ids.shape[1]
     rows, lanes = row_keys.shape
     full = tokens.shape[1]
 
     def kernel(place_ref, *refs):
-        sources, gate_hbm, rest = refs[:4], refs[4], refs[5:]
-        h_ref, g_ref, r_ref, k_ref, o_ref, gate_ref, ids_ref, sems = rest
-        own, _ = halves(place_ref[1], full // 2)
-        sources += (gate_hbm.at[0, own, :],)
-        targets = (h_ref, g_ref, r_ref, ids_ref, gate_ref)
-        copies = [pltpu.make_async_copy(sources[i], targets[i], sems.at[i]) for i in range(5)]
+        sources, rest = refs[:4], refs[4:]
+        h_ref, g_ref, r_ref, k_ref, o_ref, ids_ref, sems = rest
+        targets = (h_ref, g_ref, r_ref, ids_ref)
+        copies = [pltpu.make_async_copy(sources[i], targets[i], sems.at[i]) for i in range(4)]
         for copy in copies:
             copy.start()
         copies[3].wait()
@@ -138,9 +136,8 @@
         for copy in copies[:3]:
             copy.wait()
         pack(0, h_ref, g_ref, k_ref, r_ref, o_ref, experts)
-        copies[4].wait()
-
-    sources = (tokens, gain, row_keys, ids, gate)
+
+    sources = (tokens, gain, row_keys, ids)
     return pl.pallas_call(
         kernel,
         out_shape=[
@@ -149,11 +146,10 @@
             pltpu.VMEM(row_keys.shape, jnp.int32),
             pltpu.VMEM((steps, routes_each, lanes), jnp.int32),
             jax.ShapeDtypeStruct((2 * rows, full // (2 * PARTS)), BF16),
-            pltpu.VMEM((full // 2, gate.shape[2]), BF16),
         ],
-        in_specs=[SMEM_IN] + [HBM_IN] * 5,
-        out_specs=[VMEM_IN] * 6,
-        scratch_shapes=[pltpu.VMEM(ids.shape, jnp.int32), pltpu.SemaphoreType.DMA((5,))],
+        in_specs=[SMEM_IN] + [HBM_IN] * 4,
+        out_specs=[VMEM_IN] * 5,
+        scratch_shapes=[pltpu.VMEM(ids.shape, jnp.int32), pltpu.SemaphoreType.DMA((4,))],
         compiler_params=params(),
     )(place, *[in_hbm(array) for array in sources])
 
@@ -224,51 +220,51 @@
     o_ref[...] = mm(l_ref[...], w_ref[:part, :]) + mm(r_ref[...], w_ref[part:, :])
 
 
-def own_half_staging(place, left, right, own_gate, gate, up, down, others_down, ids, weights, sent, slots, capacity, steps):
+def own_half_staging(place, left, right, gate, up, down, others_down, ids, weights, sent, slots, capacity, steps):
     rows, part = left.shape
     depth, units = 2 * part, gate.shape[2]
     picks = ids.shape[1] * ids.shape[2]
 
-    def kernel(place_ref, l_ref, r_ref, own_ref, g_hbm, u_hbm, d_hbm, e_hbm, ids_hbm, w_hbm, sent_hbm, *rest):
+    def kernel(place_ref, l_ref, r_ref, g_hbm, u_hbm, d_hbm, e_hbm, ids_hbm, w_hbm, sent_hbm, *rest):
         og_ref, ou_ref, *targets, s_ref, c_ref, m_ref, ids_ref, w_ref, sent_ref, sems = rest
         own, other = halves(place_ref[1], depth)
         sources = [ids_hbm, w_hbm, sent_hbm]
-        sources += [u_hbm.at[0, own, :], g_hbm.at[0, other, :], u_hbm.at[0, other, :]]
+        sources += [hbm.at[0, half, :] for half in (own, other) for hbm in (g_hbm, u_hbm)]
         sources += [hbm.at[0, :, own] for hbm in (d_hbm, e_hbm)]
         targets = [ids_ref, w_ref, sent_ref] + targets
-        copies = [pltpu.make_async_copy(sources[i], targets[i], sems.at[i]) for i in range(8)]
+        copies = [pltpu.make_async_copy(sources[i], targets[i], sems.at[i]) for i in range(9)]
         for copy in copies:
             copy.start()
-        own_sums(l_ref, r_ref, own_ref, og_ref)
         for copy in copies[:3]:
             copy.wait()
         plan_combine(place_ref[0], steps, ids_ref, w_ref, sent_ref, s_ref, c_ref, m_ref, slots, capacity)
-        copies[3].wait()
-        own_sums(l_ref, r_ref, targets[3], ou_ref)
-        for copy in copies[4:]:
+        for copy, target, sums in zip(copies[3:5], targets[3:5], (og_ref, ou_ref)):
             copy.wait()
+            own_sums(l_ref, r_ref, target, sums)
+        for copy in copies[5:]:
+            copy.wait()
 
     return pl.pallas_call(
         kernel,
         out_shape=[jax.ShapeDtypeStruct((rows, units), F32)] * 2
-        + [pltpu.VMEM((depth, units), BF16)] * 3
+        + [pltpu.VMEM((depth, units), BF16)] * 4
         + [pltpu.VMEM((units, depth), BF16)] * 2
         + [
             pltpu.VMEM((steps, 2 * PARTS * picks, sent.shape[1]), BF16),
             pltpu.VMEM((steps, picks, 128), F32),
             pltpu.VMEM((steps, 8, 128), jnp.int32),
         ],
-        in_specs=[SMEM_IN] + [VMEM_IN] * 3 + [HBM_IN] * 7,
-        out_specs=[VMEM_IN] * 10,
+        in_specs=[SMEM_IN] + [VMEM_IN] * 2 + [HBM_IN] * 7,
+        out_specs=[VMEM_IN] * 11,
         scratch_shapes=[
             pltpu.VMEM(ids.shape, jnp.int32),
             pltpu.VMEM(weights.shape, F32),
             pltpu.VMEM(sent.shape, jnp.int32),
-            pltpu.SemaphoreType.DMA((8,)),
+            pltpu.SemaphoreType.DMA((9,)),
         ],
         compiler_params=params(),
         cost_estimate=cost(8 * rows * part * units, 22 * depth * units),
-    )(place, left, right, held(own_gate), *map(in_hbm, (gate, up, down, others_down, ids, weights, sent)))
+    )(place, left, right, *map(in_hbm, (gate, up, down, others_down, ids, weights, sent)))
 
 
 def third_quarter(left, gate, up, sum_gate, sum_up):
@@ -413,8 +409,8 @@
     by_route = lambda array: jnp.moveaxis(array[0], 2, 1)
     steps = batches + sections - 1
     ids, weights = by_route(routes), by_route(route_weights)
-    own, gain, row_keys, keys, packed, gate = begin(
-        place, tokens[0], norm_gain, row_keys, ids, gate_weight, slots, capacity, experts, steps
+    own, gain, row_keys, keys, packed = begin(
+        place, tokens[0], norm_gain, row_keys, ids, slots, capacity, experts, steps
     )
 
     swap = [(i, i ^ 1) for i in range(devices)]
@@ -440,7 +436,6 @@
                 place,
                 left,
                 right,
-                gate,
                 gate_weight,
                 up_weight,
                 down_weight,
@@ -452,7 +447,7 @@
                 capacity,
                 steps,
             )
-            sum_gate, sum_up, up, other_gate, other_up, down, other_down, spread, scales, modes = results
+            sum_gate, sum_up, gate, up, other_gate, other_up, down, other_down, spread, scales, modes = results
         else:
             sum_gate, sum_up = own_half(left, right, gate, up)
         sum_gate, sum_up = third_quarter(others_left, other_gate, other_up, sum_gate, sum_up)

time: 480 us -> 480 us (level)
  no operation moved by 1% of the time
where the time goes in v9:
time: 480 us; the launch traced here: 472 us
  blocking collectives  348 us (72%)
  Pallas kernels  62.8 us (13%)
  waiting for transfers between devices  46.2 us (10%)
  starting transfers between devices  13.1 us (3%)
    all_to_all x7, blocking collectives, per_device(): lax.all_to_all(packed, 'expert', split_axis=0, concat_axis=0, tiled=True)  178 us
    all_to_all x7, blocking collectives, per_device(): lax.all_to_all(partial_value, 'expert', split_axis=0, concat_axis=0, tile...  170 us
    ppermute x6, waiting for transfers between devices, per_device(): hidden = lax.ppermute(current, 'section', pairs)  45 us
    pallas_call x7, Pallas kernels, other_units(): pl.pallas_call(kernel, out_shape=jax.ShapeDtypeStruct((rows * PARTS, widt...  10.6 us
  transfers between devices with their start and end apart: 28, of which 13 were waited for; matrix products, arithmetic and copies ran while one was open for 0% of the time, Pallas kernels for 8%

profile of v9, /device:TPU:1, one launch (start us, length us, event | category | flops | bytes accessed | tf_op | source)
XLA Modules:
  0.0 471.7 jit_solution(15126365843612350394)
XLA Ops:
  0.0 1.4 collective-permute-start.1
  1.6 2.3 shard_map.91
  3.9 27.9 %all_to_all.154 = bf16[32,24,896]{2,1,0:T(8,128)(2,1)S(1)} all-to-all(bf16[32,24,896]{2,1,0:T(8,128)(2,1)S(1)} %bitcast.72), channel_id=1, replica_groups=mesh['section'=4,'expert'=32] {'expert'}, dimensions={0} | all-to-all | bytes 2752512 | tf_op jit(solution)/shard_map/all_to_all | solution.py:429
  33.2 8.0 %shard_map.94 = (f32[192,512]{1,0:T(8,128)S(1)}, f32[192,512]{1,0:T(8,128)S(1)}, bf16[3584,512]{1,0:T(8,128)(2,1)S(1)}, bf16[3584,512]{1,0:T(8,128)(2,1)S(1)}, b...) custom-call(s32[2]{0:T(128)S(1)} %pad_add_fusion.place_ref, ...), custom_call_target="tpu_custom_call" | custom-call | flops 1409286144 | bytes 40370176 | tf_op jit(solution)/shard_map/pallas_call | solution.py:247
  41.2 0.9 shard_map.95
  42.1 0.9 shard_map.96.i_ref
  43.4 1.0 shard_map.97.t_ref
  44.5 1.5 shard_map.98
  46.1 24.3 %all_to_all.155 = bf16[32,24,896]{2,1,0:T(8,128)(2,1)S(1)} all-to-all(bf16[32,24,896]{2,1,0:T(8,128)(2,1)S(1)} %bitcast.66), channel_id=1, replica_groups=mesh['section'=4,'expert'=32] {'expert'}, dimensions={0} | all-to-all | bytes 2752512 | tf_op jit(solution)/shard_map/all_to_all | solution.py:458
  70.4 0.6 shard_map.99
  71.0 1.7 collective-permute-start.4
  72.7 5.7 %collective-permute-done.4.refs_0_.h_ref = bf16[16,7168]{1,0:T(8,128)(2,1)S(1)} collective-permute-done((bf16[16,7168]{1,0:T(8,128)(2,1)S(1)}, bf16[16,7168]{1,0:T(8,128)(2,1)S(1)}, u32[]{:S(2)}, u32[]{:S(2)}) %collective-permute-start.4) | collective-permute-done | bytes 229408 | tf_op jit(solution)/shard_map/ppermute | solution.py:425
  78.9 24.9 %all_to_all.156 = bf16[32,24,896]{2,1,0:T(8,128)(2,1)S(1)} all-to-all(bf16[32,24,896]{2,1,0:T(8,128)(2,1)S(1)} %bitcast.60), channel_id=1, replica_groups=mesh['section'=4,'expert'=32] {'expert'}, dimensions={0} | all-to-all | bytes 2752512 | tf_op jit(solution)/shard_map/all_to_all | solution.py:429
  104.8 0.8 collective-permute-start.5
  105.6 1.6 shard_map.103
  107.2 0.9 shard_map.104
  108.1 0.9 shard_map.105.i_ref
  109.4 1.0 shard_map.106.t_ref
  110.6 1.5 shard_map.107
  112.1 24.3 %all_to_all.157 = bf16[32,24,896]{2,1,0:T(8,128)(2,1)S(1)} all-to-all(bf16[32,24,896]{2,1,0:T(8,128)(2,1)S(1)} %bitcast.67), channel_id=1, replica_groups=mesh['section'=4,'expert'=32] {'expert'}, dimensions={0} | all-to-all | bytes 2752512 | tf_op jit(solution)/shard_map/all_to_all | solution.py:458
  137.0 1.6 collective-permute-start.8
  138.7 7.9 %collective-permute-done.8.refs_0_.h_ref = bf16[16,7168]{1,0:T(8,128)(2,1)S(1)} collective-permute-done((bf16[16,7168]{1,0:T(8,128)(2,1)S(1)}, bf16[16,7168]{1,0:T(8,128)(2,1)S(1)}, u32[]{:S(2)}, u32[]{:S(2)}) %collective-permute-start.8) | collective-permute-done | bytes 229408 | tf_op jit(solution)/shard_map/ppermute | solution.py:425
  147.1 24.5 %all_to_all.158 = bf16[32,24,896]{2,1,0:T(8,128)(2,1)S(1)} all-to-all(bf16[32,24,896]{2,1,0:T(8,128)(2,1)S(1)} %bitcast.61), channel_id=1, replica_groups=mesh['section'=4,'expert'=32] {'expert'}, dimensions={0} | all-to-all | bytes 2752512 | tf_op jit(solution)/shard_map/all_to_all | solution.py:429
  173.0 1.6 shard_map.112
  174.6 0.9 shard_map.113
  175.6 0.9 shard_map.114.i_ref
  177.0 1.0 shard_map.115.t_ref
  178.1 1.5 shard_map.116
  179.7 24.3 %all_to_all.159 = bf16[32,24,896]{2,1,0:T(8,128)(2,1)S(1)} all-to-all(bf16[32,24,896]{2,1,0:T(8,128)(2,1)S(1)} %bitcast.68), channel_id=1, replica_groups=mesh['section'=4,'expert'=32] {'expert'}, dimensions={0} | all-to-all | bytes 2752512 | tf_op jit(solution)/shard_map/all_to_all | solution.py:458
  204.0 0.6 shard_map.117
  204.7 8.1 %collective-permute-done.12.refs_0_.h_ref = bf16[16,7168]{1,0:T(8,128)(2,1)S(1)} collective-permute-done((bf16[16,7168]{1,0:T(8,128)(2,1)S(1)}, bf16[16,7168]{1,0:T(8,128)(2,1)S(1)}, u32[]{:S(2)}, u32[]{:S(2)}) %collective-permute-start.12) | collective-permute-done | bytes 229408 | tf_op jit(solution)/shard_map/ppermute | solution.py:425
  213.3 25.2 %all_to_all.160 = bf16[32,24,896]{2,1,0:T(8,128)(2,1)S(1)} all-to-all(bf16[32,24,896]{2,1,0:T(8,128)(2,1)S(1)} %bitcast.62), channel_id=1, replica_groups=mesh['section'=4,'expert'=32] {'expert'}, dimensions={0} | all-to-all | bytes 2752512 | tf_op jit(solution)/shard_map/all_to_all | solution.py:429
  239.9 1.6 shard_map.121
  241.5 0.9 shard_map.122
  242.4 0.9 shard_map.123.i_ref
  243.7 1.0 shard_map.124.t_ref
  244.8 1.5 shard_map.125
  246.4 24.3 %all_to_all.161 = bf16[32,24,896]{2,1,0:T(8,128)(2,1)S(1)} all-to-all(bf16[32,24,896]{2,1,0:T(8,128)(2,1)S(1)} %bitcast.69), channel_id=1, replica_groups=mesh['section'=4,'expert'=32] {'expert'}, dimensions={0} | all-to-all | bytes 2752512 | tf_op jit(solution)/shard_map/all_to_all | solution.py:458
  271.4 8.1 %collective-permute-done.16.refs_0_.h_ref.t_ref = bf16[16,7168]{1,0:T(8,128)(2,1)S(1)} collective-permute-done((bf16[16,7168]{1,0:T(8,128)(2,1)S(1)}, bf16[16,7168]{1,0:T(8,128)(2,1)S(1)}, u32[]{:S(2)}, u32[]{:S(2)}) %collective-permute-start.16) | collective-permute-done | bytes 229408 | tf_op jit(solution)/shard_map/ppermute | solution.py:425
  280.0 25.3 %all_to_all.162 = bf16[32,24,896]{2,1,0:T(8,128)(2,1)S(1)} all-to-all(bf16[32,24,896]{2,1,0:T(8,128)(2,1)S(1)} %bitcast.63), channel_id=1, replica_groups=mesh['section'=4,'expert'=32] {'expert'}, dimensions={0} | all-to-all | bytes 2752512 | tf_op jit(solution)/shard_map/all_to_all | solution.py:429
  306.8 1.6 shard_map.130
  308.4 0.9 shard_map.131
  309.3 0.9 shard_map.132.i_ref
  310.6 1.0 shard_map.133.t_ref
  311.7 1.5 shard_map.134
  313.2 24.3 %all_to_all.163 = bf16[32,24,896]{2,1,0:T(8,128)(2,1)S(1)} all-to-all(bf16[32,24,896]{2,1,0:T(8,128)(2,1)S(1)} %bitcast.70), channel_id=1, replica_groups=mesh['section'=4,'expert'=32] {'expert'}, dimensions={0} | all-to-all | bytes 2752512 | tf_op jit(solution)/shard_map/all_to_all | solution.py:458
  337.5 0.6 shard_map.135
  338.2 8.1 %collective-permute-done.20.refs_0_.h_ref = bf16[16,7168]{1,0:T(8,128)(2,1)S(1)} collective-permute-done((bf16[16,7168]{1,0:T(8,128)(2,1)S(1)}, bf16[16,7168]{1,0:T(8,128)(2,1)S(1)}, u32[]{:S(2)}, u32[]{:S(2)}) %collective-permute-start.20) | collective-permute-done | bytes 229408 | tf_op jit(solution)/shard_map/ppermute | solution.py:425
  346.9 25.2 %all_to_all.164 = bf16[32,24,896]{2,1,0:T(8,128)(2,1)S(1)} all-to-all(bf16[32,24,896]{2,1,0:T(8,128)(2,1)S(1)} %bitcast.64), channel_id=1, replica_groups=mesh['section'=4,'expert'=32] {'expert'}, dimensions={0} | all-to-all | bytes 2752512 | tf_op jit(solution)/shard_map/all_to_all | solution.py:429
  373.4 1.6 shard_map.139
  375.0 0.9 shard_map.140
  376.0 0.9 shard_map.141.i_ref
  377.4 1.0 shard_map.142.t_ref
  378.6 1.5 shard_map.143
  380.2 24.3 %all_to_all.165 = bf16[32,24,896]{2,1,0:T(8,128)(2,1)S(1)} all-to-all(bf16[32,24,896]{2,1,0:T(8,128)(2,1)S(1)} %bitcast.71), channel_id=1, replica_groups=mesh['section'=4,'expert'=32] {'expert'}, dimensions={0} | all-to-all | bytes 2752512 | tf_op jit(solution)/shard_map/all_to_all | solution.py:458
  405.2 6.9 %collective-permute-done.24.refs_0_.h_ref = bf16[16,7168]{1,0:T(8,128)(2,1)S(1)} collective-permute-done((bf16[16,7168]{1,0:T(8,128)(2,1)S(1)}, bf16[16,7168]{1,0:T(8,128)(2,1)S(1)}, u32[]{:S(2)}, u32[]{:S(2)}) %collective-permute-start.24) | collective-permute-done | bytes 229408 | tf_op jit(solution)/shard_map/ppermute | solution.py:425
  412.6 25.2 %all_to_all.166 = bf16[32,24,896]{2,1,0:T(8,128)(2,1)S(1)} all-to-all(bf16[32,24,896]{2,1,0:T(8,128)(2,1)S(1)} %bitcast.54), channel_id=1, replica_groups=mesh['section'=4,'expert'=32] {'expert'}, dimensions={0} | all-to-all | bytes 2752512 | tf_op jit(solution)/shard_map/all_to_all | solution.py:429
  439.2 1.6 shard_map.148
  440.8 0.9 shard_map.149
  441.7 0.9 shard_map.150.i_ref
  442.9 1.0 shard_map.151.t_ref
  444.1 1.5 shard_map.152
  445.7 24.3 %all_to_all.167 = bf16[32,24,896]{2,1,0:T(8,128)(2,1)S(1)} all-to-all(bf16[32,24,896]{2,1,0:T(8,128)(2,1)S(1)} %bitcast.65), channel_id=1, replica_groups=mesh['section'=4,'expert'=32] {'expert'}, dimensions={0} | all-to-all | bytes 2752512 | tf_op jit(solution)/shard_map/all_to_all | solution.py:458
  470.0 1.3 shard_map.153
  (72 shorter events, 18.9 us)
Async XLA Ops:
  0.0 33.2 %collective-permute-start.1 = (bf16[1,512,7168]{2,1,0:T(8,128)(2,1)}, bf16[1,512,7168]{2,1,0:T(8,128)(2,1)}, u32[]{:S(2)}, u32[]{:S(2)}) collective-permute-start(bf16[1,512,7168]{2,1,0:T(8,128)(2,1)} %d_hbm.1), channel_id=1, source_target_pairs={{0,1},{1,0},{2,3},{3,2},{4,5},{5,4},{6,7},{7,6},{8,9},{9,8},{10,11... | collective-permute-start | bytes 22020104 | tf_op jit(solution)/shard_map/ppermute | solution.py:417
  32.2 9.1 %collective-permute-start.2 = (bf16[192,1792]{1,0:T(8,128)(2,1)S(1)}, bf16[192,1792]{1,0:T(8,128)(2,1)S(1)}, u32[]{:S(2)}, u32[]{:S(2)}) collective-permute-start(bf16[192,1792]{1,0:T(8,128)(2,1)S(1)} %shard_map.93.l_ref), channel_id=1, source_target_pairs={{0,1},{1,0},{2,3},{3,2},{4,5},{5,4},{6,7},{7,6},{8,9},{9,8},{10,11... | collective-permute-start | bytes 2064392 | tf_op jit(solution)/shard_map/ppermute | solution.py:431
  32.9 9.2 %collective-permute-start = (bf16[192,1792]{1,0:T(8,128)(2,1)S(1)}, bf16[192,1792]{1,0:T(8,128)(2,1)S(1)}, u32[]{:S(2)}, u32[]{:S(2)}) collective-permute-start(bf16[192,1792]{1,0:T(8,128)(2,1)S(1)} %shard_map.92.r_ref), channel_id=1, source_target_pairs={{0,1},{1,0},{2,3},{3,2},{4,5},{5,4},{6,7},{7,6},{8,9},{9,8},{10,11... | collective-permute-start | bytes 2064392 | tf_op jit(solution)/shard_map/ppermute | solution.py:433
  43.0 1.5 collective-permute-start.3
  71.0 7.4 %collective-permute-start.4 = (bf16[16,7168]{1,0:T(8,128)(2,1)S(1)}, bf16[16,7168]{1,0:T(8,128)(2,1)S(1)}, u32[]{:S(2)}, u32[]{:S(2)}) collective-permute-start(bf16[16,7168]{1,0:T(8,128)(2,1)S(1)} %shard_map.99), channel_id=1, source_target_pairs={{0,32},{32,0},{64,96},{96,64},{1,33},{33,1},{65,97},{97,65},{2,34}... | collective-permute-start | bytes 688136 | tf_op jit(solution)/shard_map/ppermute | solution.py:425
  104.1 3.1 collective-permute-start.6
  104.8 3.3 collective-permute-start.5
  109.0 1.5 collective-permute-start.7
  137.0 9.6 %collective-permute-start.8 = (bf16[16,7168]{1,0:T(8,128)(2,1)S(1)}, bf16[16,7168]{1,0:T(8,128)(2,1)S(1)}, u32[]{:S(2)}, u32[]{:S(2)}) collective-permute-start(bf16[16,7168]{1,0:T(8,128)(2,1)S(1)} %shard_map.108), channel_id=1, source_target_pairs={{0,32},{32,64},{64,96},{96,0},{1,33},{33,65},{65,97},{97,1},{2,34}... | collective-permute-start | bytes 688136 | tf_op jit(solution)/shard_map/ppermute | solution.py:425
  172.0 2.6 collective-permute-start.10
  172.7 2.8 collective-permute-start.9
  176.5 1.7 collective-permute-start.11
  204.6 8.2 %collective-permute-start.12 = (bf16[16,7168]{1,0:T(8,128)(2,1)S(1)}, bf16[16,7168]{1,0:T(8,128)(2,1)S(1)}, u32[]{:S(2)}, u32[]{:S(2)}) collective-permute-start(bf16[16,7168]{1,0:T(8,128)(2,1)S(1)} %shard_map.117), channel_id=1, source_target_pairs={{0,32},{32,64},{64,96},{96,0},{1,33},{33,65},{65,97},{97,1},{2,34}... | collective-permute-start | bytes 688136 | tf_op jit(solution)/shard_map/ppermute | solution.py:425
  238.9 2.6 collective-permute-start.14
  239.6 2.8 collective-permute-start.13
  243.3 1.5 collective-permute-start.15
  271.3 8.2 %collective-permute-start.16 = (bf16[16,7168]{1,0:T(8,128)(2,1)S(1)}, bf16[16,7168]{1,0:T(8,128)(2,1)S(1)}, u32[]{:S(2)}, u32[]{:S(2)}) collective-permute-start(bf16[16,7168]{1,0:T(8,128)(2,1)S(1)} %shard_map.126), channel_id=1, source_target_pairs={{0,32},{32,64},{64,96},{96,0},{1,33},{33,65},{65,97},{97,1},{2,34}... | collective-permute-start | bytes 688136 | tf_op jit(solution)/shard_map/ppermute | solution.py:425
  305.7 2.6 collective-permute-start.18
  306.5 2.8 collective-permute-start.17
  310.2 1.5 collective-permute-start.19
  338.1 8.2 %collective-permute-start.20 = (bf16[16,7168]{1,0:T(8,128)(2,1)S(1)}, bf16[16,7168]{1,0:T(8,128)(2,1)S(1)}, u32[]{:S(2)}, u32[]{:S(2)}) collective-permute-start(bf16[16,7168]{1,0:T(8,128)(2,1)S(1)} %shard_map.135), channel_id=1, source_target_pairs={{0,32},{32,64},{64,96},{96,0},{1,33},{33,65},{65,97},{97,1},{2,34}... | collective-permute-start | bytes 688136 | tf_op jit(solution)/shard_map/ppermute | solution.py:425
  372.4 2.6 collective-permute-start.22
  373.1 2.8 collective-permute-start.21
  376.9 1.8 collective-permute-start.23
  405.1 7.0 %collective-permute-start.24 = (bf16[16,7168]{1,0:T(8,128)(2,1)S(1)}, bf16[16,7168]{1,0:T(8,128)(2,1)S(1)}, u32[]{:S(2)}, u32[]{:S(2)}) collective-permute-start(bf16[16,7168]{1,0:T(8,128)(2,1)S(1)} %shard_map.144), channel_id=1, source_target_pairs={{0,32},{32,0},{64,96},{96,64},{1,33},{33,1},{65,97},{97,65},{2,34}... | collective-permute-start | bytes 688136 | tf_op jit(solution)/shard_map/ppermute | solution.py:425
  438.1 2.6 collective-permute-start.26
  438.9 2.8 collective-permute-start.25
  442.6 1.5 collective-permute-start.27

commit v10 on v9

--- a/solution.py
+++ b/solution.py
@@ -174,24 +174,24 @@
     return pltpu.with_memory_space_constraint(array, pltpu.VMEM)
 
 
-def unpack(arrived, perm, part):
+def unpack(arrived, perm):
     all_rows, width = arrived.shape
     group = perm.shape[0]
     piece = group // PARTS
     some = PARTS // 2
 
-    def kernel(a_ref, p_ref, x_ref):
-        chosen = p_ref[part * some * piece : (part + 1) * some * piece, :]
+    def kernel(a_ref, p_ref, *halved):
         for g in range(all_rows // group):
-            moved = mm(chosen, a_ref[g * group : (g + 1) * group, :]).astype(BF16)
-            for b in range(some):
-                x_ref[g * piece : (g + 1) * piece, b * width : (b + 1) * width] = moved[b * piece : (b + 1) * piece]
-
-    return pl.pallas_call(
-        kernel,
-        out_shape=jax.ShapeDtypeStruct((all_rows // PARTS, some * width), BF16),
+            moved = mm(p_ref[...], a_ref[g * group : (g + 1) * group, :]).astype(BF16)
+            for b in range(PARTS):
+                x_ref, at = halved[b // some], b % some * width
+                x_ref[g * piece : (g + 1) * piece, at : at + width] = moved[b * piece : (b + 1) * piece]
+
+    return pl.pallas_call(
+        kernel,
+        out_shape=[jax.ShapeDtypeStruct((all_rows // PARTS, some * width), BF16)] * 2,
         in_specs=[VMEM_IN] * 2,
-        out_specs=VMEM_IN,
+        out_specs=[VMEM_IN] * 2,
         compiler_params=params(),
         cost_estimate=cost(all_rows * group * width, 3 * all_rows * width),
     )(arrived, perm)
@@ -427,9 +427,8 @@
                 own = hidden
             packed = front(hidden, gain, keys, row_keys, step, width=width, experts=experts)
         arrived = lax.all_to_all(packed, "expert", split_axis=0, concat_axis=0, tiled=True)
-        left = unpack(arrived, perm, 0)
+        left, right = unpack(arrived, perm)
         others_left = lax.ppermute(left, "expert", swap)
-        right = unpack(arrived, perm, 1)
         others_right = lax.ppermute(right, "expert", swap)
         if step == 0:
             results = own_half_staging(

time: 480 us -> 478 us (level)
  transfers between devices with their start and end apart: 28 -> 28, of which waited for: 13 -> 18; matrix products, arithmetic and copies ran while one was open for 0% -> 0% of each run, Pallas kernels for 8% -> 7%
where the time goes in v10:
time: 478 us; the launch traced here: 470 us
  blocking collectives  348 us (73%)
  Pallas kernels  61.1 us (13%)
  waiting for transfers between devices  46.9 us (10%)
  starting transfers between devices  12.5 us (3%)
    all_to_all x7, blocking collectives, per_device(): lax.all_to_all(packed, 'expert', split_axis=0, concat_axis=0, tiled=True)  178 us
    all_to_all x7, blocking collectives, per_device(): lax.all_to_all(partial_value, 'expert', split_axis=0, concat_axis=0, tile...  170 us
    ppermute x6, waiting for transfers between devices, per_device(): hidden = lax.ppermute(current, 'section', pairs)  45 us
    pallas_call x7, Pallas kernels, other_units(): pl.pallas_call(kernel, out_shape=jax.ShapeDtypeStruct((rows * PARTS, widt...  10.3 us
  transfers between devices with their start and end apart: 28, of which 18 were waited for; matrix products, arithmetic and copies ran while one was open for 0% of the time, Pallas kernels for 7%

profile of v10, /device:TPU:1, one launch (start us, length us, event | category | flops | bytes accessed | tf_op | source)
XLA Modules:
  0.0 470.0 jit_solution(4379310445488126158)
XLA Ops:
  0.0 1.4 collective-permute-start.1
  1.6 2.3 shard_map.91
  3.9 27.9 %all_to_all.154 = bf16[32,24,896]{2,1,0:T(8,128)(2,1)S(1)} all-to-all(bf16[32,24,896]{2,1,0:T(8,128)(2,1)S(1)} %bitcast.65), channel_id=1, replica_groups=mesh['section'=4,'expert'=32] {'expert'}, dimensions={0} | all-to-all | bytes 2752512 | tf_op jit(solution)/shard_map/all_to_all | solution.py:429
  33.0 8.0 %shard_map.93 = (f32[192,512]{1,0:T(8,128)S(1)}, f32[192,512]{1,0:T(8,128)S(1)}, bf16[3584,512]{1,0:T(8,128)(2,1)S(1)}, bf16[3584,512]{1,0:T(8,128)(2,1)S(1)}, b...) custom-call(s32[2]{0:T(128)S(1)} %pad_add_fusion.place_ref, ...), custom_call_target="tpu_custom_call" | custom-call | flops 1409286144 | bytes 40370176 | tf_op jit(solution)/shard_map/pallas_call | solution.py:247
  41.0 0.9 shard_map.94
  41.9 0.9 shard_map.95.i_ref
  43.1 1.0 shard_map.96.t_ref
  44.3 1.5 shard_map.97
  45.8 24.3 %all_to_all.155 = bf16[32,24,896]{2,1,0:T(8,128)(2,1)S(1)} all-to-all(bf16[32,24,896]{2,1,0:T(8,128)(2,1)S(1)} %bitcast.59), channel_id=1, replica_groups=mesh['section'=4,'expert'=32] {'expert'}, dimensions={0} | all-to-all | bytes 2752512 | tf_op jit(solution)/shard_map/all_to_all | solution.py:457
  70.1 0.6 shard_map.98
  70.7 1.7 collective-permute-start.4
  72.4 5.7 %collective-permute-done.4.refs_0_.h_ref = bf16[16,7168]{1,0:T(8,128)(2,1)S(1)} collective-permute-done((bf16[16,7168]{1,0:T(8,128)(2,1)S(1)}, bf16[16,7168]{1,0:T(8,128)(2,1)S(1)}, u32[]{:S(2)}, u32[]{:S(2)}) %collective-permute-start.4) | collective-permute-done | bytes 229408 | tf_op jit(solution)/shard_map/ppermute | solution.py:425
  78.6 24.8 %all_to_all.156 = bf16[32,24,896]{2,1,0:T(8,128)(2,1)S(1)} all-to-all(bf16[32,24,896]{2,1,0:T(8,128)(2,1)S(1)} %bitcast.53), channel_id=1, replica_groups=mesh['section'=4,'expert'=32] {'expert'}, dimensions={0} | all-to-all | bytes 2752512 | tf_op jit(solution)/shard_map/all_to_all | solution.py:429
  104.3 0.7 collective-permute-start.5
  105.0 1.6 shard_map.101
  106.6 0.9 shard_map.102
  107.5 0.9 shard_map.103.i_ref
  108.8 1.0 shard_map.104.t_ref
  110.0 1.5 shard_map.105
  111.4 24.3 %all_to_all.157 = bf16[32,24,896]{2,1,0:T(8,128)(2,1)S(1)} all-to-all(bf16[32,24,896]{2,1,0:T(8,128)(2,1)S(1)} %bitcast.60), channel_id=1, replica_groups=mesh['section'=4,'expert'=32] {'expert'}, dimensions={0} | all-to-all | bytes 2752512 | tf_op jit(solution)/shard_map/all_to_all | solution.py:457
  136.3 1.7 collective-permute-start.8
  138.0 7.9 %collective-permute-done.8.refs_0_.h_ref = bf16[16,7168]{1,0:T(8,128)(2,1)S(1)} collective-permute-done((bf16[16,7168]{1,0:T(8,128)(2,1)S(1)}, bf16[16,7168]{1,0:T(8,128)(2,1)S(1)}, u32[]{:S(2)}, u32[]{:S(2)}) %collective-permute-start.8) | collective-permute-done | bytes 229408 | tf_op jit(solution)/shard_map/ppermute | solution.py:425
  146.4 24.5 %all_to_all.158 = bf16[32,24,896]{2,1,0:T(8,128)(2,1)S(1)} all-to-all(bf16[32,24,896]{2,1,0:T(8,128)(2,1)S(1)} %bitcast.54), channel_id=1, replica_groups=mesh['section'=4,'expert'=32] {'expert'}, dimensions={0} | all-to-all | bytes 2752512 | tf_op jit(solution)/shard_map/all_to_all | solution.py:429
  172.1 1.6 shard_map.109
  173.8 0.9 shard_map.110
  174.7 0.9 shard_map.111.i_ref
  176.1 1.0 shard_map.112.t_ref
  177.3 1.5 shard_map.113
  178.8 24.3 %all_to_all.159 = bf16[32,24,896]{2,1,0:T(8,128)(2,1)S(1)} all-to-all(bf16[32,24,896]{2,1,0:T(8,128)(2,1)S(1)} %bitcast.61), channel_id=1, replica_groups=mesh['section'=4,'expert'=32] {'expert'}, dimensions={0} | all-to-all | bytes 2752512 | tf_op jit(solution)/shard_map/all_to_all | solution.py:457
  203.1 0.6 shard_map.114
  203.8 8.1 %collective-permute-done.12.refs_0_.h_ref = bf16[16,7168]{1,0:T(8,128)(2,1)S(1)} collective-permute-done((bf16[16,7168]{1,0:T(8,128)(2,1)S(1)}, bf16[16,7168]{1,0:T(8,128)(2,1)S(1)}, u32[]{:S(2)}, u32[]{:S(2)}) %collective-permute-start.12) | collective-permute-done | bytes 229408 | tf_op jit(solution)/shard_map/ppermute | solution.py:425
  212.4 25.2 %all_to_all.160 = bf16[32,24,896]{2,1,0:T(8,128)(2,1)S(1)} all-to-all(bf16[32,24,896]{2,1,0:T(8,128)(2,1)S(1)} %bitcast.55), channel_id=1, replica_groups=mesh['section'=4,'expert'=32] {'expert'}, dimensions={0} | all-to-all | bytes 2752512 | tf_op jit(solution)/shard_map/all_to_all | solution.py:429
  238.8 1.6 shard_map.117
  240.4 0.9 shard_map.118
  241.4 0.9 shard_map.119.i_ref
  242.6 1.0 shard_map.120.t_ref
  243.8 1.5 shard_map.121
  245.3 24.3 %all_to_all.161 = bf16[32,24,896]{2,1,0:T(8,128)(2,1)S(1)} all-to-all(bf16[32,24,896]{2,1,0:T(8,128)(2,1)S(1)} %bitcast.62), channel_id=1, replica_groups=mesh['section'=4,'expert'=32] {'expert'}, dimensions={0} | all-to-all | bytes 2752512 | tf_op jit(solution)/shard_map/all_to_all | solution.py:457
  270.3 8.1 %collective-permute-done.16.refs_0_.h_ref.t_ref = bf16[16,7168]{1,0:T(8,128)(2,1)S(1)} collective-permute-done((bf16[16,7168]{1,0:T(8,128)(2,1)S(1)}, bf16[16,7168]{1,0:T(8,128)(2,1)S(1)}, u32[]{:S(2)}, u32[]{:S(2)}) %collective-permute-start.16) | collective-permute-done | bytes 229408 | tf_op jit(solution)/shard_map/ppermute | solution.py:425
  278.9 25.3 %all_to_all.162 = bf16[32,24,896]{2,1,0:T(8,128)(2,1)S(1)} all-to-all(bf16[32,24,896]{2,1,0:T(8,128)(2,1)S(1)} %bitcast.56), channel_id=1, replica_groups=mesh['section'=4,'expert'=32] {'expert'}, dimensions={0} | all-to-all | bytes 2752512 | tf_op jit(solution)/shard_map/all_to_all | solution.py:429
  305.4 1.6 shard_map.125
  307.0 0.9 shard_map.126
  308.0 0.9 shard_map.127.i_ref
  309.3 1.0 shard_map.128.t_ref
  310.4 1.5 shard_map.129
  311.9 24.3 %all_to_all.163 = bf16[32,24,896]{2,1,0:T(8,128)(2,1)S(1)} all-to-all(bf16[32,24,896]{2,1,0:T(8,128)(2,1)S(1)} %bitcast.63), channel_id=1, replica_groups=mesh['section'=4,'expert'=32] {'expert'}, dimensions={0} | all-to-all | bytes 2752512 | tf_op jit(solution)/shard_map/all_to_all | solution.py:457
  336.9 8.1 %collective-permute-done.20.refs_0_.h_ref = bf16[16,7168]{1,0:T(8,128)(2,1)S(1)} collective-permute-done((bf16[16,7168]{1,0:T(8,128)(2,1)S(1)}, bf16[16,7168]{1,0:T(8,128)(2,1)S(1)}, u32[]{:S(2)}, u32[]{:S(2)}) %collective-permute-start.20) | collective-permute-done | bytes 229408 | tf_op jit(solution)/shard_map/ppermute | solution.py:425
  345.6 25.2 %all_to_all.164 = bf16[32,24,896]{2,1,0:T(8,128)(2,1)S(1)} all-to-all(bf16[32,24,896]{2,1,0:T(8,128)(2,1)S(1)} %bitcast.57), channel_id=1, replica_groups=mesh['section'=4,'expert'=32] {'expert'}, dimensions={0} | all-to-all | bytes 2752512 | tf_op jit(solution)/shard_map/all_to_all | solution.py:429
  371.9 1.6 shard_map.133
  373.6 0.9 shard_map.134
  374.5 0.9 shard_map.135.i_ref
  375.4 0.6 collective-permute-start.23
  376.0 1.0 shard_map.136.t_ref
  377.2 1.5 shard_map.137
  378.7 24.3 %all_to_all.165 = bf16[32,24,896]{2,1,0:T(8,128)(2,1)S(1)} all-to-all(bf16[32,24,896]{2,1,0:T(8,128)(2,1)S(1)} %bitcast.64), channel_id=1, replica_groups=mesh['section'=4,'expert'=32] {'expert'}, dimensions={0} | all-to-all | bytes 2752512 | tf_op jit(solution)/shard_map/all_to_all | solution.py:457
  403.7 6.9 %collective-permute-done.24.refs_0_.h_ref = bf16[16,7168]{1,0:T(8,128)(2,1)S(1)} collective-permute-done((bf16[16,7168]{1,0:T(8,128)(2,1)S(1)}, bf16[16,7168]{1,0:T(8,128)(2,1)S(1)}, u32[]{:S(2)}, u32[]{:S(2)}) %collective-permute-start.24) | collective-permute-done | bytes 229408 | tf_op jit(solution)/shard_map/ppermute | solution.py:425
  411.1 25.2 %all_to_all.166 = bf16[32,24,896]{2,1,0:T(8,128)(2,1)S(1)} all-to-all(bf16[32,24,896]{2,1,0:T(8,128)(2,1)S(1)} %bitcast.47), channel_id=1, replica_groups=mesh['section'=4,'expert'=32] {'expert'}, dimensions={0} | all-to-all | bytes 2752512 | tf_op jit(solution)/shard_map/all_to_all | solution.py:429
  437.5 1.6 shard_map.141
  439.1 0.9 shard_map.142
  440.1 0.9 shard_map.143.i_ref
  441.3 1.0 shard_map.144.t_ref
  442.5 1.5 shard_map.145
  444.0 24.3 %all_to_all.167 = bf16[32,24,896]{2,1,0:T(8,128)(2,1)S(1)} all-to-all(bf16[32,24,896]{2,1,0:T(8,128)(2,1)S(1)} %bitcast.58), channel_id=1, replica_groups=mesh['section'=4,'expert'=32] {'expert'}, dimensions={0} | all-to-all | bytes 2752512 | tf_op jit(solution)/shard_map/all_to_all | solution.py:457
  468.3 1.3 shard_map.146
  (65 shorter events, 17.9 us)
Async XLA Ops:
  0.0 33.0 %collective-permute-start.1 = (bf16[1,512,7168]{2,1,0:T(8,128)(2,1)}, bf16[1,512,7168]{2,1,0:T(8,128)(2,1)}, u32[]{:S(2)}, u32[]{:S(2)}) collective-permute-start(bf16[1,512,7168]{2,1,0:T(8,128)(2,1)} %d_hbm.1), channel_id=1, source_target_pairs={{0,1},{1,0},{2,3},{3,2},{4,5},{5,4},{6,7},{7,6},{8,9},{9,8},{10,11... | collective-permute-start | bytes 22020104 | tf_op jit(solution)/shard_map/ppermute | solution.py:417
  32.4 8.6 %collective-permute-start.2 = (bf16[192,1792]{1,0:T(8,128)(2,1)S(1)}, bf16[192,1792]{1,0:T(8,128)(2,1)S(1)}, u32[]{:S(2)}, u32[]{:S(2)}) collective-permute-start(bf16[192,1792]{1,0:T(8,128)(2,1)S(1)} %get-tuple-element.68.l_ref), channel_id=1, source_target_pairs={{0,1},{1,0},{2,3},{3,2},{4,5},{5,4},{6,7},{7,6},{8,9},{9,8},{10,11... | collective-permute-start | bytes 2064392 | tf_op jit(solution)/shard_map/ppermute | solution.py:431
  32.7 9.2 %collective-permute-start = (bf16[192,1792]{1,0:T(8,128)(2,1)S(1)}, bf16[192,1792]{1,0:T(8,128)(2,1)S(1)}, u32[]{:S(2)}, u32[]{:S(2)}) collective-permute-start(bf16[192,1792]{1,0:T(8,128)(2,1)S(1)} %get-tuple-element.67.r_ref), channel_id=1, source_target_pairs={{0,1},{1,0},{2,3},{3,2},{4,5},{5,4},{6,7},{7,6},{8,9},{9,8},{10,11... | collective-permute-start | bytes 2064392 | tf_op jit(solution)/shard_map/ppermute | solution.py:432
  42.8 1.5 collective-permute-start.3
  70.7 7.4 %collective-permute-start.4 = (bf16[16,7168]{1,0:T(8,128)(2,1)S(1)}, bf16[16,7168]{1,0:T(8,128)(2,1)S(1)}, u32[]{:S(2)}, u32[]{:S(2)}) collective-permute-start(bf16[16,7168]{1,0:T(8,128)(2,1)S(1)} %shard_map.98), channel_id=1, source_target_pairs={{0,32},{32,0},{64,96},{96,64},{1,33},{33,1},{65,97},{97,65},{2,34}... | collective-permute-start | bytes 688136 | tf_op jit(solution)/shard_map/ppermute | solution.py:425
  104.0 2.6 collective-permute-start.6
  104.3 3.2 collective-permute-start.5
  108.4 1.5 collective-permute-start.7
  136.3 9.6 %collective-permute-start.8 = (bf16[16,7168]{1,0:T(8,128)(2,1)S(1)}, bf16[16,7168]{1,0:T(8,128)(2,1)S(1)}, u32[]{:S(2)}, u32[]{:S(2)}) collective-permute-start(bf16[16,7168]{1,0:T(8,128)(2,1)S(1)} %shard_map.106), channel_id=1, source_target_pairs={{0,32},{32,64},{64,96},{96,0},{1,33},{33,65},{65,97},{97,1},{2,34}... | collective-permute-start | bytes 688136 | tf_op jit(solution)/shard_map/ppermute | solution.py:425
  171.5 2.2 collective-permute-start.10
  171.9 2.9 collective-permute-start.9
  175.6 1.7 collective-permute-start.11
  203.7 8.2 %collective-permute-start.12 = (bf16[16,7168]{1,0:T(8,128)(2,1)S(1)}, bf16[16,7168]{1,0:T(8,128)(2,1)S(1)}, u32[]{:S(2)}, u32[]{:S(2)}) collective-permute-start(bf16[16,7168]{1,0:T(8,128)(2,1)S(1)} %shard_map.114), channel_id=1, source_target_pairs={{0,32},{32,64},{64,96},{96,0},{1,33},{33,65},{65,97},{97,1},{2,34}... | collective-permute-start | bytes 688136 | tf_op jit(solution)/shard_map/ppermute | solution.py:425
  238.2 2.2 collective-permute-start.14
  238.5 2.9 collective-permute-start.13
  242.3 1.5 collective-permute-start.15
  270.2 8.2 %collective-permute-start.16 = (bf16[16,7168]{1,0:T(8,128)(2,1)S(1)}, bf16[16,7168]{1,0:T(8,128)(2,1)S(1)}, u32[]{:S(2)}, u32[]{:S(2)}) collective-permute-start(bf16[16,7168]{1,0:T(8,128)(2,1)S(1)} %shard_map.122), channel_id=1, source_target_pairs={{0,32},{32,64},{64,96},{96,0},{1,33},{33,65},{65,97},{97,1},{2,34}... | collective-permute-start | bytes 688136 | tf_op jit(solution)/shard_map/ppermute | solution.py:425
  304.8 2.2 collective-permute-start.18
  305.2 2.8 collective-permute-start.17
  308.9 1.5 collective-permute-start.19
  336.9 8.2 %collective-permute-start.20 = (bf16[16,7168]{1,0:T(8,128)(2,1)S(1)}, bf16[16,7168]{1,0:T(8,128)(2,1)S(1)}, u32[]{:S(2)}, u32[]{:S(2)}) collective-permute-start(bf16[16,7168]{1,0:T(8,128)(2,1)S(1)} %shard_map.130), channel_id=1, source_target_pairs={{0,32},{32,64},{64,96},{96,0},{1,33},{33,65},{65,97},{97,1},{2,34}... | collective-permute-start | bytes 688136 | tf_op jit(solution)/shard_map/ppermute | solution.py:425
  371.3 2.2 collective-permute-start.22
  371.7 2.9 collective-permute-start.21
  375.4 1.8 collective-permute-start.23
  403.6 7.0 %collective-permute-start.24 = (bf16[16,7168]{1,0:T(8,128)(2,1)S(1)}, bf16[16,7168]{1,0:T(8,128)(2,1)S(1)}, u32[]{:S(2)}, u32[]{:S(2)}) collective-permute-start(bf16[16,7168]{1,0:T(8,128)(2,1)S(1)} %shard_map.138), channel_id=1, source_target_pairs={{0,32},{32,0},{64,96},{96,64},{1,33},{33,1},{65,97},{97,65},{2,34}... | collective-permute-start | bytes 688136 | tf_op jit(solution)/shard_map/ppermute | solution.py:425
  436.9 2.2 collective-permute-start.26
  437.2 2.9 collective-permute-start.25
  441.0 1.5 collective-permute-start.27
